TPU v7x, 128 devices: a whole 4x4x4 slice. The times are simulated.
128 devices in a mesh: ctx: 16 (over x, z_lo, core), dp: 8 (over y, z_hi).
Axes of the slice: x: 4, y: 4, z: 4 (z_hi: 2, z_lo: 2; z = z_hi * 2 + z_lo), core: 2. Of those that a mesh axis runs over, the one named last changes fastest.
Arguments:
- query: bfloat16 [8, 8192, 1024], P('dp', 'ctx'), may hold values from -30 to 30
- key: bfloat16 [8, 8192, 1024], P('dp', 'ctx'), may hold values from -30 to 30
- value: bfloat16 [8, 8192, 1024], P('dp', 'ctx'), may hold values from -6 to 6
- segment_ids: int32 [8, 8192], P('dp', 'ctx'), may hold values from 0 to 1, never falling along the last dimension, each value on 1 to 7680 neighbouring positions
- out_weight: bfloat16 [1024, 2048], replicated, may hold values from -0.1875 to 0.1875
- cotangent: bfloat16 [8, 8192, 2048], P('dp', 'ctx'), may hold values from -6 to 6
Outputs:
- output: bfloat16 [8, 8192, 2048], P('dp', 'ctx')
- grad_query: bfloat16 [8, 8192, 1024], P('dp', 'ctx')
- grad_key: bfloat16 [8, 8192, 1024], P('dp', 'ctx')
- grad_value: bfloat16 [8, 8192, 1024], P('dp', 'ctx')
- grad_weight: float32 [1024, 2048], P(('ctx', 'dp'))
All inputs are finite; a program needn't handle non-finite values.
Results may differ from a plain program's by a relative error of at most 0.023.
Values may be sent and summed in bfloat16 or wider, within the bound.
No kernel may reach another device: no remote copies, remote signals or barrier semaphores. Data moves between devices by JAX's collectives and lax.ppermute only.
A program may use at most 192 MiB of HBM per device.

v0:
```python
from functools import partial
import math

import jax
import jax.numpy as jnp
import numpy as np
from jax import lax
from jax.experimental import pallas as pl
from jax.experimental.pallas import tpu as pltpu
from jax.sharding import PartitionSpec as P

HEADS = 8
HEAD_DIM = 128
HD = 1024
D = 2048
ROWS = 512
GROUPS = 1
PER = HEADS // GROUPS
COLS = PER * HEAD_DIM
FACTORS = (4, 8, 16)
COARSE = tuple(ROWS // factor for factor in FACTORS)
SCALE = 1.0 / math.sqrt(HEAD_DIM)
BIG = float(2**30)
F32 = jnp.float32
BF16 = jnp.bfloat16
SMALL = pl.CostEstimate(flops=1024, bytes_accessed=1024, transcendentals=0)


def params(mebibytes):
    return pltpu.CompilerParams(vmem_limit_bytes=mebibytes * 2**20)


def swap(array, axis, bits):
    return lax.ppermute(array, axis, [(i, i ^ bits) for i in range(lax.axis_size(axis))])


def shift(array, axis, step):
    size = lax.axis_size(axis)
    return lax.ppermute(array, axis, [(i, (i + step) % size) for i in range(size)])


def dot_nt(a, b):
    return lax.dot_general(a, b, (((1,), (1,)), ((), ())), preferred_element_type=F32)


def dot_nn(a, b):
    return lax.dot_general(a, b, (((1,), (0,)), ((), ())), preferred_element_type=F32)


def dot_tn(a, b):
    return lax.dot_general(a, b, (((0,), (0,)), ((), ())), preferred_element_type=F32)


def iota(shape, dim):
    return lax.broadcasted_iota(jnp.int32, shape, dim)


def offset_parts(factor):
    rest = math.log(factor) / SCALE
    parts = []
    for _ in range(3):
        part = float(np.asarray(rest, dtype=jnp.bfloat16))
        parts.append(part)
        rest = rest - part
    return parts


def pool_matrix(factor, weight):
    count = ROWS // factor
    row, col = iota((count, ROWS), 0), iota((count, ROWS), 1)
    inside = (col >= row * factor) & (col < row * factor + weight)
    return jnp.where(inside, 1.0 / weight, 0.0).astype(BF16)


def pool_kernel(place_ref, seg_hbm, key_hbm, value_hbm, one, two, three, fq_ref, fk_ref, mark_ref, seg_ref, key_ref, value_ref, sems):
    copies = [
        pltpu.make_async_copy(source, target, sems.at[place])
        for place, (source, target) in enumerate(((seg_hbm, seg_ref), (key_hbm, key_ref), (value_hbm, value_ref)))
    ]
    for copy in copies:
        copy.start()
    mark_ref[...] = jnp.zeros_like(mark_ref)
    outs = (one, two, three)
    starts = np.cumsum((0,) + COARSE)
    pool = jnp.concatenate([pool_matrix(factor, factor) for factor in FACTORS], 0)
    pick = jnp.concatenate([pool_matrix(factor, 1) for factor in FACTORS], 0)
    copies[0].wait()
    seg = seg_ref[...]
    kind = iota((8, ROWS), 0)
    rows = jnp.where(kind < 2, jnp.where(seg == kind, 1.0, 0.0), jnp.where(kind == 2, 1.0, 0.0)).astype(BF16)
    i, j = iota((8, HEAD_DIM), 0), iota((8, HEAD_DIM), 1)
    to_key = jnp.where((i < 2) & (i == j), 1.0, 0.0).astype(BF16)
    wrong = ((i == 0) & (j == 1)) | ((i == 1) & (j == 0))
    ones = (i == 2) & (j >= 2) & (j < 5)
    to_query = jnp.where(wrong, -BIG, jnp.where(ones, 1.0, 0.0)).astype(BF16)
    own = dot_tn(rows, to_key).astype(BF16)
    fk_ref[...] = own
    fq_ref[...] = dot_tn(rows, to_query).astype(BF16)
    picked = dot_nn(pick, own)
    lane = iota((1, HEAD_DIM), 1)
    for place, (factor, out) in enumerate(zip(FACTORS, outs)):
        parts = offset_parts(factor)
        offset = jnp.where(lane == 2, parts[0], jnp.where(lane == 3, parts[1], jnp.where(lane == 4, parts[2], 0.0)))
        out[:, 2 * HD :] = (picked[starts[place] : starts[place + 1]] + offset).astype(BF16)
    for copy, ref, column in zip(copies[1:], (key_ref, value_ref), (0, HD)):
        copy.wait()
        for start in range(0, HD, 256):
            mean = dot_nn(pool, ref[:, start : start + 256])
            for place, out in enumerate(outs):
                out[:, column + start : column + start + 256] = mean[starts[place] : starts[place + 1]].astype(BF16)


WIDTH = 2 * HD + HEAD_DIM
POOL_LIMIT = 52
WHOLE = pl.BlockSpec(memory_space=pltpu.VMEM)
ANY = pl.BlockSpec(memory_space=pl.ANY)
HBM = pl.BlockSpec(memory_space=pltpu.HBM)
MARK = jax.ShapeDtypeStruct((8, 128), F32)


def pool(place, seg, key, value):
    feature = jax.ShapeDtypeStruct((ROWS, HEAD_DIM), BF16)
    token = pltpu.VMEM((ROWS, HD), BF16)
    return pl.pallas_call(
        pool_kernel,
        in_specs=[pl.BlockSpec(memory_space=pltpu.SMEM)] + [HBM] * 3,
        out_specs=[WHOLE] * 6,
        out_shape=[jax.ShapeDtypeStruct((count, WIDTH), BF16) for count in COARSE] + [feature, feature, MARK],
        scratch_shapes=[pltpu.VMEM((1, ROWS), jnp.int32), token, token, pltpu.SemaphoreType.DMA((3,))],
        compiler_params=params(POOL_LIMIT),
        cost_estimate=SMALL,
    )(place, seg, key, value)


def pause_kernel(*refs):
    refs[-1][...] = jnp.zeros_like(refs[-1])


def pause(after):
    return pl.pallas_call(
        pause_kernel,
        in_specs=[ANY] * len(after),
        out_specs=WHOLE,
        out_shape=MARK,
        compiler_params=params(1),
        cost_estimate=SMALL,
    )(*after)


COARSE_ROWS = 768
FIRST = 7
RATE = SCALE * math.log2(math.e)


def columns(h):
    if isinstance(h, int):
        return slice(h * HEAD_DIM, h * HEAD_DIM + HEAD_DIM)
    return pl.ds(pl.multiple_of(h * HEAD_DIM, HEAD_DIM), HEAD_DIM)


def pair(refs, place, at):
    return jnp.concatenate([refs[2 * place][:, at], refs[2 * place + 1][:, at]], 0)


def joined(total, add):
    return add if total is None else total + add


def each_head(step, heads, unroll):
    if unroll == len(heads):
        for h in heads:
            step(h)
    else:
        lax.fori_loop(heads[0], heads[-1] + 1, lambda h, carry: (step(h), carry)[1], 0, unroll=unroll)


EARLY = 1024
LATE = 256


def early_forward_kernel(*refs):
    q_ref, k_ref, v_ref, fq_ref, fk_ref = refs[:5]
    pieces = refs[5:9]
    p_ref, mixed_ref, stat_ref, scores = refs[-4:]

    def step(h):
        at, beside = columns(h), columns(HEADS + h)
        query = jnp.concatenate([q_ref[:, at], fq_ref[...]], 1)
        top = None
        for place in range(4):
            rows = pl.ds(place * 256, 256)
            if place < 2:
                key = jnp.concatenate([k_ref[rows, at], fk_ref[rows, :]], 1)
            else:
                key = jnp.concatenate([pair(pieces, place - 2, at), pair(pieces, place - 2, slice(2 * HD, WIDTH))], 1)
            here = dot_nt(key, query) * RATE
            scores[rows, :] = here
            peak = jnp.max(here, 0, keepdims=True)
            top = peak if top is None else jnp.maximum(top, peak)
        total, mixed = None, None
        for place in range(4):
            rows = pl.ds(place * 256, 256)
            here = jnp.exp2(scores[rows, :] - top)
            total = joined(total, jnp.sum(here, 0, keepdims=True))
            here = here.astype(BF16)
            p_ref[h, rows, :] = here
            value = v_ref[rows, at] if place < 2 else pair(pieces, place - 2, beside)
            mixed = joined(mixed, dot_tn(value, here))
        mixed_ref[at, :] = mixed
        stat_ref[h, 0:1, :] = top
        stat_ref[h, 1:2, :] = total

    each_head(step, range(HEADS), 2)


def early_forward(query, key, value, fq, fk, pieces, after):
    return pl.pallas_call(
        early_forward_kernel,
        in_specs=[WHOLE] * 9 + [ANY] * len(after),
        out_specs=[WHOLE] * 3,
        out_shape=[
            jax.ShapeDtypeStruct((HEADS, EARLY, ROWS), BF16),
            jax.ShapeDtypeStruct((HD, ROWS), F32),
            jax.ShapeDtypeStruct((HEADS, 8, ROWS), F32),
        ],
        scratch_shapes=[pltpu.VMEM((EARLY, ROWS), F32)],
        compiler_params=params(12),
        cost_estimate=SMALL,
    )(query, key, value, fq, fk, *pieces, *after)


def late_forward_kernel(*refs):
    q_ref, across_ref, fq_ref, mixed_ref, stat_ref = refs[:5]
    pieces = refs[5:7]
    p_ref, ot_ref, row_ref = refs[7:]

    feature = pair(pieces, 0, slice(2 * HD, WIDTH))
    scores = []
    for h in range(HEADS):
        query = jnp.concatenate([q_ref[:, columns(h)], fq_ref[...]], 1)
        scores.append(dot_nt(jnp.concatenate([pair(pieces, 0, columns(h)), feature], 1), query) * RATE)
    for h in range(HEADS):
        before, total = stat_ref[h, 0:1, :], stat_ref[h, 1:2, :]
        top = jnp.maximum(before, jnp.max(scores[h], 0, keepdims=True))
        factor = jnp.exp2(before - top)
        here = jnp.exp2(scores[h] - top)
        inverse = 1.0 / (total * factor + jnp.sum(here, 0, keepdims=True))
        row_ref[h, 1:2, :] = factor * inverse
        p_ref[h] = (here * inverse).astype(BF16)
    for h in range(HEADS):
        at = columns(h)
        mixed = dot_tn(pair(pieces, 0, columns(HEADS + h)), p_ref[h]) + mixed_ref[at, :] * row_ref[h, 1:2, :]
        ot_ref[at, :] = mixed.astype(BF16)
        row_ref[h, 0:1, :] = jnp.sum(across_ref[at, :].astype(F32) * mixed, 0, keepdims=True)


def late_forward(query, across, fq, mixed, stats, pieces):
    return pl.pallas_call(
        late_forward_kernel,
        in_specs=[WHOLE] * 7,
        out_specs=[WHOLE] * 3,
        out_shape=[
            jax.ShapeDtypeStruct((HEADS, LATE, ROWS), BF16),
            jax.ShapeDtypeStruct((HD, ROWS), BF16),
            jax.ShapeDtypeStruct((HEADS, 8, ROWS), F32),
        ],
        compiler_params=params(12),
        cost_estimate=SMALL,
    )(query, across, fq, mixed, stats, *pieces)


def scaled(across, factor):
    across = (across.astype(F32) * factor).astype(BF16)
    return across, across.T


def coarse_backward_kernel(heads, *refs):
    q_ref, g_ref, across_ref, row_ref, early_ref, late_ref = refs[:6]
    pieces = refs[6:12]
    keep_ref, give_ref, dq_ref, mark_ref = refs[-4:]
    mark_ref[...] = jnp.zeros_like(mark_ref)

    def step(h):
        at, to = columns(h), columns(h - heads[0])
        q, g = q_ref[:, at], g_ref[:, at]
        delta, factor = row_ref[h, 0:1, :], row_ref[h, 1:2, :]
        across, scaled_g = scaled(across_ref[at, :], factor)
        scaled_delta = delta * factor
        grad_q = None
        for place in range(3):
            key, value = pair(pieces, place, at), pair(pieces, place, columns(HEADS + h))
            if place < 2:
                weight = early_ref[h, pl.ds(512 + place * 256, 256), :]
                slope = dot_nn(value, across) - scaled_delta
                grad_v = dot_nn(weight, scaled_g)
            else:
                weight = late_ref[h]
                slope = dot_nn(value, across_ref[at, :]) - delta
                grad_v = dot_nn(weight, g)
            slope = (weight.astype(F32) * slope).astype(BF16)
            grads = ((dot_nn(slope, q) * SCALE).astype(BF16), grad_v.astype(BF16))
            for side, grad in enumerate(grads):
                for half in range(2):
                    out, row = ((keep_ref, give_ref)[half], place * 128) if place == 2 else ((keep_ref, give_ref)[place], half * 128)
                    out[side, pl.ds(row, 128), to] = grad[half * 128 : half * 128 + 128]
            grad_q = joined(grad_q, dot_tn(key, slope))
        dq_ref[to, :] = grad_q

    each_head(step, heads, len(heads))


def coarse_backward(query, grad, across, rows, early, late, pieces, heads, after):
    width = len(heads) * HEAD_DIM
    return pl.pallas_call(
        partial(coarse_backward_kernel, heads),
        in_specs=[WHOLE] * 12 + [ANY] * len(after),
        out_specs=[WHOLE] * 4,
        out_shape=[
            jax.ShapeDtypeStruct((2, 384, width), BF16),
            jax.ShapeDtypeStruct((2, 384, width), BF16),
            jax.ShapeDtypeStruct((width, ROWS), F32),
            MARK,
        ],
        compiler_params=params(12),
        cost_estimate=SMALL,
    )(query, grad, across, rows, early, late, *pieces, *after)


def local_backward_kernel(heads, parts, before, *refs):
    q_ref, k_ref, v_ref, across_ref, row_ref, p_ref = refs[:6]
    part_refs = refs[6 : 6 + len(parts)]
    dq_ref, dk_ref, dv_ref, mark_ref = refs[-4:]
    mark_ref[...] = jnp.zeros_like(mark_ref)
    for ref, out in zip(refs[6 + len(parts) : 6 + len(parts) + before], (dq_ref, dk_ref, dv_ref)):
        out[:, : heads[0] * HEAD_DIM] = ref[...]

    def step(part, first, h):
        at = columns(h)
        q = q_ref[:, at]
        delta, factor = row_ref[h, 0:1, :], row_ref[h, 1:2, :]
        across, g = scaled(across_ref[at, :], factor)
        delta = delta * factor
        grad_q = part[columns(h - first), :]
        for start in (0, 256):
            rows = pl.ds(start, 256)
            weight = p_ref[h, rows, :]
            slope = (weight.astype(F32) * (dot_nn(v_ref[rows, at], across) - delta)).astype(BF16)
            dk_ref[rows, at] = (dot_nn(slope, q) * SCALE).astype(BF16)
            dv_ref[rows, at] = dot_nn(weight, g).astype(BF16)
            grad_q = grad_q + dot_tn(k_ref[rows, at], slope)
        dq_ref[:, at] = (grad_q * SCALE).astype(BF16).T

    for part, (first, last) in zip(part_refs, parts):
        inside = [h for h in heads if first <= h < last]
        each_head(partial(step, part, first), inside, len(inside))


def local_backward(query, key, value, across, rows, weights, partials, heads, earlier, after):
    partials = [part for part in partials if part[0] <= heads[-1] and heads[0] < part[1]]
    token = jax.ShapeDtypeStruct((ROWS, (heads[-1] + 1) * HEAD_DIM), BF16)
    return pl.pallas_call(
        partial(local_backward_kernel, heads, [part[:2] for part in partials], len(earlier)),
        in_specs=[WHOLE] * (6 + len(partials) + len(earlier)) + [ANY] * len(after),
        out_specs=[WHOLE] * 4,
        out_shape=[token, token, token, MARK],
        compiler_params=params(12),
        cost_estimate=SMALL,
    )(query, key, value, across, rows, weights, *[part[2] for part in partials], *earlier, *after)


def grad_attention_kernel(c_ref, w_ref, out_ref, across_ref):
    for start in range(0, HD, 256):
        out = dot_nt(c_ref[...], w_ref[start : start + 256, :]).astype(BF16)
        out_ref[:, start : start + 256] = out
        across_ref[start : start + 256, :] = out.T


def grad_attention_of(cotangent, weight):
    return pl.pallas_call(
        grad_attention_kernel,
        in_specs=[WHOLE] * 2,
        out_specs=[WHOLE] * 2,
        out_shape=[jax.ShapeDtypeStruct((ROWS, HD), BF16), jax.ShapeDtypeStruct((HD, ROWS), BF16)],
        compiler_params=params(8),
        cost_estimate=SMALL,
    )(cotangent, weight)


def project_kernel(a_ref, w_ref, _, out_ref, mark_ref):
    mark_ref[...] = jnp.zeros_like(mark_ref)
    for start in range(0, D, 512):
        out_ref[:, start : start + 512] = dot_tn(a_ref[...], w_ref[:, start : start + 512]).astype(BF16)


def project(attention, weight, after):
    return pl.pallas_call(
        project_kernel,
        in_specs=[WHOLE] * 2 + [ANY],
        out_specs=[WHOLE] * 2,
        out_shape=[jax.ShapeDtypeStruct((ROWS, D), BF16), MARK],
        compiler_params=params(8),
        cost_estimate=SMALL,
    )(attention, weight, after)


def stack_kernel(count, *refs):
    out, start = refs[-1], 0
    for ref in refs[:count]:
        out[pl.ds(start, ref.shape[0]), :] = ref[...]
        start = start + ref.shape[0]


def stack(arrays, after):
    rows, width = sum(array.shape[0] for array in arrays), arrays[0].shape[1]
    return pl.pallas_call(
        partial(stack_kernel, len(arrays)),
        in_specs=[WHOLE] * len(arrays) + [ANY] * len(after),
        out_specs=WHOLE,
        out_shape=jax.ShapeDtypeStruct((rows, width), BF16),
        compiler_params=params(4),
        cost_estimate=SMALL,
    )(*arrays, *after)


def grad_weight_kernel(place_ref, ot_ref, c_ref, keep_ref, give_ref, mark_ref, lhs):
    mark_ref[...] = jnp.zeros_like(mark_ref)
    core, y = place_ref[0], place_ref[1]
    for slot in range(2):
        half = core if slot == 0 else 1 - core
        for step in range(4):
            target = lax.rem(y + step, 4)
            for j in range(HEADS):
                source = pl.multiple_of(j * 128 + half * 64 + target * 16, 16)
                row = ((slot * 4 + step) * HEADS + j) * 16
                lhs[row : row + 16, :] = ot_ref[pl.ds(source, 16), :]
    for out, row in ((give_ref, HD // 2), (keep_ref, 0)):
        for start in range(0, D, 512):
            at = slice(start, start + 512)
            out[:, at] = dot_nn(lhs[row : row + HD // 2, :], c_ref[:, at]).astype(BF16)


def grad_weight_part(place, ot, cotangent):
    shape = jax.ShapeDtypeStruct((HD // 2, D), BF16)
    return pl.pallas_call(
        grad_weight_kernel,
        in_specs=[pl.BlockSpec(memory_space=pltpu.SMEM)] + [WHOLE] * 2,
        out_specs=[WHOLE] * 3,
        out_shape=[shape, shape, MARK],
        scratch_shapes=[pltpu.VMEM((HD, ROWS), BF16)],
        compiler_params=params(8),
        cost_estimate=SMALL,
    )(place, ot, cotangent)


def split_sum_kernel(count, axis, bounds, *refs):
    ins, outs = refs[:count], refs[len(refs) - len(bounds) :]
    for (start, size), out in zip(bounds, outs):
        at = (slice(None),) * axis + (pl.ds(start, size),)
        total = ins[0][at].astype(F32)
        for ref in ins[1:]:
            total = total + ref[at].astype(F32)
        out[...] = total.astype(out.dtype)


def split_sum(arrays, axis, sizes, after=()):
    shape = arrays[0].shape
    starts = np.cumsum([0] + list(sizes))
    bounds = [(int(start), int(size)) for start, size in zip(starts, sizes)]
    whole = pl.BlockSpec(memory_space=pltpu.VMEM)
    outs = [jax.ShapeDtypeStruct(shape[:axis] + (size,) + shape[axis + 1 :], BF16) for size in sizes]
    count = math.prod(shape)
    return pl.pallas_call(
        partial(split_sum_kernel, len(arrays), axis, bounds),
        in_specs=[whole] * len(arrays) + [ANY] * len(after),
        out_specs=[whole] * len(sizes),
        out_shape=outs,
        compiler_params=params(16),
        cost_estimate=SMALL,
    )(*arrays, *after)


def add_all(refs, at):
    terms = [ref[at].astype(F32) for ref in refs]
    return (terms[0] + terms[1]) + (terms[2] + terms[3])


def relay_kernel(one_ref, three_ref, lower_ref, upper_ref, *refs):
    up, down = refs[len(refs) - 2 :]
    up[:64, :] = (one_ref[:64, :].astype(F32) + lower_ref[...].astype(F32)).astype(BF16)
    up[64:, :] = one_ref[64:, :]
    down[:64, :] = three_ref[:64, :]
    down[64:, :] = (three_ref[64:, :].astype(F32) + upper_ref[...].astype(F32)).astype(BF16)


def relay(arrays, after):
    return pl.pallas_call(
        relay_kernel,
        in_specs=[WHOLE] * 4 + [ANY] * len(after),
        out_specs=[WHOLE] * 2,
        out_shape=[jax.ShapeDtypeStruct((128, D), BF16)] * 2,
        compiler_params=params(8),
        cost_estimate=SMALL,
    )(*arrays, *after)


def y_sum_kernel(place_ref, *refs):
    for step, out in enumerate(refs[len(refs) - 4 :]):
        at = pl.ds(pl.multiple_of(lax.rem(place_ref[2] + step, 4) * 32, 32), 32)
        out[...] = (refs[0][at, :].astype(F32) + refs[1][at, :].astype(F32) + refs[2][at, :].astype(F32)).astype(BF16)


def y_sum(place, arrays, after):
    return pl.pallas_call(
        y_sum_kernel,
        in_specs=[pl.BlockSpec(memory_space=pltpu.SMEM)] + [WHOLE] * 3 + [ANY] * len(after),
        out_specs=[WHOLE] * 4,
        out_shape=[jax.ShapeDtypeStruct((32, D), BF16)] * 4,
        compiler_params=params(8),
        cost_estimate=SMALL,
    )(place, *arrays, *after)


def back_sum_kernel(*refs):
    outs = refs[len(refs) - 3 :]
    column = 0
    for keep, received in ((refs[0], refs[1]), (refs[2], refs[3])):
        width = keep.shape[2]
        for place, out in enumerate(outs):
            at = (slice(None), slice(place * 128, place * 128 + 128), slice(None))
            total = keep[at].astype(F32) + received[at].astype(F32)
            out[:, :, column : column + width] = total.astype(BF16)
        column = column + width


def back_sum(arrays, after):
    return pl.pallas_call(
        back_sum_kernel,
        in_specs=[WHOLE] * 4 + [ANY] * len(after),
        out_specs=[WHOLE] * 3,
        out_shape=[jax.ShapeDtypeStruct((2, 128, HD), BF16)] * 3,
        compiler_params=params(8),
        cost_estimate=SMALL,
    )(*arrays, *after)


def second_sum_kernel(own_ref, received_ref, *refs):
    near, far = refs[len(refs) - 2 :]

    def rows(start, stop):
        return (own_ref[:, start:stop, :].astype(F32) + received_ref[:, start:stop, :].astype(F32)).astype(BF16)

    near[:, :64, :] = rows(0, 64)
    near[:, 64:, :] = rows(96, 128)
    far[...] = rows(64, 96)


def second_sum(own, received, after):
    return pl.pallas_call(
        second_sum_kernel,
        in_specs=[WHOLE] * 2 + [ANY] * len(after),
        out_specs=[WHOLE] * 2,
        out_shape=[jax.ShapeDtypeStruct((2, 96, HD), BF16), jax.ShapeDtypeStruct((2, 32, HD), BF16)],
        compiler_params=params(8),
        cost_estimate=SMALL,
    )(own, received, *after)


def third_sum_kernel(far_ref, near_ref, *refs):
    refs[-1][...] = (far_ref[...].astype(F32) + near_ref[:, 64:, :].astype(F32)).astype(BF16)


def third_sum(far, near, after):
    return pl.pallas_call(
        third_sum_kernel,
        in_specs=[WHOLE] * 2 + [ANY] * len(after),
        out_specs=WHOLE,
        out_shape=jax.ShapeDtypeStruct((2, 32, HD), BF16),
        compiler_params=params(8),
        cost_estimate=SMALL,
    )(far, near, *after)


def finish_kernel(*refs):
    dk_ref, dv_ref, one, two, three = refs[:5]
    outs, mark_ref = refs[-3:-1], refs[-1]
    mark_ref[...] = jnp.zeros_like(mark_ref)
    token, row = iota((256, 128), 0), iota((256, 128), 1)
    spread = jnp.zeros((256, 128), F32)
    start = 0
    for factor, count in ((4, 64), (8, 32), (16, 16)):
        local = row - start
        inside = (local >= 0) & (local < count) & (token >= local * factor) & (token < local * factor + factor)
        spread = jnp.where(inside, 1.0 / factor, spread)
        start = start + count
    spread = spread.astype(BF16)
    for place, (own, out) in enumerate(zip((dk_ref, dv_ref), outs)):
        rows = jnp.concatenate([one[place], two[place], three[place], jnp.zeros((16, HD), BF16)], 0)
        out[...] = (own[...].astype(F32) + dot_nn(spread, rows)).astype(BF16)


def finish(dk, dv, one, two, three, after):
    half = pl.BlockSpec((256, HD), lambda i: (i, 0))
    shape = jax.ShapeDtypeStruct((ROWS, HD), BF16)
    coarse = [pl.BlockSpec((2, rows, HD), lambda i: (0, i, 0)) for rows in (64, 32, 16)]
    return pl.pallas_call(
        finish_kernel,
        grid=(2,),
        in_specs=[half] * 2 + coarse + [ANY] * len(after),
        out_specs=[half, half, pl.BlockSpec((8, 128), lambda i: (0, 0))],
        out_shape=[shape, shape, MARK],
        compiler_params=params(16),
        cost_estimate=SMALL,
    )(dk, dv, one, two, three, *after)


def add_all(refs, at):
    terms = [ref[at].astype(F32) for ref in refs]
    return (terms[0] + terms[1]) + (terms[2] + terms[3])


def last_sum_kernel(place_ref, *refs):
    outs = refs[len(refs) - 4 :]
    z_lo, z_hi = place_ref[3], place_ref[4]
    sums = add_all(refs[:4], slice(None))
    for lo in range(2):
        for hi in range(2):
            rows = sums[lo * 16 + hi * 8 : lo * 16 + hi * 8 + 8]
            for place, out in enumerate(outs):

                @pl.when((lax.rem(z_lo + place % 2, 2) == lo) & (lax.rem(z_hi + place // 2, 2) == hi))
                def _():
                    out[...] = rows


def last_sum(place, arrays, after):
    return pl.pallas_call(
        last_sum_kernel,
        in_specs=[pl.BlockSpec(memory_space=pltpu.SMEM)] + [WHOLE] * 4 + [ANY] * len(after),
        out_specs=[WHOLE] * 4,
        out_shape=[jax.ShapeDtypeStruct((8, D), F32)] * 4,
        compiler_params=params(4),
        cost_estimate=SMALL,
    )(place, *arrays, *after)


def total_kernel(*refs):
    refs[-1][...] = add_all(refs[:4], slice(None))


def total(arrays, after):
    return pl.pallas_call(
        total_kernel,
        in_specs=[WHOLE] * 4 + [ANY] * len(after),
        out_specs=WHOLE,
        out_shape=jax.ShapeDtypeStruct((8, D), F32),
        compiler_params=params(4),
        cost_estimate=SMALL,
    )(*arrays, *after)


def body(query, key, value, segment_ids, out_weight, cotangent):
    query, key, value = query[0], key[0], value[0]
    cotangent = cotangent[0]
    index = lax.axis_index("ctx")
    other = lax.axis_index("dp")
    core, x = jnp.bitwise_and(index, 1), jnp.right_shift(index, 2)
    z_lo = jnp.bitwise_and(jnp.right_shift(index, 1), 1)
    y, z_hi = jnp.right_shift(other, 1), jnp.bitwise_and(other, 1)
    place = jnp.stack([core, y, x, z_lo, z_hi]).astype(jnp.int32)

    one, two, three, fq, fk, mark = pool(place, segment_ids, key, value)
    from_z = swap(one, "ctx", 2)
    two, three, mark = lax.optimization_barrier((two, three, pause([mark])))
    grad_attention, grad_across = grad_attention_of(cotangent, out_weight)
    from_x = stack([swap(two, "ctx", 4), swap(three, "ctx", 12), swap(three, "ctx", 8)], [grad_attention, mark])
    from_xz = swap(from_x, "ctx", 2)
    sooner = [from_z, from_x, swap(from_z, "ctx", 1), swap(from_x, "ctx", 1)]
    early, mixed, stats = early_forward(query, key, value, fq, fk, sooner, [])
    from_xz, stats = lax.optimization_barrier((from_xz, stats))
    later = [from_xz, swap(from_xz, "ctx", 1)]
    pieces = sooner + later

    late, attention, rows = late_forward(query, grad_across, fq, mixed, stats, later)
    kept, given, mark = grad_weight_part(place, attention, cotangent)
    one = coarse_backward(query, grad_attention, grad_across, rows, early, late, pieces, range(FIRST), [mark])
    parts = split_sum([kept, swap(given, "ctx", 1)], 0, (128, 128, 64, 64, 128), [one[3]])
    lower, upper = shift(parts[2], "dp", 2), shift(parts[3], "dp", -2)
    rest = coarse_backward(query, grad_attention, grad_across, rows, early, late, pieces, range(FIRST, HEADS), [parts[0]])
    own_one, own_two, own_xz = back_sum([one[0], swap(one[1], "ctx", 1), rest[0], swap(rest[1], "ctx", 1)], [])
    back_xz = swap(own_xz, "ctx", 2)
    back_z = swap(own_one, "ctx", 2)
    partials = [(0, FIRST, one[2]), (FIRST, HEADS, rest[2])]
    *earlier, mark = local_backward(
        query, key, value, grad_across, rows, early, partials, range(4), (), [own_one]
    )
    up, down = relay([parts[1], parts[4], lower, upper], [mark])
    near, far = second_sum(own_two, back_xz, [up])
    near = swap(near, "ctx", 4)
    grad_query, dk, dv, mark = local_backward(
        query, key, value, grad_across, rows, early, partials, range(4, HEADS), earlier, [far]
    )
    output, mark = project(attention, out_weight, mark)
    parts = y_sum(place, [parts[0], shift(up, "dp", 2), shift(down, "dp", -2)], [mark])
    far = third_sum(far, near, [parts[0]])
    parts = [parts[0]] + [shift(parts[step], "ctx", 4 * step) for step in (1, 2, 3)]
    parts = last_sum(place, parts, [far])
    grad_key, grad_value, mark = finish(dk, dv, back_z, near, swap(far, "ctx", 12), [parts[0]])
    count = lax.axis_size("dp")
    both = [(i, (i // count ^ 2) * count + (i % count ^ 1)) for i in range(lax.axis_size("ctx") * count)]
    grad_weight = total(
        [parts[0], swap(parts[1], "ctx", 2), swap(parts[2], "dp", 1), lax.ppermute(parts[3], ("ctx", "dp"), both)],
        [mark],
    )
    return output[None], grad_query[None], grad_key[None], grad_value[None], grad_weight


def solution(mesh):
    in_specs = (
        P("dp", "ctx", None),
        P("dp", "ctx", None),
        P("dp", "ctx", None),
        P("dp", "ctx"),
        P(),
        P("dp", "ctx", None),
    )
    out_specs = (
        P("dp", "ctx", None),
        P("dp", "ctx", None),
        P("dp", "ctx", None),
        P("dp", "ctx", None),
        P(("ctx", "dp"), None),
    )
    return jax.shard_map(body, mesh=mesh, in_specs=in_specs, out_specs=out_specs, check_vma=False)
```

profile of v0, /device:TPU:0, one launch (start us, length us, event | category | flops | bytes accessed | tf_op | source)
XLA Modules:
  0.0 100.2 jit_solution(13645683632821338241)
XLA Ops:
  0.6 0.1 stack.23.place_ref
  0.7 0.8 copy-done.6
  1.5 2.6 %shard_map.102 = (bf16[128,2176]{1,0:T(8,128)(2,1)S(1)}, bf16[64,2176]{1,0:T(8,128)(2,1)S(1)}, bf16[32,2176]{1,0:T(8,128)(2,1)S(1)}, bf16[512,128]{1,0:T(8,128)(...) custom-call(s32[5]{0:T(128)S(1)} %stack.23.place_ref, s32[1,512]{1,0:T(1,128)S(1)} %copy-done.6, ...), custom_call_target="tpu_custom_call" | custom-call | flops 1024 | bytes 1024 | tf_op jit(solution)/shard_map/pallas_call | solution.py:124
  4.2 2.1 %collective-permute-start = (bf16[128,2176]{1,0:T(8,128)(2,1)S(1)}, bf16[128,2176]{1,0:T(8,128)(2,1)S(1)}, u32[]{:S(2)}, u32[]{:S(2)}) collective-permute-start(bf16[128,2176]{1,0:T(8,128)(2,1)S(1)} %get-tuple-element.70), channel_id=1, source_target_pairs={{0,16},{8,24},{16,0},{24,8},{32,48},{40,56},{48,32},{56,40},{64,80... | collective-permute-start | bytes 1671176 | tf_op jit(solution)/shard_map/ppermute | solution.py:34
  6.3 1.5 %collective-permute-start.1 = (bf16[64,2176]{1,0:T(8,128)(2,1)S(1)}, bf16[64,2176]{1,0:T(8,128)(2,1)S(1)}, u32[]{:S(2)}, u32[]{:S(2)}) collective-permute-start(bf16[64,2176]{1,0:T(8,128)(2,1)S(1)} %get-tuple-element.74), channel_id=1, source_target_pairs={{0,32},{8,40},{16,48},{24,56},{32,0},{40,8},{48,16},{56,24},{64,96... | collective-permute-start | bytes 835592 | tf_op jit(solution)/shard_map/ppermute | solution.py:34
  7.8 2.7 %collective-permute-start.3 = (bf16[32,2176]{1,0:T(8,128)(2,1)S(1)}, bf16[32,2176]{1,0:T(8,128)(2,1)S(1)}, u32[]{:S(2)}, u32[]{:S(2)}) collective-permute-start(bf16[32,2176]{1,0:T(8,128)(2,1)S(1)} %get-tuple-element.75), channel_id=1, source_target_pairs={{0,64},{8,72},{16,80},{24,88},{32,96},{40,104},{48,112},{56,120},{... | collective-permute-start | bytes 417800 | tf_op jit(solution)/shard_map/ppermute | solution.py:34
  10.5 0.5 collective-permute-start.2
  11.0 2.2 %copy-done.3 = bf16[1024,2048]{1,0:T(8,128)(2,1)S(1)} copy-done((bf16[1024,2048]{1,0:T(8,128)(2,1)S(1)}, bf16[1024,2048]{1,0:T(8,128)(2,1)}, u32[]{:S(2)}) %copy-start.3) | copy-done | bytes 4194328
  13.1 2.4 %shard_map.101 = (bf16[512,1024]{1,0:T(8,128)(2,1)S(1)}, bf16[1024,512]{1,0:T(8,128)(2,1)S(1)}) custom-call(bf16[512,2048]{1,0:T(8,128)(2,1)S(1)} %bitcast.27, bf16[1024,2048]{1,0:T(8,128)(2,1)S(1)} %copy-done.3), custom_call_target="tpu_custom_call" | custom-call | flops 1024 | bytes 1024 | tf_op jit(solution)/shard_map/pallas_call | solution.py:379
  15.6 0.0 copy-start
  15.6 0.0 copy-start.1
  15.6 4.0 %collective-permute-done.3.refs_2_ = bf16[32,2176]{1,0:T(8,128)(2,1)S(1)} collective-permute-done((bf16[32,2176]{1,0:T(8,128)(2,1)S(1)}, bf16[32,2176]{1,0:T(8,128)(2,1)S(1)}, u32[]{:S(2)}, u32[]{:S(2)}) %collective-permute-start.3) | collective-permute-done | bytes 139296 | tf_op jit(solution)/shard_map/ppermute | solution.py:34
  19.7 0.1 collective-permute-start.5
  19.8 0.0 collective-permute-done.refs_5_.refs_6_
  19.8 0.5 collective-permute-start.4
  20.3 0.3 collective-permute-start.6
  20.6 1.1 %collective-permute-done.5.refs_8_.refs_9_ = bf16[128,2176]{1,0:T(8,128)(2,1)S(1)} collective-permute-done((bf16[128,2176]{1,0:T(8,128)(2,1)S(1)}, bf16[128,2176]{1,0:T(8,128)(2,1)S(1)}, u32[]{:S(2)}, u32[]{:S(2)}) %collective-permute-start.5) | collective-permute-done | bytes 557088 | tf_op jit(solution)/shard_map/ppermute | solution.py:34
  21.7 0.8 collective-permute-done.4.refs_7_.refs_8_
  22.5 9.3 %shard_map.105 = (bf16[8,1024,512]{2,1,0:T(8,128)(2,1)S(1)}, f32[1024,512]{1,0:T(8,128)S(1)}, f32[8,8,512]{2,1,0:T(8,128)S(1)}) custom-call(bf16[512,1024]{1,0:T(8,128)(2,1)S(1)} %bitcast.13, bf16[512,1024]{1,0:T(8,128)(2,1)S(1)} %bitcast.20, bf16[512,1024]{1,0:T(8,128)(2,1)S(1)} %bitcast.24, bf16[512,128]{1,0:T(8,128)(2,1)S(1)} %get-tuple-element.68.refs_3_.refs_2_, ...), custom_call_target="tpu_custom_call" | custom-call | flops 1024 | bytes 1024 | tf_op jit(solution)/shard_map/pallas_call | solution.py:217
  31.9 3.0 %collective-permute-done.6.refs_5_.refs_10_ = bf16[128,2176]{1,0:T(8,128)(2,1)S(1)} collective-permute-done((bf16[128,2176]{1,0:T(8,128)(2,1)S(1)}, bf16[128,2176]{1,0:T(8,128)(2,1)S(1)}, u32[]{:S(2)}, u32[]{:S(2)}) %collective-permute-start.6) | collective-permute-done | bytes 557088 | tf_op jit(solution)/shard_map/ppermute | solution.py:34
  34.9 2.0 %collective-permute-done.7.refs_6_.refs_11_ = bf16[128,2176]{1,0:T(8,128)(2,1)S(1)} collective-permute-done((bf16[128,2176]{1,0:T(8,128)(2,1)S(1)}, bf16[128,2176]{1,0:T(8,128)(2,1)S(1)}, u32[]{:S(2)}, u32[]{:S(2)}) %collective-permute-start.7) | collective-permute-done | bytes 557088 | tf_op jit(solution)/shard_map/ppermute | solution.py:34
  36.9 2.6 %shard_map.106 = (bf16[8,256,512]{2,1,0:T(8,128)(2,1)S(1)}, bf16[1024,512]{1,0:T(8,128)(2,1)S(1)}, f32[8,8,512]{2,1,0:T(8,128)S(1)}) custom-call(bf16[512,1024]{1,0:T(8,128)(2,1)S(1)} %bitcast.14, bf16[1024,512]{1,0:T(8,128)(2,1)S(1)} %get-tuple-element.67.refs_1_.refs_2_.refs_3_, bf16[512,128]{1,0:T(8,128)(2,1)S(1)} %get-tuple-element.68.refs_3_.refs_2_, ...), custom_call_target="tpu_custom_call" | custom-call | flops 1024 | bytes 1024 | tf_op jit(solution)/shard_map/pallas_call | solution.py:258
  39.5 2.9 %shard_map.107 = (bf16[512,2048]{1,0:T(8,128)(2,1)S(1)}, bf16[512,2048]{1,0:T(8,128)(2,1)S(1)}, f32[8,128]{1,0:T(8,128)S(1)}) custom-call(s32[5]{0:T(128)S(1)} %stack.23.place_ref, bf16[1024,512]{1,0:T(8,128)(2,1)S(1)} %get-tuple-element.82.ot_ref.a_ref, bf16[512,2048]{1,0:T(8,128)(2,1)S(1)} %bitcast.28), custom_call_target="tpu_custom_call" | custom-call | flops 1024 | bytes 1024 | tf_op jit(solution)/shard_map/pallas_call | solution.py:444
  42.4 0.4 collective-permute-start.8
  42.8 5.3 %shard_map.108 = (bf16[2,384,896]{2,1,0:T(8,128)(2,1)S(1)}, bf16[2,384,896]{2,1,0:T(8,128)(2,1)S(1)}, f32[896,512]{1,0:T(8,128)S(1)}, f32[8,128]{1,0:T(8,128)S(1)}) custom-call(bf16[512,1024]{1,0:T(8,128)(2,1)S(1)} %bitcast.15, bf16[512,1024]{1,0:T(8,128)(2,1)S(1)} %get-tuple-element.76.refs_3_.refs_1_, ...), custom_call_target="tpu_custom_call" | custom-call | flops 1024 | bytes 1024 | tf_op jit(solution)/shard_map/pallas_call | solution.py:314
  48.1 0.4 collective-permute-start.9
  48.5 0.5 shard_map.109
  49.0 1.4 %shard_map.110 = (bf16[2,384,128]{2,1,0:T(8,128)(2,1)S(1)}, bf16[2,384,128]{2,1,0:T(8,128)(2,1)S(1)}, f32[128,512]{1,0:T(8,128)S(1)}, f32[8,128]{1,0:T(8,128)}) custom-call(bf16[512,1024]{1,0:T(8,128)(2,1)S(1)} %bitcast.16, bf16[512,1024]{1,0:T(8,128)(2,1)S(1)} %get-tuple-element.76.refs_3_.refs_1_, ...), custom_call_target="tpu_custom_call" | custom-call | flops 1024 | bytes 1024 | tf_op jit(solution)/shard_map/pallas_call | solution.py:314
  50.4 0.1 collective-permute-start.10
  50.6 0.7 collective-permute-done.9.refs_1_
  51.3 0.6 collective-permute-done.10.refs_3_
  51.9 0.4 shard_map.111
  52.3 0.8 collective-permute-start.11
  53.1 1.6 %collective-permute-start.12 = (bf16[64,2048]{1,0:T(8,128)(2,1)S(1)}, bf16[64,2048]{1,0:T(8,128)(2,1)S(1)}, u32[]{:S(2)}, u32[]{:S(2)}) collective-permute-start(bf16[64,2048]{1,0:T(8,128)(2,1)S(1)} %get-tuple-element.105), channel_id=1, source_target_pairs={{0,2},{1,3},{2,4},{3,5},{4,6},{5,7},{6,0},{7,1},{8,10},{9,11},{10,... | collective-permute-start | bytes 786440 | tf_op jit(solution)/shard_map/ppermute | solution.py:39
  54.7 1.7 %collective-permute-start.13 = (bf16[64,2048]{1,0:T(8,128)(2,1)S(1)}, bf16[64,2048]{1,0:T(8,128)(2,1)S(1)}, u32[]{:S(2)}, u32[]{:S(2)}) collective-permute-start(bf16[64,2048]{1,0:T(8,128)(2,1)S(1)} %get-tuple-element.106), channel_id=1, source_target_pairs={{0,6},{1,7},{2,0},{3,1},{4,2},{5,3},{6,4},{7,5},{8,14},{9,15},{10,... | collective-permute-start | bytes 786440 | tf_op jit(solution)/shard_map/ppermute | solution.py:39
  56.3 2.6 %shard_map.112 = (bf16[512,512]{1,0:T(8,128)(2,1)S(1)}, bf16[512,512]{1,0:T(8,128)(2,1)S(1)}, bf16[512,512]{1,0:T(8,128)(2,1)S(1)}, f32[8,128]{1,0:T(8,128)S(1)}) custom-call(bf16[512,1024]{1,0:T(8,128)(2,1)S(1)} %bitcast.17, bf16[512,1024]{1,0:T(8,128)(2,1)S(1)} %bitcast.21, bf16[512,1024]{1,0:T(8,128)(2,1)S(1)} %bitcast.25, ...), custom_call_target="tpu_custom_call" | custom-call | flops 1024 | bytes 1024 | tf_op jit(solution)/shard_map/pallas_call | solution.py:361
  58.9 3.5 %collective-permute-done.12.lower_ref = bf16[64,2048]{1,0:T(8,128)(2,1)S(1)} collective-permute-done((bf16[64,2048]{1,0:T(8,128)(2,1)S(1)}, bf16[64,2048]{1,0:T(8,128)(2,1)S(1)}, u32[]{:S(2)}, u32[]{:S(2)}) %collective-permute-start.12) | collective-permute-done | bytes 262176 | tf_op jit(solution)/shard_map/ppermute | solution.py:39
  62.4 0.0 collective-permute-done.13.upper_ref
  62.4 0.1 shard_map.113
  62.6 3.0 %collective-permute-start.17 = (bf16[128,2048]{1,0:T(8,128)(2,1)S(1)}, bf16[128,2048]{1,0:T(8,128)(2,1)S(1)}, u32[]{:S(2)}, u32[]{:S(2)}) collective-permute-start(bf16[128,2048]{1,0:T(8,128)(2,1)S(1)} %get-tuple-element.116), channel_id=1, source_target_pairs={{0,6},{1,7},{2,0},{3,1},{4,2},{5,3},{6,4},{7,5},{8,14},{9,15},{10,... | collective-permute-start | bytes 1572872 | tf_op jit(solution)/shard_map/ppermute | solution.py:39
  65.6 0.0 collective-permute-start.16
  65.6 0.7 collective-permute-done.11.received_ref
  66.3 0.1 shard_map.114
  66.5 0.9 collective-permute-start.15
  67.3 1.4 %collective-permute-start.14 = (bf16[2,128,1024]{2,1,0:T(8,128)(2,1)S(1)}, bf16[2,128,1024]{2,1,0:T(8,128)(2,1)S(1)}, u32[]{:S(2)}, u32[]{:S(2)}) collective-permute-start(bf16[2,128,1024]{2,1,0:T(8,128)(2,1)S(1)} %get-tuple-element.97.refs_7_), channel_id=1, source_target_pairs={{0,16},{8,24},{16,0},{24,8},{32,48},{40,56},{48,32},{56,40},{64,80... | collective-permute-start | bytes 1572872 | tf_op jit(solution)/shard_map/ppermute | solution.py:34
  68.8 3.6 %shard_map.115 = (bf16[512,1024]{1,0:T(8,128)(2,1)}, bf16[512,1024]{1,0:T(8,128)(2,1)S(1)}, bf16[512,1024]{1,0:T(8,128)(2,1)S(1)}, f32[8,128]{1,0:T(8,128)S(1)}) custom-call(bf16[512,1024]{1,0:T(8,128)(2,1)S(1)} %bitcast.18, bf16[512,1024]{1,0:T(8,128)(2,1)S(1)} %bitcast.22, bf16[512,1024]{1,0:T(8,128)(2,1)S(1)} %bitcast.26, ...), custom_call_target="tpu_custom_call" | custom-call | flops 1024 | bytes 1024 | tf_op jit(solution)/shard_map/pallas_call | solution.py:361
  72.4 3.7 %shard_map.116 = (bf16[512,2048]{1,0:T(8,128)(2,1)}, f32[8,128]{1,0:T(8,128)S(1)}) custom-call(bf16[1024,512]{1,0:T(8,128)(2,1)S(1)} %get-tuple-element.82.ot_ref.a_ref, bf16[1024,2048]{1,0:T(8,128)(2,1)S(1)} %copy-done.4, f32[8,128]{1,0:T(8,128)S(1)} %get-tuple-element.110._), custom_call_target="tpu_custom_call" | custom-call | flops 1024 | bytes 1024 | tf_op jit(solution)/shard_map/pallas_call | solution.py:396
  76.1 3.0 %collective-permute-done.16.refs_1_ = bf16[128,2048]{1,0:T(8,128)(2,1)S(1)} collective-permute-done((bf16[128,2048]{1,0:T(8,128)(2,1)S(1)}, bf16[128,2048]{1,0:T(8,128)(2,1)S(1)}, u32[]{:S(2)}, u32[]{:S(2)}) %collective-permute-start.16) | collective-permute-done | bytes 524320 | tf_op jit(solution)/shard_map/ppermute | solution.py:39
  79.1 0.7 shard_map.117
  79.9 1.6 %collective-permute-start.19 = (bf16[32,2048]{1,0:T(8,128)(2,1)S(1)}, bf16[32,2048]{1,0:T(8,128)(2,1)S(1)}, u32[]{:S(2)}, u32[]{:S(2)}) collective-permute-start(bf16[32,2048]{1,0:T(8,128)(2,1)S(1)} %get-tuple-element.119), channel_id=1, source_target_pairs={{0,32},{8,40},{16,48},{24,56},{32,64},{40,72},{48,80},{56,88},{64,... | collective-permute-start | bytes 393224 | tf_op jit(solution)/shard_map/ppermute | solution.py:39
  81.4 2.7 %collective-permute-start.20 = (bf16[32,2048]{1,0:T(8,128)(2,1)S(1)}, bf16[32,2048]{1,0:T(8,128)(2,1)S(1)}, u32[]{:S(2)}, u32[]{:S(2)}) collective-permute-start(bf16[32,2048]{1,0:T(8,128)(2,1)S(1)} %get-tuple-element.120), channel_id=1, source_target_pairs={{0,64},{8,72},{16,80},{24,88},{32,96},{40,104},{48,112},{56,120},{... | collective-permute-start | bytes 393224 | tf_op jit(solution)/shard_map/ppermute | solution.py:39
  84.1 1.4 %collective-permute-start.21 = (bf16[32,2048]{1,0:T(8,128)(2,1)S(1)}, bf16[32,2048]{1,0:T(8,128)(2,1)S(1)}, u32[]{:S(2)}, u32[]{:S(2)}) collective-permute-start(bf16[32,2048]{1,0:T(8,128)(2,1)S(1)} %get-tuple-element.121), channel_id=1, source_target_pairs={{0,96},{8,104},{16,112},{24,120},{32,0},{40,8},{48,16},{56,24},{64... | collective-permute-start | bytes 393224 | tf_op jit(solution)/shard_map/ppermute | solution.py:39
  85.6 0.1 collective-permute-start.18
  85.7 1.0 %collective-permute-done.19.refs_1_ = bf16[32,2048]{1,0:T(8,128)(2,1)S(1)} collective-permute-done((bf16[32,2048]{1,0:T(8,128)(2,1)S(1)}, bf16[32,2048]{1,0:T(8,128)(2,1)S(1)}, u32[]{:S(2)}, u32[]{:S(2)}) %collective-permute-start.19) | collective-permute-done | bytes 131104 | tf_op jit(solution)/shard_map/ppermute | solution.py:39
  86.7 1.9 %collective-permute-done.20.refs_2_ = bf16[32,2048]{1,0:T(8,128)(2,1)S(1)} collective-permute-done((bf16[32,2048]{1,0:T(8,128)(2,1)S(1)}, bf16[32,2048]{1,0:T(8,128)(2,1)S(1)}, u32[]{:S(2)}, u32[]{:S(2)}) %collective-permute-start.20) | collective-permute-done | bytes 131104 | tf_op jit(solution)/shard_map/ppermute | solution.py:39
  88.6 0.5 collective-permute-done.21.refs_3_
  89.1 0.7 shard_map.119
  89.8 0.7 collective-permute-start.22
  90.5 3.6 %collective-permute-start.23 = (f32[8,2048]{1,0:T(8,128)S(1)}, f32[8,2048]{1,0:T(8,128)S(1)}, u32[]{:S(2)}, u32[]{:S(2)}) collective-permute-start(f32[8,2048]{1,0:T(8,128)S(1)} %get-tuple-element.126), channel_id=1, source_target_pairs={{0,1},{1,0},{2,3},{3,2},{4,5},{5,4},{6,7},{7,6},{8,9},{9,8},{10,11... | collective-permute-start | bytes 196616 | tf_op jit(solution)/shard_map/ppermute | solution.py:34
  94.1 0.5 collective-permute-start.24
  94.6 1.8 %shard_map.120 = (bf16[512,1024]{1,0:T(8,128)(2,1)}, bf16[512,1024]{1,0:T(8,128)(2,1)}, f32[8,128]{1,0:T(8,128)S(1)}) custom-call(bf16[512,1024]{1,0:T(8,128)(2,1)S(1)} %get-tuple-element.113.refs_0_, bf16[512,1024]{1,0:T(8,128)(2,1)S(1)} %get-tuple-element.114.refs_1_, bf16[2,128,1024]{2,1,0:T(8,128)(2,1)S(1)} %collective-permute-done.14.refs_2_, ...), custom_call_target="tpu_custom_call" | custom-call | flops 1024 | bytes 1024 | tf_op jit(solution)/shard_map/pallas_call | solution.py:605
  96.4 0.6 collective-permute-done.23.refs_2_
  97.0 2.5 %collective-permute-done.24.refs_3_ = f32[8,2048]{1,0:T(8,128)S(1)} collective-permute-done((f32[8,2048]{1,0:T(8,128)S(1)}, f32[8,2048]{1,0:T(8,128)S(1)}, u32[]{:S(2)}, u32[]{:S(2)}) %collective-permute-start.24) | collective-permute-done | bytes 65568 | tf_op jit(solution)/shard_map/ppermute | solution.py:711
  99.6 0.6 shard_map.121
  (22 shorter events, 0.1 us)
Async XLA Ops:
  0.6 10.3 %copy-start.5 = (bf16[1,512,2048]{2,1,0:T(8,128)(2,1)S(1)}, bf16[1,512,2048]{2,1,0:T(8,128)(2,1)}, u32[]{:S(2)}) copy-start(bf16[1,512,2048]{2,1,0:T(8,128)(2,1)} %param.11) | copy-start | bytes 6291460
  0.7 0.8 copy-start.6
  4.2 15.6 %collective-permute-start = (bf16[128,2176]{1,0:T(8,128)(2,1)S(1)}, bf16[128,2176]{1,0:T(8,128)(2,1)S(1)}, u32[]{:S(2)}, u32[]{:S(2)}) collective-permute-start(bf16[128,2176]{1,0:T(8,128)(2,1)S(1)} %get-tuple-element.70), channel_id=1, source_target_pairs={{0,16},{8,24},{16,0},{24,8},{32,48},{40,56},{48,32},{56,40},{64,80... | collective-permute-start | bytes 1671176 | tf_op jit(solution)/shard_map/ppermute | solution.py:34
  6.3 13.4 %collective-permute-start.1 = (bf16[64,2176]{1,0:T(8,128)(2,1)S(1)}, bf16[64,2176]{1,0:T(8,128)(2,1)S(1)}, u32[]{:S(2)}, u32[]{:S(2)}) collective-permute-start(bf16[64,2176]{1,0:T(8,128)(2,1)S(1)} %get-tuple-element.74), channel_id=1, source_target_pairs={{0,32},{8,40},{16,48},{24,56},{32,0},{40,8},{48,16},{56,24},{64,96... | collective-permute-start | bytes 835592 | tf_op jit(solution)/shard_map/ppermute | solution.py:34
  7.8 11.9 %collective-permute-start.3 = (bf16[32,2176]{1,0:T(8,128)(2,1)S(1)}, bf16[32,2176]{1,0:T(8,128)(2,1)S(1)}, u32[]{:S(2)}, u32[]{:S(2)}) collective-permute-start(bf16[32,2176]{1,0:T(8,128)(2,1)S(1)} %get-tuple-element.75), channel_id=1, source_target_pairs={{0,64},{8,72},{16,80},{24,88},{32,96},{40,104},{48,112},{56,120},{... | collective-permute-start | bytes 417800 | tf_op jit(solution)/shard_map/ppermute | solution.py:34
  10.5 9.2 %collective-permute-start.2 = (bf16[32,2176]{1,0:T(8,128)(2,1)S(1)}, bf16[32,2176]{1,0:T(8,128)(2,1)S(1)}, u32[]{:S(2)}, u32[]{:S(2)}) collective-permute-start(bf16[32,2176]{1,0:T(8,128)(2,1)S(1)} %get-tuple-element.75), channel_id=1, source_target_pairs={{0,96},{8,104},{16,112},{24,120},{32,64},{40,72},{48,80},{56,88},{... | collective-permute-start | bytes 417800 | tf_op jit(solution)/shard_map/ppermute | solution.py:34
  11.0 2.2 %copy-start.3 = (bf16[1024,2048]{1,0:T(8,128)(2,1)S(1)}, bf16[1024,2048]{1,0:T(8,128)(2,1)}, u32[]{:S(2)}) copy-start(bf16[1024,2048]{1,0:T(8,128)(2,1)} %w_ref.3) | copy-start | bytes 12582916
  13.1 9.4 %copy-start.2 = (bf16[1,512,1024]{2,1,0:T(8,128)(2,1)S(1)}, bf16[1,512,1024]{2,1,0:T(8,128)(2,1)}, u32[]{:S(2)}) copy-start(bf16[1,512,1024]{2,1,0:T(8,128)(2,1)} %param.8) | copy-start | bytes 3145732
  15.6 7.0 %copy-start = (bf16[1,512,1024]{2,1,0:T(8,128)(2,1)S(1)}, bf16[1,512,1024]{2,1,0:T(8,128)(2,1)}, u32[]{:S(2)}) copy-start(bf16[1,512,1024]{2,1,0:T(8,128)(2,1)} %param.6) | copy-start | bytes 3145732
  15.6 6.9 %copy-start.1 = (bf16[1,512,1024]{2,1,0:T(8,128)(2,1)S(1)}, bf16[1,512,1024]{2,1,0:T(8,128)(2,1)}, u32[]{:S(2)}) copy-start(bf16[1,512,1024]{2,1,0:T(8,128)(2,1)} %param.7) | copy-start | bytes 3145732
  19.7 2.0 %collective-permute-start.5 = (bf16[128,2176]{1,0:T(8,128)(2,1)S(1)}, bf16[128,2176]{1,0:T(8,128)(2,1)S(1)}, u32[]{:S(2)}, u32[]{:S(2)}) collective-permute-start(bf16[128,2176]{1,0:T(8,128)(2,1)S(1)} %shard_map.104.refs_6_.refs_7_), channel_id=1, source_target_pairs={{0,8},{8,0},{16,24},{24,16},{32,40},{40,32},{48,56},{56,48},{64,72... | collective-permute-start | bytes 1671176 | tf_op jit(solution)/shard_map/ppermute | solution.py:34
  19.8 2.7 %collective-permute-start.4 = (bf16[128,2176]{1,0:T(8,128)(2,1)S(1)}, bf16[128,2176]{1,0:T(8,128)(2,1)S(1)}, u32[]{:S(2)}, u32[]{:S(2)}) collective-permute-start(bf16[128,2176]{1,0:T(8,128)(2,1)S(1)} %collective-permute-done.refs_5_.refs_6_), channel_id=1, source_target_pairs={{0,8},{8,0},{16,24},{24,16},{32,40},{40,32},{48,56},{56,48},{64,72... | collective-permute-start | bytes 1671176 | tf_op jit(solution)/shard_map/ppermute | solution.py:34
  20.3 14.6 %collective-permute-start.6 = (bf16[128,2176]{1,0:T(8,128)(2,1)S(1)}, bf16[128,2176]{1,0:T(8,128)(2,1)S(1)}, u32[]{:S(2)}, u32[]{:S(2)}) collective-permute-start(bf16[128,2176]{1,0:T(8,128)(2,1)S(1)} %shard_map.104.refs_6_.refs_7_), channel_id=1, source_target_pairs={{0,16},{8,24},{16,0},{24,8},{32,48},{40,56},{48,32},{56,40},{64,80... | collective-permute-start | bytes 1671176 | tf_op jit(solution)/shard_map/ppermute | solution.py:34
  34.9 2.0 %collective-permute-start.7 = (bf16[128,2176]{1,0:T(8,128)(2,1)S(1)}, bf16[128,2176]{1,0:T(8,128)(2,1)S(1)}, u32[]{:S(2)}, u32[]{:S(2)}) collective-permute-start(bf16[128,2176]{1,0:T(8,128)(2,1)S(1)} %collective-permute-done.6.refs_5_.refs_10_), channel_id=1, source_target_pairs={{0,8},{8,0},{16,24},{24,16},{32,40},{40,32},{48,56},{56,48},{64,72... | collective-permute-start | bytes 1671176 | tf_op jit(solution)/shard_map/ppermute | solution.py:34
  42.4 6.1 %collective-permute-start.8 = (bf16[512,2048]{1,0:T(8,128)(2,1)S(1)}, bf16[512,2048]{1,0:T(8,128)(2,1)S(1)}, u32[]{:S(2)}, u32[]{:S(2)}) collective-permute-start(bf16[512,2048]{1,0:T(8,128)(2,1)S(1)} %get-tuple-element.89), channel_id=1, source_target_pairs={{0,8},{8,0},{16,24},{24,16},{32,40},{40,32},{48,56},{56,48},{64,72... | collective-permute-start | bytes 6291464 | tf_op jit(solution)/shard_map/ppermute | solution.py:34
  48.1 3.2 %collective-permute-start.9 = (bf16[2,384,896]{2,1,0:T(8,128)(2,1)S(1)}, bf16[2,384,896]{2,1,0:T(8,128)(2,1)S(1)}, u32[]{:S(2)}, u32[]{:S(2)}) collective-permute-start(bf16[2,384,896]{2,1,0:T(8,128)(2,1)S(1)} %get-tuple-element.94), channel_id=1, source_target_pairs={{0,8},{8,0},{16,24},{24,16},{32,40},{40,32},{48,56},{56,48},{64,72... | collective-permute-start | bytes 4128776 | tf_op jit(solution)/shard_map/ppermute | solution.py:34
  50.4 1.4 %collective-permute-start.10 = (bf16[2,384,128]{2,1,0:T(8,128)(2,1)S(1)}, bf16[2,384,128]{2,1,0:T(8,128)(2,1)S(1)}, u32[]{:S(2)}, u32[]{:S(2)}) collective-permute-start(bf16[2,384,128]{2,1,0:T(8,128)(2,1)S(1)} %get-tuple-element.96), channel_id=1, source_target_pairs={{0,8},{8,0},{16,24},{24,16},{32,40},{40,32},{48,56},{56,48},{64,72... | collective-permute-start | bytes 589832 | tf_op jit(solution)/shard_map/ppermute | solution.py:34
  52.3 14.1 %collective-permute-start.11 = (bf16[2,128,1024]{2,1,0:T(8,128)(2,1)S(1)}, bf16[2,128,1024]{2,1,0:T(8,128)(2,1)S(1)}, u32[]{:S(2)}, u32[]{:S(2)}) collective-permute-start(bf16[2,128,1024]{2,1,0:T(8,128)(2,1)S(1)} %get-tuple-element.102), channel_id=1, source_target_pairs={{0,16},{8,24},{16,0},{24,8},{32,48},{40,56},{48,32},{56,40},{64,80... | collective-permute-start | bytes 1572872 | tf_op jit(solution)/shard_map/ppermute | solution.py:34
  53.1 9.4 %collective-permute-start.12 = (bf16[64,2048]{1,0:T(8,128)(2,1)S(1)}, bf16[64,2048]{1,0:T(8,128)(2,1)S(1)}, u32[]{:S(2)}, u32[]{:S(2)}) collective-permute-start(bf16[64,2048]{1,0:T(8,128)(2,1)S(1)} %get-tuple-element.105), channel_id=1, source_target_pairs={{0,2},{1,3},{2,4},{3,5},{4,6},{5,7},{6,0},{7,1},{8,10},{9,11},{10,... | collective-permute-start | bytes 786440 | tf_op jit(solution)/shard_map/ppermute | solution.py:39
  54.7 7.8 %collective-permute-start.13 = (bf16[64,2048]{1,0:T(8,128)(2,1)S(1)}, bf16[64,2048]{1,0:T(8,128)(2,1)S(1)}, u32[]{:S(2)}, u32[]{:S(2)}) collective-permute-start(bf16[64,2048]{1,0:T(8,128)(2,1)S(1)} %get-tuple-element.106), channel_id=1, source_target_pairs={{0,6},{1,7},{2,0},{3,1},{4,2},{5,3},{6,4},{7,5},{8,14},{9,15},{10,... | collective-permute-start | bytes 786440 | tf_op jit(solution)/shard_map/ppermute | solution.py:39
  62.6 13.5 %collective-permute-start.17 = (bf16[128,2048]{1,0:T(8,128)(2,1)S(1)}, bf16[128,2048]{1,0:T(8,128)(2,1)S(1)}, u32[]{:S(2)}, u32[]{:S(2)}) collective-permute-start(bf16[128,2048]{1,0:T(8,128)(2,1)S(1)} %get-tuple-element.116), channel_id=1, source_target_pairs={{0,6},{1,7},{2,0},{3,1},{4,2},{5,3},{6,4},{7,5},{8,14},{9,15},{10,... | collective-permute-start | bytes 1572872 | tf_op jit(solution)/shard_map/ppermute | solution.py:39
  65.6 13.5 %collective-permute-start.16 = (bf16[128,2048]{1,0:T(8,128)(2,1)S(1)}, bf16[128,2048]{1,0:T(8,128)(2,1)S(1)}, u32[]{:S(2)}, u32[]{:S(2)}) collective-permute-start(bf16[128,2048]{1,0:T(8,128)(2,1)S(1)} %get-tuple-element.108.refs_0_), channel_id=1, source_target_pairs={{0,2},{1,3},{2,4},{3,5},{4,6},{5,7},{6,0},{7,1},{8,10},{9,11},{10,... | collective-permute-start | bytes 1572872 | tf_op jit(solution)/shard_map/ppermute | solution.py:39
  66.5 19.1 %collective-permute-start.15 = (bf16[2,96,1024]{2,1,0:T(8,128)(2,1)S(1)}, bf16[2,96,1024]{2,1,0:T(8,128)(2,1)S(1)}, u32[]{:S(2)}, u32[]{:S(2)}) collective-permute-start(bf16[2,96,1024]{2,1,0:T(8,128)(2,1)S(1)} %get-tuple-element.115), channel_id=1, source_target_pairs={{0,32},{8,40},{16,48},{24,56},{32,0},{40,8},{48,16},{56,24},{64,96... | collective-permute-start | bytes 1179656 | tf_op jit(solution)/shard_map/ppermute | solution.py:34
  67.3 27.3 %collective-permute-start.14 = (bf16[2,128,1024]{2,1,0:T(8,128)(2,1)S(1)}, bf16[2,128,1024]{2,1,0:T(8,128)(2,1)S(1)}, u32[]{:S(2)}, u32[]{:S(2)}) collective-permute-start(bf16[2,128,1024]{2,1,0:T(8,128)(2,1)S(1)} %get-tuple-element.97.refs_7_), channel_id=1, source_target_pairs={{0,16},{8,24},{16,0},{24,8},{32,48},{40,56},{48,32},{56,40},{64,80... | collective-permute-start | bytes 1572872 | tf_op jit(solution)/shard_map/ppermute | solution.py:34
  68.8 3.7 %copy-start.4 = (bf16[1024,2048]{1,0:T(8,128)(2,1)S(1)}, bf16[1024,2048]{1,0:T(8,128)(2,1)}, u32[]{:S(2)}) copy-start(bf16[1024,2048]{1,0:T(8,128)(2,1)} %w_ref.3) | copy-start | bytes 12582916
  79.9 6.8 %collective-permute-start.19 = (bf16[32,2048]{1,0:T(8,128)(2,1)S(1)}, bf16[32,2048]{1,0:T(8,128)(2,1)S(1)}, u32[]{:S(2)}, u32[]{:S(2)}) collective-permute-start(bf16[32,2048]{1,0:T(8,128)(2,1)S(1)} %get-tuple-element.119), channel_id=1, source_target_pairs={{0,32},{8,40},{16,48},{24,56},{32,64},{40,72},{48,80},{56,88},{64,... | collective-permute-start | bytes 393224 | tf_op jit(solution)/shard_map/ppermute | solution.py:39
  81.4 7.2 %collective-permute-start.20 = (bf16[32,2048]{1,0:T(8,128)(2,1)S(1)}, bf16[32,2048]{1,0:T(8,128)(2,1)S(1)}, u32[]{:S(2)}, u32[]{:S(2)}) collective-permute-start(bf16[32,2048]{1,0:T(8,128)(2,1)S(1)} %get-tuple-element.120), channel_id=1, source_target_pairs={{0,64},{8,72},{16,80},{24,88},{32,96},{40,104},{48,112},{56,120},{... | collective-permute-start | bytes 393224 | tf_op jit(solution)/shard_map/ppermute | solution.py:39
  84.1 5.0 %collective-permute-start.21 = (bf16[32,2048]{1,0:T(8,128)(2,1)S(1)}, bf16[32,2048]{1,0:T(8,128)(2,1)S(1)}, u32[]{:S(2)}, u32[]{:S(2)}) collective-permute-start(bf16[32,2048]{1,0:T(8,128)(2,1)S(1)} %get-tuple-element.121), channel_id=1, source_target_pairs={{0,96},{8,104},{16,112},{24,120},{32,0},{40,8},{48,16},{56,24},{64... | collective-permute-start | bytes 393224 | tf_op jit(solution)/shard_map/ppermute | solution.py:39
  85.6 9.0 %collective-permute-start.18 = (bf16[2,32,1024]{2,1,0:T(8,128)(2,1)S(1)}, bf16[2,32,1024]{2,1,0:T(8,128)(2,1)S(1)}, u32[]{:S(2)}, u32[]{:S(2)}) collective-permute-start(bf16[2,32,1024]{2,1,0:T(8,128)(2,1)S(1)} %shard_map.118.refs_4_), channel_id=1, source_target_pairs={{0,96},{8,104},{16,112},{24,120},{32,64},{40,72},{48,80},{56,88},{... | collective-permute-start | bytes 393224 | tf_op jit(solution)/shard_map/ppermute | solution.py:34
  89.8 6.6 %collective-permute-start.22 = (f32[8,2048]{1,0:T(8,128)S(1)}, f32[8,2048]{1,0:T(8,128)S(1)}, u32[]{:S(2)}, u32[]{:S(2)}) collective-permute-start(f32[8,2048]{1,0:T(8,128)S(1)} %get-tuple-element.125), channel_id=1, source_target_pairs={{0,16},{8,24},{16,0},{24,8},{32,48},{40,56},{48,32},{56,40},{64,80... | collective-permute-start | bytes 196616 | tf_op jit(solution)/shard_map/ppermute | solution.py:34
  90.5 6.5 %collective-permute-start.23 = (f32[8,2048]{1,0:T(8,128)S(1)}, f32[8,2048]{1,0:T(8,128)S(1)}, u32[]{:S(2)}, u32[]{:S(2)}) collective-permute-start(f32[8,2048]{1,0:T(8,128)S(1)} %get-tuple-element.126), channel_id=1, source_target_pairs={{0,1},{1,0},{2,3},{3,2},{4,5},{5,4},{6,7},{7,6},{8,9},{9,8},{10,11... | collective-permute-start | bytes 196616 | tf_op jit(solution)/shard_map/ppermute | solution.py:34
  94.1 5.5 %collective-permute-start.24 = (f32[8,2048]{1,0:T(8,128)S(1)}, f32[8,2048]{1,0:T(8,128)S(1)}, u32[]{:S(2)}, u32[]{:S(2)}) collective-permute-start(f32[8,2048]{1,0:T(8,128)S(1)} %get-tuple-element.127), channel_id=1, source_target_pairs={{0,17},{1,16},{2,19},{3,18},{4,21},{5,20},{6,23},{7,22},{8,25},{9,... | collective-permute-start | bytes 196616 | tf_op jit(solution)/shard_map/ppermute | solution.py:711
where the time goes:
time: 101 us; the launch traced here: 100 us
  Pallas kernels  41.6 us (41%)
  starting transfers between devices  28.6 us (28%)
  waiting for transfers between devices  26.1 us (26%)
  local copies, waits for them, and re-layouts  3.11 us (3%)
    ppermute x17, starting transfers between devices, swap(): lax.ppermute(array, axis, [(i, i ^ bits) for i in range(lax.axis_size(axi...  16.1 us
    ppermute x17, waiting for transfers between devices, swap(): lax.ppermute(array, axis, [(i, i ^ bits) for i in range(lax.axis_size(axi...  13.6 us
    ppermute x7, starting transfers between devices, shift(): lax.ppermute(array, axis, [(i, (i + step) % size) for i in range(size)])  12 us
    ppermute x7, waiting for transfers between devices, shift(): lax.ppermute(array, axis, [(i, (i + step) % size) for i in range(size)])  9.97 us
    pallas_call x1, Pallas kernels, early_forward(): pl.pallas_call(early_forward_kernel, in_specs=[WHOLE] * 9 + [ANY] * len(a...  9.32 us
    pallas_call x2, Pallas kernels, coarse_backward(): pl.pallas_call(partial(coarse_backward_kernel, heads), in_specs=[WHOLE] *...  6.71 us
    pallas_call x2, Pallas kernels, local_backward(): pl.pallas_call(partial(local_backward_kernel, heads, [part[:2] for part i...  6.23 us
    pallas_call x1, Pallas kernels, project(): pl.pallas_call(project_kernel, in_specs=[WHOLE] * 2 + [ANY], out_specs=[W...  3.68 us
  transfers between devices with their start and end apart: 25, of which 15 were waited for; matrix products, arithmetic and copies ran while one was open for 0% of the time, Pallas kernels for 32%

commit v1 on v0

--- a/solution.py
+++ b/solution.py
@@ -23,11 +23,12 @@
 BIG = float(2**30)
 F32 = jnp.float32
 BF16 = jnp.bfloat16
+LARGE = pl.CostEstimate(flops=2 * 10**10, bytes_accessed=1024, transcendentals=0)
 SMALL = pl.CostEstimate(flops=1024, bytes_accessed=1024, transcendentals=0)
 
 
 def params(mebibytes):
-    return pltpu.CompilerParams(vmem_limit_bytes=mebibytes * 2**20)
+    return pltpu.CompilerParams(vmem_limit_bytes=int(mebibytes * 2**20))
 
 
 def swap(array, axis, bits):
@@ -37,6 +38,11 @@
 def shift(array, axis, step):
     size = lax.axis_size(axis)
     return lax.ppermute(array, axis, [(i, (i + step) % size) for i in range(size)])
+
+
+def position(place_ref):
+    place = place_ref[0]
+    return place >> 5, (place >> 4) & 1, (place >> 3) & 1, (place >> 1) & 3, place & 1
 
 
 def dot_nt(a, b):
@@ -399,7 +405,7 @@
         out_specs=[WHOLE] * 2,
         out_shape=[jax.ShapeDtypeStruct((ROWS, D), BF16), MARK],
         compiler_params=params(8),
-        cost_estimate=SMALL,
+        cost_estimate=LARGE,
     )(attention, weight, after)
 
 
@@ -424,7 +430,7 @@
 
 def grad_weight_kernel(place_ref, ot_ref, c_ref, keep_ref, give_ref, mark_ref, lhs):
     mark_ref[...] = jnp.zeros_like(mark_ref)
-    core, y = place_ref[0], place_ref[1]
+    _, _, core, y, _ = position(place_ref)
     for slot in range(2):
         half = core if slot == 0 else 1 - core
         for step in range(4):
@@ -505,7 +511,7 @@
 
 def y_sum_kernel(place_ref, *refs):
     for step, out in enumerate(refs[len(refs) - 4 :]):
-        at = pl.ds(pl.multiple_of(lax.rem(place_ref[2] + step, 4) * 32, 32), 32)
+        at = pl.ds(pl.multiple_of(lax.rem(position(place_ref)[0] + step, 4) * 32, 32), 32)
         out[...] = (refs[0][at, :].astype(F32) + refs[1][at, :].astype(F32) + refs[2][at, :].astype(F32)).astype(BF16)
 
 
@@ -620,7 +626,7 @@
 
 def last_sum_kernel(place_ref, *refs):
     outs = refs[len(refs) - 4 :]
-    z_lo, z_hi = place_ref[3], place_ref[4]
+    _, z_lo, _, _, z_hi = position(place_ref)
     sums = add_all(refs[:4], slice(None))
     for lo in range(2):
         for hi in range(2):
@@ -661,12 +667,7 @@
 def body(query, key, value, segment_ids, out_weight, cotangent):
     query, key, value = query[0], key[0], value[0]
     cotangent = cotangent[0]
-    index = lax.axis_index("ctx")
-    other = lax.axis_index("dp")
-    core, x = jnp.bitwise_and(index, 1), jnp.right_shift(index, 2)
-    z_lo = jnp.bitwise_and(jnp.right_shift(index, 1), 1)
-    y, z_hi = jnp.right_shift(other, 1), jnp.bitwise_and(other, 1)
-    place = jnp.stack([core, y, x, z_lo, z_hi]).astype(jnp.int32)
+    place = lax.axis_index(("ctx", "dp")).astype(jnp.int32).reshape(1)
 
     one, two, three, fq, fk, mark = pool(place, segment_ids, key, value)
     from_z = swap(one, "ctx", 2)
@@ -694,13 +695,13 @@
         query, key, value, grad_across, rows, early, partials, range(4), (), [own_one]
     )
     up, down = relay([parts[1], parts[4], lower, upper], [mark])
-    near, far = second_sum(own_two, back_xz, [up])
+    output, mark = project(attention, out_weight, up)
+    grad_query, dk, dv, mark = local_backward(
+        query, key, value, grad_across, rows, early, partials, range(4, HEADS), earlier, [mark]
+    )
+    near, far = second_sum(own_two, back_xz, [mark])
     near = swap(near, "ctx", 4)
-    grad_query, dk, dv, mark = local_backward(
-        query, key, value, grad_across, rows, early, partials, range(4, HEADS), earlier, [far]
-    )
-    output, mark = project(attention, out_weight, mark)
-    parts = y_sum(place, [parts[0], shift(up, "dp", 2), shift(down, "dp", -2)], [mark])
+    parts = y_sum(place, [parts[0], shift(up, "dp", 2), shift(down, "dp", -2)], [far])
     far = third_sum(far, near, [parts[0]])
     parts = [parts[0]] + [shift(parts[step], "ctx", 4 * step) for step in (1, 2, 3)]
     parts = last_sum(place, parts, [far])

time: 101 us -> 97.8 us (0.968)
  waiting for transfers between devices: 26.1 us -> 23.5 us
  starting transfers between devices: 28.6 us -> 30.8 us
  Pallas kernels: 41.6 us -> 39.5 us
    ppermute x17, starting transfers between devices: 16.1 us -> 19.2 us  [swap(): lax.ppermute(array, axis, [(i, i ^ bits) for i in range(lax.axis_size(axi...]
    ppermute x7, waiting for transfers between devices: 9.97 us -> 7.11 us  [shift(): lax.ppermute(array, axis, [(i, (i + step) % size) for i in range(size)])]
  transfers between devices with their start and end apart: 25 -> 25, of which waited for: 15 -> 12; matrix products, arithmetic and copies ran while one was open for 0% -> 0% of each run, Pallas kernels for 32% -> 33%
where the time goes in v1:
time: 97.8 us; the launch traced here: 97.7 us
  Pallas kernels  39.5 us (40%)
  starting transfers between devices  30.8 us (31%)
  waiting for transfers between devices  23.5 us (24%)
  local copies, waits for them, and re-layouts  3.03 us (3%)
    ppermute x17, starting transfers between devices, swap(): lax.ppermute(array, axis, [(i, i ^ bits) for i in range(lax.axis_size(axi...  19.2 us
    ppermute x17, waiting for transfers between devices, swap(): lax.ppermute(array, axis, [(i, i ^ bits) for i in range(lax.axis_size(axi...  13.9 us
    ppermute x7, starting transfers between devices, shift(): lax.ppermute(array, axis, [(i, (i + step) % size) for i in range(size)])  11.6 us
    pallas_call x1, Pallas kernels, early_forward(): pl.pallas_call(early_forward_kernel, in_specs=[WHOLE] * 9 + [ANY] * len(a...  9.35 us
    ppermute x7, waiting for transfers between devices, shift(): lax.ppermute(array, axis, [(i, (i + step) % size) for i in range(size)])  7.11 us
    pallas_call x2, Pallas kernels, coarse_backward(): pl.pallas_call(partial(coarse_backward_kernel, heads), in_specs=[WHOLE] *...  6.7 us
    pallas_call x2, Pallas kernels, local_backward(): pl.pallas_call(partial(local_backward_kernel, heads, [part[:2] for part i...  6.23 us
    pallas_call x1, Pallas kernels, project(): pl.pallas_call(project_kernel, in_specs=[WHOLE] * 2 + [ANY], out_specs=[W...  3.68 us
  transfers between devices with their start and end apart: 25, of which 12 were waited for; matrix products, arithmetic and copies ran while one was open for 0% of the time, Pallas kernels for 33%

profile of v1, /device:TPU:0, one launch (start us, length us, event | category | flops | bytes accessed | tf_op | source)
XLA Modules:
  0.0 97.7 jit_solution(6280831837031099417)
XLA Ops:
  0.7 0.8 copy-done.6
  1.5 2.1 %shard_map.102 = (bf16[128,2176]{1,0:T(8,128)(2,1)S(1)}, bf16[64,2176]{1,0:T(8,128)(2,1)S(1)}, bf16[32,2176]{1,0:T(8,128)(2,1)S(1)}, bf16[512,128]{1,0:T(8,128)(...) custom-call(s32[1]{0:T(128)} %bitcast.2.place_ref, s32[1,512]{1,0:T(1,128)S(1)} %copy-done.6, ...), custom_call_target="tpu_custom_call" | custom-call | flops 1024 | bytes 1024 | tf_op jit(solution)/shard_map/pallas_call | solution.py:130
  3.6 2.1 %collective-permute-start = (bf16[128,2176]{1,0:T(8,128)(2,1)S(1)}, bf16[128,2176]{1,0:T(8,128)(2,1)S(1)}, u32[]{:S(2)}, u32[]{:S(2)}) collective-permute-start(bf16[128,2176]{1,0:T(8,128)(2,1)S(1)} %get-tuple-element.70), channel_id=1, source_target_pairs={{0,16},{8,24},{16,0},{24,8},{32,48},{40,56},{48,32},{56,40},{64,80... | collective-permute-start | bytes 1671176 | tf_op jit(solution)/shard_map/ppermute | solution.py:35
  5.6 1.5 %collective-permute-start.1 = (bf16[64,2176]{1,0:T(8,128)(2,1)S(1)}, bf16[64,2176]{1,0:T(8,128)(2,1)S(1)}, u32[]{:S(2)}, u32[]{:S(2)}) collective-permute-start(bf16[64,2176]{1,0:T(8,128)(2,1)S(1)} %get-tuple-element.74), channel_id=1, source_target_pairs={{0,32},{8,40},{16,48},{24,56},{32,0},{40,8},{48,16},{56,24},{64,96... | collective-permute-start | bytes 835592 | tf_op jit(solution)/shard_map/ppermute | solution.py:35
  7.1 2.7 %collective-permute-start.3 = (bf16[32,2176]{1,0:T(8,128)(2,1)S(1)}, bf16[32,2176]{1,0:T(8,128)(2,1)S(1)}, u32[]{:S(2)}, u32[]{:S(2)}) collective-permute-start(bf16[32,2176]{1,0:T(8,128)(2,1)S(1)} %get-tuple-element.75), channel_id=1, source_target_pairs={{0,64},{8,72},{16,80},{24,88},{32,96},{40,104},{48,112},{56,120},{... | collective-permute-start | bytes 417800 | tf_op jit(solution)/shard_map/ppermute | solution.py:35
  9.9 0.5 collective-permute-start.2
  10.3 2.2 %copy-done.4 = bf16[1024,2048]{1,0:T(8,128)(2,1)S(1)} copy-done((bf16[1024,2048]{1,0:T(8,128)(2,1)S(1)}, bf16[1024,2048]{1,0:T(8,128)(2,1)}, u32[]{:S(2)}) %copy-start.4) | copy-done | bytes 4194328
  12.5 2.4 %shard_map.101 = (bf16[512,1024]{1,0:T(8,128)(2,1)S(1)}, bf16[1024,512]{1,0:T(8,128)(2,1)S(1)}) custom-call(bf16[512,2048]{1,0:T(8,128)(2,1)S(1)} %bitcast.23, bf16[1024,2048]{1,0:T(8,128)(2,1)S(1)} %copy-done.4), custom_call_target="tpu_custom_call" | custom-call | flops 1024 | bytes 1024 | tf_op jit(solution)/shard_map/pallas_call | solution.py:385
  15.0 0.0 copy-start
  15.0 0.0 copy-start.1
  15.0 4.0 %collective-permute-done.3.refs_2_ = bf16[32,2176]{1,0:T(8,128)(2,1)S(1)} collective-permute-done((bf16[32,2176]{1,0:T(8,128)(2,1)S(1)}, bf16[32,2176]{1,0:T(8,128)(2,1)S(1)}, u32[]{:S(2)}, u32[]{:S(2)}) %collective-permute-start.3) | collective-permute-done | bytes 139296 | tf_op jit(solution)/shard_map/ppermute | solution.py:35
  19.0 0.0 collective-permute-done.1.refs_0_
  19.1 0.1 collective-permute-start.5
  19.2 0.0 collective-permute-done.refs_5_.refs_6_
  19.2 0.5 collective-permute-start.4
  19.7 0.3 collective-permute-start.6
  20.0 1.1 %collective-permute-done.5.refs_8_.refs_9_ = bf16[128,2176]{1,0:T(8,128)(2,1)S(1)} collective-permute-done((bf16[128,2176]{1,0:T(8,128)(2,1)S(1)}, bf16[128,2176]{1,0:T(8,128)(2,1)S(1)}, u32[]{:S(2)}, u32[]{:S(2)}) %collective-permute-start.5) | collective-permute-done | bytes 557088 | tf_op jit(solution)/shard_map/ppermute | solution.py:35
  21.1 0.8 collective-permute-done.4.refs_7_.refs_8_
  21.9 9.3 %shard_map.105 = (bf16[8,1024,512]{2,1,0:T(8,128)(2,1)S(1)}, f32[1024,512]{1,0:T(8,128)S(1)}, f32[8,8,512]{2,1,0:T(8,128)S(1)}) custom-call(bf16[512,1024]{1,0:T(8,128)(2,1)S(1)} %bitcast.9, bf16[512,1024]{1,0:T(8,128)(2,1)S(1)} %bitcast.16, bf16[512,1024]{1,0:T(8,128)(2,1)S(1)} %bitcast.20, bf16[512,128]{1,0:T(8,128)(2,1)S(1)} %get-tuple-element.68.refs_3_.refs_2_, ...), custom_call_target="tpu_custom_call" | custom-call | flops 1024 | bytes 1024 | tf_op jit(solution)/shard_map/pallas_call | solution.py:223
  31.3 3.0 %collective-permute-done.6.refs_5_.refs_10_ = bf16[128,2176]{1,0:T(8,128)(2,1)S(1)} collective-permute-done((bf16[128,2176]{1,0:T(8,128)(2,1)S(1)}, bf16[128,2176]{1,0:T(8,128)(2,1)S(1)}, u32[]{:S(2)}, u32[]{:S(2)}) %collective-permute-start.6) | collective-permute-done | bytes 557088 | tf_op jit(solution)/shard_map/ppermute | solution.py:35
  34.3 0.0 collective-permute-start.7
  34.3 2.0 %collective-permute-done.7.refs_6_.refs_11_ = bf16[128,2176]{1,0:T(8,128)(2,1)S(1)} collective-permute-done((bf16[128,2176]{1,0:T(8,128)(2,1)S(1)}, bf16[128,2176]{1,0:T(8,128)(2,1)S(1)}, u32[]{:S(2)}, u32[]{:S(2)}) %collective-permute-start.7) | collective-permute-done | bytes 557088 | tf_op jit(solution)/shard_map/ppermute | solution.py:35
  36.3 2.6 %shard_map.106 = (bf16[8,256,512]{2,1,0:T(8,128)(2,1)S(1)}, bf16[1024,512]{1,0:T(8,128)(2,1)S(1)}, f32[8,8,512]{2,1,0:T(8,128)S(1)}) custom-call(bf16[512,1024]{1,0:T(8,128)(2,1)S(1)} %bitcast.10, bf16[1024,512]{1,0:T(8,128)(2,1)S(1)} %get-tuple-element.67.refs_1_.refs_2_.refs_3_, bf16[512,128]{1,0:T(8,128)(2,1)S(1)} %get-tuple-element.68.refs_3_.refs_2_, ...), custom_call_target="tpu_custom_call" | custom-call | flops 1024 | bytes 1024 | tf_op jit(solution)/shard_map/pallas_call | solution.py:264
  38.9 2.4 %shard_map.107 = (bf16[512,2048]{1,0:T(8,128)(2,1)S(1)}, bf16[512,2048]{1,0:T(8,128)(2,1)S(1)}, f32[8,128]{1,0:T(8,128)S(1)}) custom-call(s32[1]{0:T(128)} %bitcast.2.place_ref, bf16[1024,512]{1,0:T(8,128)(2,1)S(1)} %get-tuple-element.82.ot_ref.a_ref, bf16[512,2048]{1,0:T(8,128)(2,1)S(1)} %bitcast.24), custom_call_target="tpu_custom_call" | custom-call | flops 1024 | bytes 1024 | tf_op jit(solution)/shard_map/pallas_call | solution.py:450
  41.3 0.4 collective-permute-start.8
  41.7 5.3 %shard_map.108 = (bf16[2,384,896]{2,1,0:T(8,128)(2,1)S(1)}, bf16[2,384,896]{2,1,0:T(8,128)(2,1)S(1)}, f32[896,512]{1,0:T(8,128)S(1)}, f32[8,128]{1,0:T(8,128)S(1)}) custom-call(bf16[512,1024]{1,0:T(8,128)(2,1)S(1)} %bitcast.11, bf16[512,1024]{1,0:T(8,128)(2,1)S(1)} %get-tuple-element.76.refs_3_.refs_1_, ...), custom_call_target="tpu_custom_call" | custom-call | flops 1024 | bytes 1024 | tf_op jit(solution)/shard_map/pallas_call | solution.py:320
  46.9 0.5 collective-permute-start.11
  47.4 0.5 shard_map.109
  47.9 1.7 %collective-permute-start.9 = (bf16[64,2048]{1,0:T(8,128)(2,1)S(1)}, bf16[64,2048]{1,0:T(8,128)(2,1)S(1)}, u32[]{:S(2)}, u32[]{:S(2)}) collective-permute-start(bf16[64,2048]{1,0:T(8,128)(2,1)S(1)} %get-tuple-element.92), channel_id=1, source_target_pairs={{0,2},{1,3},{2,4},{3,5},{4,6},{5,7},{6,0},{7,1},{8,10},{9,11},{10,... | collective-permute-start | bytes 786440 | tf_op jit(solution)/shard_map/ppermute | solution.py:40
  49.5 1.7 %collective-permute-start.10 = (bf16[64,2048]{1,0:T(8,128)(2,1)S(1)}, bf16[64,2048]{1,0:T(8,128)(2,1)S(1)}, u32[]{:S(2)}, u32[]{:S(2)}) collective-permute-start(bf16[64,2048]{1,0:T(8,128)(2,1)S(1)} %get-tuple-element.93), channel_id=1, source_target_pairs={{0,6},{1,7},{2,0},{3,1},{4,2},{5,3},{6,4},{7,5},{8,14},{9,15},{10,... | collective-permute-start | bytes 786440 | tf_op jit(solution)/shard_map/ppermute | solution.py:40
  51.2 1.4 %shard_map.110 = (bf16[2,384,128]{2,1,0:T(8,128)(2,1)S(1)}, bf16[2,384,128]{2,1,0:T(8,128)(2,1)S(1)}, f32[128,512]{1,0:T(8,128)S(1)}, f32[8,128]{1,0:T(8,128)}) custom-call(bf16[512,1024]{1,0:T(8,128)(2,1)S(1)} %bitcast.12, bf16[512,1024]{1,0:T(8,128)(2,1)S(1)} %get-tuple-element.76.refs_3_.refs_1_, ...), custom_call_target="tpu_custom_call" | custom-call | flops 1024 | bytes 1024 | tf_op jit(solution)/shard_map/pallas_call | solution.py:320
  52.6 0.0 collective-permute-start.12
  52.6 0.0 collective-permute-done.11.refs_1_
  52.6 1.4 %collective-permute-done.12.refs_3_ = bf16[2,384,128]{2,1,0:T(8,128)(2,1)S(1)} collective-permute-done((bf16[2,384,128]{2,1,0:T(8,128)(2,1)S(1)}, bf16[2,384,128]{2,1,0:T(8,128)(2,1)S(1)}, u32[]{:S(2)}, u32[]{:S(2)}) %collective-permute-start.12) | collective-permute-done | bytes 196640 | tf_op jit(solution)/shard_map/ppermute | solution.py:35
  54.1 0.4 shard_map.111
  54.4 0.8 collective-permute-start.14
  55.3 2.6 %shard_map.112 = (bf16[512,512]{1,0:T(8,128)(2,1)S(1)}, bf16[512,512]{1,0:T(8,128)(2,1)S(1)}, bf16[512,512]{1,0:T(8,128)(2,1)S(1)}, f32[8,128]{1,0:T(8,128)S(1)}) custom-call(bf16[512,1024]{1,0:T(8,128)(2,1)S(1)} %bitcast.13, bf16[512,1024]{1,0:T(8,128)(2,1)S(1)} %bitcast.17, bf16[512,1024]{1,0:T(8,128)(2,1)S(1)} %bitcast.21, ...), custom_call_target="tpu_custom_call" | custom-call | flops 1024 | bytes 1024 | tf_op jit(solution)/shard_map/pallas_call | solution.py:367
  57.9 0.0 collective-permute-done.10.upper_ref
  57.9 0.1 shard_map.113
  58.0 2.8 %collective-permute-start.17 = (bf16[128,2048]{1,0:T(8,128)(2,1)S(1)}, bf16[128,2048]{1,0:T(8,128)(2,1)S(1)}, u32[]{:S(2)}, u32[]{:S(2)}) collective-permute-start(bf16[128,2048]{1,0:T(8,128)(2,1)S(1)} %get-tuple-element.117), channel_id=1, source_target_pairs={{0,6},{1,7},{2,0},{3,1},{4,2},{5,3},{6,4},{7,5},{8,14},{9,15},{10,... | collective-permute-start | bytes 1572872 | tf_op jit(solution)/shard_map/ppermute | solution.py:40
  60.8 0.0 collective-permute-start.16
  60.8 3.7 %shard_map.114 = (bf16[512,2048]{1,0:T(8,128)(2,1)}, f32[8,128]{1,0:T(8,128)S(1)}) custom-call(bf16[1024,512]{1,0:T(8,128)(2,1)S(1)} %get-tuple-element.82.ot_ref.a_ref, bf16[1024,2048]{1,0:T(8,128)(2,1)S(1)} %copy-done.5, bf16[128,2048]{1,0:T(8,128)(2,1)S(1)} %get-tuple-element.102._), custom_call_target="tpu_custom_call" | custom-call | flops 20000000000 | bytes 1024 | tf_op jit(solution)/shard_map/pallas_call | solution.py:402
  64.5 3.6 %shard_map.115 = (bf16[512,1024]{1,0:T(8,128)(2,1)}, bf16[512,1024]{1,0:T(8,128)(2,1)S(1)}, bf16[512,1024]{1,0:T(8,128)(2,1)S(1)}, f32[8,128]{1,0:T(8,128)S(1)}) custom-call(bf16[512,1024]{1,0:T(8,128)(2,1)S(1)} %bitcast.14, bf16[512,1024]{1,0:T(8,128)(2,1)S(1)} %bitcast.18, bf16[512,1024]{1,0:T(8,128)(2,1)S(1)} %bitcast.22, ...), custom_call_target="tpu_custom_call" | custom-call | flops 1024 | bytes 1024 | tf_op jit(solution)/shard_map/pallas_call | solution.py:367
  68.2 0.3 collective-permute-done.14.received_ref
  68.5 0.1 shard_map.116
  68.6 0.6 collective-permute-start.15
  69.2 1.7 %collective-permute-start.13 = (bf16[2,128,1024]{2,1,0:T(8,128)(2,1)S(1)}, bf16[2,128,1024]{2,1,0:T(8,128)(2,1)S(1)}, u32[]{:S(2)}, u32[]{:S(2)}) collective-permute-start(bf16[2,128,1024]{2,1,0:T(8,128)(2,1)S(1)} %get-tuple-element.100.refs_7_), channel_id=1, source_target_pairs={{0,16},{8,24},{16,0},{24,8},{32,48},{40,56},{48,32},{56,40},{64,80... | collective-permute-start | bytes 1572872 | tf_op jit(solution)/shard_map/ppermute | solution.py:35
  70.9 0.9 collective-permute-done.17.refs_2_
  71.8 2.9 %collective-permute-done.16.refs_1_ = bf16[128,2048]{1,0:T(8,128)(2,1)S(1)} collective-permute-done((bf16[128,2048]{1,0:T(8,128)(2,1)S(1)}, bf16[128,2048]{1,0:T(8,128)(2,1)S(1)}, u32[]{:S(2)}, u32[]{:S(2)}) %collective-permute-start.16) | collective-permute-done | bytes 524320 | tf_op jit(solution)/shard_map/ppermute | solution.py:40
  74.7 0.2 shard_map.117
  74.9 1.4 %collective-permute-start.19 = (bf16[32,2048]{1,0:T(8,128)(2,1)S(1)}, bf16[32,2048]{1,0:T(8,128)(2,1)S(1)}, u32[]{:S(2)}, u32[]{:S(2)}) collective-permute-start(bf16[32,2048]{1,0:T(8,128)(2,1)S(1)} %get-tuple-element.119), channel_id=1, source_target_pairs={{0,32},{8,40},{16,48},{24,56},{32,64},{40,72},{48,80},{56,88},{64,... | collective-permute-start | bytes 393224 | tf_op jit(solution)/shard_map/ppermute | solution.py:40
  76.3 2.7 %collective-permute-start.20 = (bf16[32,2048]{1,0:T(8,128)(2,1)S(1)}, bf16[32,2048]{1,0:T(8,128)(2,1)S(1)}, u32[]{:S(2)}, u32[]{:S(2)}) collective-permute-start(bf16[32,2048]{1,0:T(8,128)(2,1)S(1)} %get-tuple-element.120), channel_id=1, source_target_pairs={{0,64},{8,72},{16,80},{24,88},{32,96},{40,104},{48,112},{56,120},{... | collective-permute-start | bytes 393224 | tf_op jit(solution)/shard_map/ppermute | solution.py:40
  79.0 1.4 %collective-permute-start.21 = (bf16[32,2048]{1,0:T(8,128)(2,1)S(1)}, bf16[32,2048]{1,0:T(8,128)(2,1)S(1)}, u32[]{:S(2)}, u32[]{:S(2)}) collective-permute-start(bf16[32,2048]{1,0:T(8,128)(2,1)S(1)} %get-tuple-element.121), channel_id=1, source_target_pairs={{0,96},{8,104},{16,112},{24,120},{32,0},{40,8},{48,16},{56,24},{64... | collective-permute-start | bytes 393224 | tf_op jit(solution)/shard_map/ppermute | solution.py:40
  80.4 0.0 collective-permute-done.15.near_ref.refs_3_
  80.5 2.2 %collective-permute-start.18 = (bf16[2,32,1024]{2,1,0:T(8,128)(2,1)S(1)}, bf16[2,32,1024]{2,1,0:T(8,128)(2,1)S(1)}, u32[]{:S(2)}, u32[]{:S(2)}) collective-permute-start(bf16[2,32,1024]{2,1,0:T(8,128)(2,1)S(1)} %shard_map.118.refs_4_), channel_id=1, source_target_pairs={{0,96},{8,104},{16,112},{24,120},{32,64},{40,72},{48,80},{56,88},{... | collective-permute-start | bytes 393224 | tf_op jit(solution)/shard_map/ppermute | solution.py:35
  82.6 0.0 collective-permute-done.19.refs_1_
  82.6 3.3 %collective-permute-done.20.refs_2_ = bf16[32,2048]{1,0:T(8,128)(2,1)S(1)} collective-permute-done((bf16[32,2048]{1,0:T(8,128)(2,1)S(1)}, bf16[32,2048]{1,0:T(8,128)(2,1)S(1)}, u32[]{:S(2)}, u32[]{:S(2)}) %collective-permute-start.20) | collective-permute-done | bytes 131104 | tf_op jit(solution)/shard_map/ppermute | solution.py:40
  86.0 0.2 shard_map.119
  86.1 1.8 %collective-permute-start.22 = (f32[8,2048]{1,0:T(8,128)S(1)}, f32[8,2048]{1,0:T(8,128)S(1)}, u32[]{:S(2)}, u32[]{:S(2)}) collective-permute-start(f32[8,2048]{1,0:T(8,128)S(1)} %get-tuple-element.125), channel_id=1, source_target_pairs={{0,16},{8,24},{16,0},{24,8},{32,48},{40,56},{48,32},{56,40},{64,80... | collective-permute-start | bytes 196616 | tf_op jit(solution)/shard_map/ppermute | solution.py:35
  87.9 3.6 %collective-permute-start.23 = (f32[8,2048]{1,0:T(8,128)S(1)}, f32[8,2048]{1,0:T(8,128)S(1)}, u32[]{:S(2)}, u32[]{:S(2)}) collective-permute-start(f32[8,2048]{1,0:T(8,128)S(1)} %get-tuple-element.126), channel_id=1, source_target_pairs={{0,1},{1,0},{2,3},{3,2},{4,5},{5,4},{6,7},{7,6},{8,9},{9,8},{10,11... | collective-permute-start | bytes 196616 | tf_op jit(solution)/shard_map/ppermute | solution.py:35
  91.5 1.8 %shard_map.120 = (bf16[512,1024]{1,0:T(8,128)(2,1)}, bf16[512,1024]{1,0:T(8,128)(2,1)}, f32[8,128]{1,0:T(8,128)S(1)}) custom-call(bf16[512,1024]{1,0:T(8,128)(2,1)S(1)} %get-tuple-element.110.refs_0_, bf16[512,1024]{1,0:T(8,128)(2,1)S(1)} %get-tuple-element.111.refs_1_, bf16[2,128,1024]{2,1,0:T(8,128)(2,1)S(1)} %collective-permute-done.13.refs_2_, ...), custom_call_target="tpu_custom_call" | custom-call | flops 1024 | bytes 1024 | tf_op jit(solution)/shard_map/pallas_call | solution.py:611
  93.4 1.1 %collective-permute-done.23.refs_2_ = f32[8,2048]{1,0:T(8,128)S(1)} collective-permute-done((f32[8,2048]{1,0:T(8,128)S(1)}, f32[8,2048]{1,0:T(8,128)S(1)}, u32[]{:S(2)}, u32[]{:S(2)}) %collective-permute-start.23) | collective-permute-done | bytes 65568 | tf_op jit(solution)/shard_map/ppermute | solution.py:35
  94.5 2.5 %collective-permute-done.24.refs_3_ = f32[8,2048]{1,0:T(8,128)S(1)} collective-permute-done((f32[8,2048]{1,0:T(8,128)S(1)}, f32[8,2048]{1,0:T(8,128)S(1)}, u32[]{:S(2)}, u32[]{:S(2)}) %collective-permute-start.24) | collective-permute-done | bytes 65568 | tf_op jit(solution)/shard_map/ppermute | solution.py:712
  97.0 0.6 shard_map.121
  (21 shorter events, 0.1 us)
Async XLA Ops:
  0.6 9.7 %copy-start.3 = (bf16[1,512,2048]{2,1,0:T(8,128)(2,1)S(1)}, bf16[1,512,2048]{2,1,0:T(8,128)(2,1)}, u32[]{:S(2)}) copy-start(bf16[1,512,2048]{2,1,0:T(8,128)(2,1)} %param.11) | copy-start | bytes 6291460
  0.6 0.8 copy-start.6
  3.6 15.6 %collective-permute-start = (bf16[128,2176]{1,0:T(8,128)(2,1)S(1)}, bf16[128,2176]{1,0:T(8,128)(2,1)S(1)}, u32[]{:S(2)}, u32[]{:S(2)}) collective-permute-start(bf16[128,2176]{1,0:T(8,128)(2,1)S(1)} %get-tuple-element.70), channel_id=1, source_target_pairs={{0,16},{8,24},{16,0},{24,8},{32,48},{40,56},{48,32},{56,40},{64,80... | collective-permute-start | bytes 1671176 | tf_op jit(solution)/shard_map/ppermute | solution.py:35
  5.6 13.4 %collective-permute-start.1 = (bf16[64,2176]{1,0:T(8,128)(2,1)S(1)}, bf16[64,2176]{1,0:T(8,128)(2,1)S(1)}, u32[]{:S(2)}, u32[]{:S(2)}) collective-permute-start(bf16[64,2176]{1,0:T(8,128)(2,1)S(1)} %get-tuple-element.74), channel_id=1, source_target_pairs={{0,32},{8,40},{16,48},{24,56},{32,0},{40,8},{48,16},{56,24},{64,96... | collective-permute-start | bytes 835592 | tf_op jit(solution)/shard_map/ppermute | solution.py:35
  7.1 11.9 %collective-permute-start.3 = (bf16[32,2176]{1,0:T(8,128)(2,1)S(1)}, bf16[32,2176]{1,0:T(8,128)(2,1)S(1)}, u32[]{:S(2)}, u32[]{:S(2)}) collective-permute-start(bf16[32,2176]{1,0:T(8,128)(2,1)S(1)} %get-tuple-element.75), channel_id=1, source_target_pairs={{0,64},{8,72},{16,80},{24,88},{32,96},{40,104},{48,112},{56,120},{... | collective-permute-start | bytes 417800 | tf_op jit(solution)/shard_map/ppermute | solution.py:35
  9.9 9.2 %collective-permute-start.2 = (bf16[32,2176]{1,0:T(8,128)(2,1)S(1)}, bf16[32,2176]{1,0:T(8,128)(2,1)S(1)}, u32[]{:S(2)}, u32[]{:S(2)}) collective-permute-start(bf16[32,2176]{1,0:T(8,128)(2,1)S(1)} %get-tuple-element.75), channel_id=1, source_target_pairs={{0,96},{8,104},{16,112},{24,120},{32,64},{40,72},{48,80},{56,88},{... | collective-permute-start | bytes 417800 | tf_op jit(solution)/shard_map/ppermute | solution.py:35
  10.3 2.2 %copy-start.4 = (bf16[1024,2048]{1,0:T(8,128)(2,1)S(1)}, bf16[1024,2048]{1,0:T(8,128)(2,1)}, u32[]{:S(2)}) copy-start(bf16[1024,2048]{1,0:T(8,128)(2,1)} %w_ref.3) | copy-start | bytes 12582916
  12.5 9.4 %copy-start.2 = (bf16[1,512,1024]{2,1,0:T(8,128)(2,1)S(1)}, bf16[1,512,1024]{2,1,0:T(8,128)(2,1)}, u32[]{:S(2)}) copy-start(bf16[1,512,1024]{2,1,0:T(8,128)(2,1)} %param.8) | copy-start | bytes 3145732
  15.0 7.0 %copy-start = (bf16[1,512,1024]{2,1,0:T(8,128)(2,1)S(1)}, bf16[1,512,1024]{2,1,0:T(8,128)(2,1)}, u32[]{:S(2)}) copy-start(bf16[1,512,1024]{2,1,0:T(8,128)(2,1)} %param.6) | copy-start | bytes 3145732
  15.0 6.9 %copy-start.1 = (bf16[1,512,1024]{2,1,0:T(8,128)(2,1)S(1)}, bf16[1,512,1024]{2,1,0:T(8,128)(2,1)}, u32[]{:S(2)}) copy-start(bf16[1,512,1024]{2,1,0:T(8,128)(2,1)} %param.7) | copy-start | bytes 3145732
  19.1 2.0 %collective-permute-start.5 = (bf16[128,2176]{1,0:T(8,128)(2,1)S(1)}, bf16[128,2176]{1,0:T(8,128)(2,1)S(1)}, u32[]{:S(2)}, u32[]{:S(2)}) collective-permute-start(bf16[128,2176]{1,0:T(8,128)(2,1)S(1)} %shard_map.104.refs_6_.refs_7_), channel_id=1, source_target_pairs={{0,8},{8,0},{16,24},{24,16},{32,40},{40,32},{48,56},{56,48},{64,72... | collective-permute-start | bytes 1671176 | tf_op jit(solution)/shard_map/ppermute | solution.py:35
  19.2 2.7 %collective-permute-start.4 = (bf16[128,2176]{1,0:T(8,128)(2,1)S(1)}, bf16[128,2176]{1,0:T(8,128)(2,1)S(1)}, u32[]{:S(2)}, u32[]{:S(2)}) collective-permute-start(bf16[128,2176]{1,0:T(8,128)(2,1)S(1)} %collective-permute-done.refs_5_.refs_6_), channel_id=1, source_target_pairs={{0,8},{8,0},{16,24},{24,16},{32,40},{40,32},{48,56},{56,48},{64,72... | collective-permute-start | bytes 1671176 | tf_op jit(solution)/shard_map/ppermute | solution.py:35
  19.7 14.6 %collective-permute-start.6 = (bf16[128,2176]{1,0:T(8,128)(2,1)S(1)}, bf16[128,2176]{1,0:T(8,128)(2,1)S(1)}, u32[]{:S(2)}, u32[]{:S(2)}) collective-permute-start(bf16[128,2176]{1,0:T(8,128)(2,1)S(1)} %shard_map.104.refs_6_.refs_7_), channel_id=1, source_target_pairs={{0,16},{8,24},{16,0},{24,8},{32,48},{40,56},{48,32},{56,40},{64,80... | collective-permute-start | bytes 1671176 | tf_op jit(solution)/shard_map/ppermute | solution.py:35
  34.3 2.0 %collective-permute-start.7 = (bf16[128,2176]{1,0:T(8,128)(2,1)S(1)}, bf16[128,2176]{1,0:T(8,128)(2,1)S(1)}, u32[]{:S(2)}, u32[]{:S(2)}) collective-permute-start(bf16[128,2176]{1,0:T(8,128)(2,1)S(1)} %collective-permute-done.6.refs_5_.refs_10_), channel_id=1, source_target_pairs={{0,8},{8,0},{16,24},{24,16},{32,40},{40,32},{48,56},{56,48},{64,72... | collective-permute-start | bytes 1671176 | tf_op jit(solution)/shard_map/ppermute | solution.py:35
  41.3 6.1 %collective-permute-start.8 = (bf16[512,2048]{1,0:T(8,128)(2,1)S(1)}, bf16[512,2048]{1,0:T(8,128)(2,1)S(1)}, u32[]{:S(2)}, u32[]{:S(2)}) collective-permute-start(bf16[512,2048]{1,0:T(8,128)(2,1)S(1)} %get-tuple-element.84), channel_id=1, source_target_pairs={{0,8},{8,0},{16,24},{24,16},{32,40},{40,32},{48,56},{56,48},{64,72... | collective-permute-start | bytes 6291464 | tf_op jit(solution)/shard_map/ppermute | solution.py:35
  46.9 5.7 %collective-permute-start.11 = (bf16[2,384,896]{2,1,0:T(8,128)(2,1)S(1)}, bf16[2,384,896]{2,1,0:T(8,128)(2,1)S(1)}, u32[]{:S(2)}, u32[]{:S(2)}) collective-permute-start(bf16[2,384,896]{2,1,0:T(8,128)(2,1)S(1)} %get-tuple-element.96), channel_id=1, source_target_pairs={{0,8},{8,0},{16,24},{24,16},{32,40},{40,32},{48,56},{56,48},{64,72... | collective-permute-start | bytes 4128776 | tf_op jit(solution)/shard_map/ppermute | solution.py:35
  47.9 10.0 %collective-permute-start.9 = (bf16[64,2048]{1,0:T(8,128)(2,1)S(1)}, bf16[64,2048]{1,0:T(8,128)(2,1)S(1)}, u32[]{:S(2)}, u32[]{:S(2)}) collective-permute-start(bf16[64,2048]{1,0:T(8,128)(2,1)S(1)} %get-tuple-element.92), channel_id=1, source_target_pairs={{0,2},{1,3},{2,4},{3,5},{4,6},{5,7},{6,0},{7,1},{8,10},{9,11},{10,... | collective-permute-start | bytes 786440 | tf_op jit(solution)/shard_map/ppermute | solution.py:40
  49.5 8.3 %collective-permute-start.10 = (bf16[64,2048]{1,0:T(8,128)(2,1)S(1)}, bf16[64,2048]{1,0:T(8,128)(2,1)S(1)}, u32[]{:S(2)}, u32[]{:S(2)}) collective-permute-start(bf16[64,2048]{1,0:T(8,128)(2,1)S(1)} %get-tuple-element.93), channel_id=1, source_target_pairs={{0,6},{1,7},{2,0},{3,1},{4,2},{5,3},{6,4},{7,5},{8,14},{9,15},{10,... | collective-permute-start | bytes 786440 | tf_op jit(solution)/shard_map/ppermute | solution.py:40
  52.6 1.4 %collective-permute-start.12 = (bf16[2,384,128]{2,1,0:T(8,128)(2,1)S(1)}, bf16[2,384,128]{2,1,0:T(8,128)(2,1)S(1)}, u32[]{:S(2)}, u32[]{:S(2)}) collective-permute-start(bf16[2,384,128]{2,1,0:T(8,128)(2,1)S(1)} %get-tuple-element.99), channel_id=1, source_target_pairs={{0,8},{8,0},{16,24},{24,16},{32,40},{40,32},{48,56},{56,48},{64,72... | collective-permute-start | bytes 589832 | tf_op jit(solution)/shard_map/ppermute | solution.py:35
  54.4 14.0 %collective-permute-start.14 = (bf16[2,128,1024]{2,1,0:T(8,128)(2,1)S(1)}, bf16[2,128,1024]{2,1,0:T(8,128)(2,1)S(1)}, u32[]{:S(2)}, u32[]{:S(2)}) collective-permute-start(bf16[2,128,1024]{2,1,0:T(8,128)(2,1)S(1)} %get-tuple-element.113), channel_id=1, source_target_pairs={{0,16},{8,24},{16,0},{24,8},{32,48},{40,56},{48,32},{56,40},{64,80... | collective-permute-start | bytes 1572872 | tf_op jit(solution)/shard_map/ppermute | solution.py:35
  55.3 5.6 %copy-start.5 = (bf16[1024,2048]{1,0:T(8,128)(2,1)S(1)}, bf16[1024,2048]{1,0:T(8,128)(2,1)}, u32[]{:S(2)}) copy-start(bf16[1024,2048]{1,0:T(8,128)(2,1)} %w_ref.3) | copy-start | bytes 12582916
  58.0 13.8 %collective-permute-start.17 = (bf16[128,2048]{1,0:T(8,128)(2,1)S(1)}, bf16[128,2048]{1,0:T(8,128)(2,1)S(1)}, u32[]{:S(2)}, u32[]{:S(2)}) collective-permute-start(bf16[128,2048]{1,0:T(8,128)(2,1)S(1)} %get-tuple-element.117), channel_id=1, source_target_pairs={{0,6},{1,7},{2,0},{3,1},{4,2},{5,3},{6,4},{7,5},{8,14},{9,15},{10,... | collective-permute-start | bytes 1572872 | tf_op jit(solution)/shard_map/ppermute | solution.py:40
  60.8 13.9 %collective-permute-start.16 = (bf16[128,2048]{1,0:T(8,128)(2,1)S(1)}, bf16[128,2048]{1,0:T(8,128)(2,1)S(1)}, u32[]{:S(2)}, u32[]{:S(2)}) collective-permute-start(bf16[128,2048]{1,0:T(8,128)(2,1)S(1)} %get-tuple-element.102._), channel_id=1, source_target_pairs={{0,2},{1,3},{2,4},{3,5},{4,6},{5,7},{6,0},{7,1},{8,10},{9,11},{10,... | collective-permute-start | bytes 1572872 | tf_op jit(solution)/shard_map/ppermute | solution.py:40
  68.6 11.8 %collective-permute-start.15 = (bf16[2,96,1024]{2,1,0:T(8,128)(2,1)S(1)}, bf16[2,96,1024]{2,1,0:T(8,128)(2,1)S(1)}, u32[]{:S(2)}, u32[]{:S(2)}) collective-permute-start(bf16[2,96,1024]{2,1,0:T(8,128)(2,1)S(1)} %get-tuple-element.115), channel_id=1, source_target_pairs={{0,32},{8,40},{16,48},{24,56},{32,0},{40,8},{48,16},{56,24},{64,96... | collective-permute-start | bytes 1179656 | tf_op jit(solution)/shard_map/ppermute | solution.py:35
  69.2 22.3 %collective-permute-start.13 = (bf16[2,128,1024]{2,1,0:T(8,128)(2,1)S(1)}, bf16[2,128,1024]{2,1,0:T(8,128)(2,1)S(1)}, u32[]{:S(2)}, u32[]{:S(2)}) collective-permute-start(bf16[2,128,1024]{2,1,0:T(8,128)(2,1)S(1)} %get-tuple-element.100.refs_7_), channel_id=1, source_target_pairs={{0,16},{8,24},{16,0},{24,8},{32,48},{40,56},{48,32},{56,40},{64,80... | collective-permute-start | bytes 1572872 | tf_op jit(solution)/shard_map/ppermute | solution.py:35
  74.9 7.7 %collective-permute-start.19 = (bf16[32,2048]{1,0:T(8,128)(2,1)S(1)}, bf16[32,2048]{1,0:T(8,128)(2,1)S(1)}, u32[]{:S(2)}, u32[]{:S(2)}) collective-permute-start(bf16[32,2048]{1,0:T(8,128)(2,1)S(1)} %get-tuple-element.119), channel_id=1, source_target_pairs={{0,32},{8,40},{16,48},{24,56},{32,64},{40,72},{48,80},{56,88},{64,... | collective-permute-start | bytes 393224 | tf_op jit(solution)/shard_map/ppermute | solution.py:40
  76.3 9.7 %collective-permute-start.20 = (bf16[32,2048]{1,0:T(8,128)(2,1)S(1)}, bf16[32,2048]{1,0:T(8,128)(2,1)S(1)}, u32[]{:S(2)}, u32[]{:S(2)}) collective-permute-start(bf16[32,2048]{1,0:T(8,128)(2,1)S(1)} %get-tuple-element.120), channel_id=1, source_target_pairs={{0,64},{8,72},{16,80},{24,88},{32,96},{40,104},{48,112},{56,120},{... | collective-permute-start | bytes 393224 | tf_op jit(solution)/shard_map/ppermute | solution.py:40
  79.0 7.0 %collective-permute-start.21 = (bf16[32,2048]{1,0:T(8,128)(2,1)S(1)}, bf16[32,2048]{1,0:T(8,128)(2,1)S(1)}, u32[]{:S(2)}, u32[]{:S(2)}) collective-permute-start(bf16[32,2048]{1,0:T(8,128)(2,1)S(1)} %get-tuple-element.121), channel_id=1, source_target_pairs={{0,96},{8,104},{16,112},{24,120},{32,0},{40,8},{48,16},{56,24},{64... | collective-permute-start | bytes 393224 | tf_op jit(solution)/shard_map/ppermute | solution.py:40
  80.5 11.1 %collective-permute-start.18 = (bf16[2,32,1024]{2,1,0:T(8,128)(2,1)S(1)}, bf16[2,32,1024]{2,1,0:T(8,128)(2,1)S(1)}, u32[]{:S(2)}, u32[]{:S(2)}) collective-permute-start(bf16[2,32,1024]{2,1,0:T(8,128)(2,1)S(1)} %shard_map.118.refs_4_), channel_id=1, source_target_pairs={{0,96},{8,104},{16,112},{24,120},{32,64},{40,72},{48,80},{56,88},{... | collective-permute-start | bytes 393224 | tf_op jit(solution)/shard_map/ppermute | solution.py:35
  86.1 7.2 %collective-permute-start.22 = (f32[8,2048]{1,0:T(8,128)S(1)}, f32[8,2048]{1,0:T(8,128)S(1)}, u32[]{:S(2)}, u32[]{:S(2)}) collective-permute-start(f32[8,2048]{1,0:T(8,128)S(1)} %get-tuple-element.125), channel_id=1, source_target_pairs={{0,16},{8,24},{16,0},{24,8},{32,48},{40,56},{48,32},{56,40},{64,80... | collective-permute-start | bytes 196616 | tf_op jit(solution)/shard_map/ppermute | solution.py:35
  87.9 6.5 %collective-permute-start.23 = (f32[8,2048]{1,0:T(8,128)S(1)}, f32[8,2048]{1,0:T(8,128)S(1)}, u32[]{:S(2)}, u32[]{:S(2)}) collective-permute-start(f32[8,2048]{1,0:T(8,128)S(1)} %get-tuple-element.126), channel_id=1, source_target_pairs={{0,1},{1,0},{2,3},{3,2},{4,5},{5,4},{6,7},{7,6},{8,9},{9,8},{10,11... | collective-permute-start | bytes 196616 | tf_op jit(solution)/shard_map/ppermute | solution.py:35
  91.5 5.5 %collective-permute-start.24 = (f32[8,2048]{1,0:T(8,128)S(1)}, f32[8,2048]{1,0:T(8,128)S(1)}, u32[]{:S(2)}, u32[]{:S(2)}) collective-permute-start(f32[8,2048]{1,0:T(8,128)S(1)} %get-tuple-element.127), channel_id=1, source_target_pairs={{0,17},{1,16},{2,19},{3,18},{4,21},{5,20},{6,23},{7,22},{8,25},{9,... | collective-permute-start | bytes 196616 | tf_op jit(solution)/shard_map/ppermute | solution.py:712

commit v2 on v1

--- a/solution.py
+++ b/solution.py
@@ -485,11 +485,6 @@
     )(*arrays, *after)
 
 
-def add_all(refs, at):
-    terms = [ref[at].astype(F32) for ref in refs]
-    return (terms[0] + terms[1]) + (terms[2] + terms[3])
-
-
 def relay_kernel(one_ref, three_ref, lower_ref, upper_ref, *refs):
     up, down = refs[len(refs) - 2 :]
     up[:64, :] = (one_ref[:64, :].astype(F32) + lower_ref[...].astype(F32)).astype(BF16)
@@ -507,23 +502,6 @@
         compiler_params=params(8),
         cost_estimate=SMALL,
     )(*arrays, *after)
-
-
-def y_sum_kernel(place_ref, *refs):
-    for step, out in enumerate(refs[len(refs) - 4 :]):
-        at = pl.ds(pl.multiple_of(lax.rem(position(place_ref)[0] + step, 4) * 32, 32), 32)
-        out[...] = (refs[0][at, :].astype(F32) + refs[1][at, :].astype(F32) + refs[2][at, :].astype(F32)).astype(BF16)
-
-
-def y_sum(place, arrays, after):
-    return pl.pallas_call(
-        y_sum_kernel,
-        in_specs=[pl.BlockSpec(memory_space=pltpu.SMEM)] + [WHOLE] * 3 + [ANY] * len(after),
-        out_specs=[WHOLE] * 4,
-        out_shape=[jax.ShapeDtypeStruct((32, D), BF16)] * 4,
-        compiler_params=params(8),
-        cost_estimate=SMALL,
-    )(place, *arrays, *after)
 
 
 def back_sum_kernel(*refs):
@@ -549,119 +527,62 @@
     )(*arrays, *after)
 
 
-def second_sum_kernel(own_ref, received_ref, *refs):
-    near, far = refs[len(refs) - 2 :]
-
-    def rows(start, stop):
-        return (own_ref[:, start:stop, :].astype(F32) + received_ref[:, start:stop, :].astype(F32)).astype(BF16)
-
-    near[:, :64, :] = rows(0, 64)
-    near[:, 64:, :] = rows(96, 128)
-    far[...] = rows(64, 96)
-
-
-def second_sum(own, received, after):
-    return pl.pallas_call(
-        second_sum_kernel,
-        in_specs=[WHOLE] * 2 + [ANY] * len(after),
-        out_specs=[WHOLE] * 2,
-        out_shape=[jax.ShapeDtypeStruct((2, 96, HD), BF16), jax.ShapeDtypeStruct((2, 32, HD), BF16)],
-        compiler_params=params(8),
-        cost_estimate=SMALL,
-    )(own, received, *after)
-
-
-def third_sum_kernel(far_ref, near_ref, *refs):
-    refs[-1][...] = (far_ref[...].astype(F32) + near_ref[:, 64:, :].astype(F32)).astype(BF16)
-
-
-def third_sum(far, near, after):
-    return pl.pallas_call(
-        third_sum_kernel,
-        in_specs=[WHOLE] * 2 + [ANY] * len(after),
-        out_specs=WHOLE,
-        out_shape=jax.ShapeDtypeStruct((2, 32, HD), BF16),
-        compiler_params=params(8),
-        cost_estimate=SMALL,
-    )(far, near, *after)
-
-
 def finish_kernel(*refs):
-    dk_ref, dv_ref, one, two, three = refs[:5]
+    dk_ref, dv_ref, one, two, three, four = refs[:6]
     outs, mark_ref = refs[-3:-1], refs[-1]
     mark_ref[...] = jnp.zeros_like(mark_ref)
     token, row = iota((256, 128), 0), iota((256, 128), 1)
     spread = jnp.zeros((256, 128), F32)
     start = 0
-    for factor, count in ((4, 64), (8, 32), (16, 16)):
+    for factor, count in ((4, 64), (8, 32), (16, 16), (16, 16)):
         local = row - start
         inside = (local >= 0) & (local < count) & (token >= local * factor) & (token < local * factor + factor)
         spread = jnp.where(inside, 1.0 / factor, spread)
         start = start + count
     spread = spread.astype(BF16)
     for place, (own, out) in enumerate(zip((dk_ref, dv_ref), outs)):
-        rows = jnp.concatenate([one[place], two[place], three[place], jnp.zeros((16, HD), BF16)], 0)
+        rows = jnp.concatenate([ref[place] for ref in (one, two, three, four)], 0)
         out[...] = (own[...].astype(F32) + dot_nn(spread, rows)).astype(BF16)
 
 
-def finish(dk, dv, one, two, three, after):
+def finish(dk, dv, returned):
     half = pl.BlockSpec((256, HD), lambda i: (i, 0))
     shape = jax.ShapeDtypeStruct((ROWS, HD), BF16)
-    coarse = [pl.BlockSpec((2, rows, HD), lambda i: (0, i, 0)) for rows in (64, 32, 16)]
     return pl.pallas_call(
         finish_kernel,
         grid=(2,),
-        in_specs=[half] * 2 + coarse + [ANY] * len(after),
+        in_specs=[half] * 2 + [pl.BlockSpec((2, r.shape[1] // 2, HD), lambda i: (0, i, 0)) for r in returned],
         out_specs=[half, half, pl.BlockSpec((8, 128), lambda i: (0, 0))],
         out_shape=[shape, shape, MARK],
         compiler_params=params(16),
-        cost_estimate=SMALL,
-    )(dk, dv, one, two, three, *after)
-
-
-def add_all(refs, at):
-    terms = [ref[at].astype(F32) for ref in refs]
-    return (terms[0] + terms[1]) + (terms[2] + terms[3])
-
-
-def last_sum_kernel(place_ref, *refs):
-    outs = refs[len(refs) - 4 :]
-    _, z_lo, _, _, z_hi = position(place_ref)
-    sums = add_all(refs[:4], slice(None))
-    for lo in range(2):
-        for hi in range(2):
-            rows = sums[lo * 16 + hi * 8 : lo * 16 + hi * 8 + 8]
-            for place, out in enumerate(outs):
-
-                @pl.when((lax.rem(z_lo + place % 2, 2) == lo) & (lax.rem(z_hi + place // 2, 2) == hi))
-                def _():
-                    out[...] = rows
-
-
-def last_sum(place, arrays, after):
-    return pl.pallas_call(
-        last_sum_kernel,
-        in_specs=[pl.BlockSpec(memory_space=pltpu.SMEM)] + [WHOLE] * 4 + [ANY] * len(after),
-        out_specs=[WHOLE] * 4,
-        out_shape=[jax.ShapeDtypeStruct((8, D), F32)] * 4,
-        compiler_params=params(4),
-        cost_estimate=SMALL,
-    )(place, *arrays, *after)
-
-
-def total_kernel(*refs):
-    refs[-1][...] = add_all(refs[:4], slice(None))
-
-
-def total(arrays, after):
+        cost_estimate=LARGE,
+    )(dk, dv, *returned)
+
+
+def total_kernel(ref, _, out_ref):
+    sums = ref[0].astype(F32)
+    for place in range(1, 16):
+        sums = sums + ref[place].astype(F32)
+    out_ref[...] = sums
+
+
+def total(parts, after):
     return pl.pallas_call(
         total_kernel,
-        in_specs=[WHOLE] * 4 + [ANY] * len(after),
+        in_specs=[WHOLE, ANY],
         out_specs=WHOLE,
         out_shape=jax.ShapeDtypeStruct((8, D), F32),
         compiler_params=params(4),
         cost_estimate=SMALL,
-    )(*arrays, *after)
+    )(parts, after)
+
+
+def xz_groups():
+    return [
+        [(((x * 2 + z_lo) * 2 + core) * 4 + y) * 2 + z_hi for x in range(4) for z_lo in range(2) for z_hi in range(2)]
+        for core in range(2)
+        for y in range(4)
+    ]
 
 
 def body(query, key, value, segment_ids, out_weight, cotangent):
@@ -699,19 +620,12 @@
     grad_query, dk, dv, mark = local_backward(
         query, key, value, grad_across, rows, early, partials, range(4, HEADS), earlier, [mark]
     )
-    near, far = second_sum(own_two, back_xz, [mark])
-    near = swap(near, "ctx", 4)
-    parts = y_sum(place, [parts[0], shift(up, "dp", 2), shift(down, "dp", -2)], [far])
-    far = third_sum(far, near, [parts[0]])
-    parts = [parts[0]] + [shift(parts[step], "ctx", 4 * step) for step in (1, 2, 3)]
-    parts = last_sum(place, parts, [far])
-    grad_key, grad_value, mark = finish(dk, dv, back_z, near, swap(far, "ctx", 12), [parts[0]])
-    count = lax.axis_size("dp")
-    both = [(i, (i // count ^ 2) * count + (i % count ^ 1)) for i in range(lax.axis_size("ctx") * count)]
-    grad_weight = total(
-        [parts[0], swap(parts[1], "ctx", 2), swap(parts[2], "dp", 1), lax.ppermute(parts[3], ("ctx", "dp"), both)],
-        [mark],
-    )
+    two, three, four = split_sum([own_two, back_xz], 1, (64, 32, 32), [mark])
+    returned = [back_z, swap(two, "ctx", 4), swap(three, "ctx", 12), swap(four, "ctx", 8)]
+    (summed,) = split_sum([parts[0], shift(up, "dp", 2), shift(down, "dp", -2)], 0, (128,), [two])
+    spread = lax.all_to_all(summed.reshape(16, 8, D), ("ctx", "dp"), 0, 0, axis_index_groups=xz_groups())
+    grad_key, grad_value, mark = finish(dk, dv, returned)
+    grad_weight = total(spread, mark)
     return output[None], grad_query[None], grad_key[None], grad_value[None], grad_weight
 
 

time: 97.8 us -> 94.3 us (0.964)
  starting transfers between devices: 30.8 us -> 27.4 us
  waiting for transfers between devices: 23.5 us -> 21 us
  Pallas kernels: 39.5 us -> 41.7 us
    all_to_all x0 -> x1, waiting for transfers between devices: none -> 7.23 us  [body(): lax.all_to_all(summed.reshape(16, 8, D), ('ctx', 'dp'), 0, 0, axis_index_...]
    all_to_all x0 -> x1, starting transfers between devices: none -> 6.68 us  [body(): lax.all_to_all(summed.reshape(16, 8, D), ('ctx', 'dp'), 0, 0, axis_index_...]
    ppermute x7 -> x4, waiting for transfers between devices: 7.11 us -> 0.81 us  [shift(): lax.ppermute(array, axis, [(i, (i + step) % size) for i in range(size)])]
    ppermute x7 -> x4, starting transfers between devices: 11.6 us -> 5.4 us  [shift(): lax.ppermute(array, axis, [(i, (i + step) % size) for i in range(size)])]
    ppermute x17 -> x16, starting transfers between devices: 19.2 us -> 15.3 us  [swap(): lax.ppermute(array, axis, [(i, i ^ bits) for i in range(lax.axis_size(axi...]
    ppermute x1 -> x0, waiting for transfers between devices: 2.53 us -> none  [body(): lax.ppermute(parts[3], ('ctx', 'dp'), both)]
    pallas_call x1 -> x3, Pallas kernels: 0.48 us -> 2.23 us  [split_sum(): pl.pallas_call(partial(split_sum_kernel, len(arrays), axis, bounds), in_s...]
    ppermute x17 -> x16, waiting for transfers between devices: 13.9 us -> 12.9 us  [swap(): lax.ppermute(array, axis, [(i, i ^ bits) for i in range(lax.axis_size(axi...]
  transfers between devices with their start and end apart: 25 -> 21, of which waited for: 12 -> 10; matrix products, arithmetic and copies ran while one was open for 0% -> 0% of each run, Pallas kernels for 33% -> 36%
where the time goes in v2:
time: 94.3 us; the launch traced here: 94 us
  Pallas kernels  41.7 us (44%)
  starting transfers between devices  27.4 us (29%)
  waiting for transfers between devices  21 us (22%)
  local copies, waits for them, and re-layouts  3.03 us (3%)
    ppermute x16, starting transfers between devices, swap(): lax.ppermute(array, axis, [(i, i ^ bits) for i in range(lax.axis_size(axi...  15.3 us
    ppermute x16, waiting for transfers between devices, swap(): lax.ppermute(array, axis, [(i, i ^ bits) for i in range(lax.axis_size(axi...  12.9 us
    pallas_call x1, Pallas kernels, early_forward(): pl.pallas_call(early_forward_kernel, in_specs=[WHOLE] * 9 + [ANY] * len(a...  9.35 us
    all_to_all x1, waiting for transfers between devices, body(): lax.all_to_all(summed.reshape(16, 8, D), ('ctx', 'dp'), 0, 0, axis_index_...  7.23 us
    pallas_call x2, Pallas kernels, coarse_backward(): pl.pallas_call(partial(coarse_backward_kernel, heads), in_specs=[WHOLE] *...  6.7 us
    all_to_all x1, starting transfers between devices, body(): lax.all_to_all(summed.reshape(16, 8, D), ('ctx', 'dp'), 0, 0, axis_index_...  6.68 us
    pallas_call x2, Pallas kernels, local_backward(): pl.pallas_call(partial(local_backward_kernel, heads, [part[:2] for part i...  6.23 us
    ppermute x4, starting transfers between devices, shift(): lax.ppermute(array, axis, [(i, (i + step) % size) for i in range(size)])  5.4 us
  transfers between devices with their start and end apart: 21, of which 10 were waited for; matrix products, arithmetic and copies ran while one was open for 0% of the time, Pallas kernels for 36%

profile of v2, /device:TPU:0, one launch (start us, length us, event | category | flops | bytes accessed | tf_op | source)
XLA Modules:
  0.0 94.0 jit_solution(17372666866750623815)
XLA Ops:
  0.6 0.0 copy-start.3
  0.7 0.8 copy-done.6
  1.5 2.1 %shard_map.102 = (bf16[128,2176]{1,0:T(8,128)(2,1)S(1)}, bf16[64,2176]{1,0:T(8,128)(2,1)S(1)}, bf16[32,2176]{1,0:T(8,128)(2,1)S(1)}, bf16[512,128]{1,0:T(8,128)(...) custom-call(s32[1]{0:T(128)} %bitcast.2.place_ref, s32[1,512]{1,0:T(1,128)S(1)} %copy-done.6, ...), custom_call_target="tpu_custom_call" | custom-call | flops 1024 | bytes 1024 | tf_op jit(solution)/shard_map/pallas_call | solution.py:130
  3.6 2.1 %collective-permute-start = (bf16[128,2176]{1,0:T(8,128)(2,1)S(1)}, bf16[128,2176]{1,0:T(8,128)(2,1)S(1)}, u32[]{:S(2)}, u32[]{:S(2)}) collective-permute-start(bf16[128,2176]{1,0:T(8,128)(2,1)S(1)} %get-tuple-element.63), channel_id=1, source_target_pairs={{0,16},{8,24},{16,0},{24,8},{32,48},{40,56},{48,32},{56,40},{64,80... | collective-permute-start | bytes 1671176 | tf_op jit(solution)/shard_map/ppermute | solution.py:35
  5.6 1.5 %collective-permute-start.1 = (bf16[64,2176]{1,0:T(8,128)(2,1)S(1)}, bf16[64,2176]{1,0:T(8,128)(2,1)S(1)}, u32[]{:S(2)}, u32[]{:S(2)}) collective-permute-start(bf16[64,2176]{1,0:T(8,128)(2,1)S(1)} %get-tuple-element.67), channel_id=1, source_target_pairs={{0,32},{8,40},{16,48},{24,56},{32,0},{40,8},{48,16},{56,24},{64,96... | collective-permute-start | bytes 835592 | tf_op jit(solution)/shard_map/ppermute | solution.py:35
  7.1 2.7 %collective-permute-start.3 = (bf16[32,2176]{1,0:T(8,128)(2,1)S(1)}, bf16[32,2176]{1,0:T(8,128)(2,1)S(1)}, u32[]{:S(2)}, u32[]{:S(2)}) collective-permute-start(bf16[32,2176]{1,0:T(8,128)(2,1)S(1)} %get-tuple-element.68), channel_id=1, source_target_pairs={{0,64},{8,72},{16,80},{24,88},{32,96},{40,104},{48,112},{56,120},{... | collective-permute-start | bytes 417800 | tf_op jit(solution)/shard_map/ppermute | solution.py:35
  9.9 0.5 collective-permute-start.2
  10.3 2.2 %copy-done.4 = bf16[1024,2048]{1,0:T(8,128)(2,1)S(1)} copy-done((bf16[1024,2048]{1,0:T(8,128)(2,1)S(1)}, bf16[1024,2048]{1,0:T(8,128)(2,1)}, u32[]{:S(2)}) %copy-start.4) | copy-done | bytes 4194328
  12.5 2.4 %shard_map.101 = (bf16[512,1024]{1,0:T(8,128)(2,1)S(1)}, bf16[1024,512]{1,0:T(8,128)(2,1)S(1)}) custom-call(bf16[512,2048]{1,0:T(8,128)(2,1)S(1)} %bitcast.24, bf16[1024,2048]{1,0:T(8,128)(2,1)S(1)} %copy-done.4), custom_call_target="tpu_custom_call" | custom-call | flops 1024 | bytes 1024 | tf_op jit(solution)/shard_map/pallas_call | solution.py:385
  15.0 0.0 copy-start
  15.0 0.0 copy-start.1
  15.0 4.0 %collective-permute-done.3.refs_2_ = bf16[32,2176]{1,0:T(8,128)(2,1)S(1)} collective-permute-done((bf16[32,2176]{1,0:T(8,128)(2,1)S(1)}, bf16[32,2176]{1,0:T(8,128)(2,1)S(1)}, u32[]{:S(2)}, u32[]{:S(2)}) %collective-permute-start.3) | collective-permute-done | bytes 139296 | tf_op jit(solution)/shard_map/ppermute | solution.py:35
  19.0 0.0 collective-permute-done.2.refs_1_
  19.0 0.0 collective-permute-done.1.refs_0_
  19.1 0.1 collective-permute-start.5
  19.2 0.0 collective-permute-done.refs_5_.refs_6_
  19.2 0.5 collective-permute-start.4
  19.7 0.3 collective-permute-start.6
  20.0 1.1 %collective-permute-done.5.refs_8_.refs_9_ = bf16[128,2176]{1,0:T(8,128)(2,1)S(1)} collective-permute-done((bf16[128,2176]{1,0:T(8,128)(2,1)S(1)}, bf16[128,2176]{1,0:T(8,128)(2,1)S(1)}, u32[]{:S(2)}, u32[]{:S(2)}) %collective-permute-start.5) | collective-permute-done | bytes 557088 | tf_op jit(solution)/shard_map/ppermute | solution.py:35
  21.1 0.8 collective-permute-done.4.refs_7_.refs_8_
  21.9 9.3 %shard_map.105 = (bf16[8,1024,512]{2,1,0:T(8,128)(2,1)S(1)}, f32[1024,512]{1,0:T(8,128)S(1)}, f32[8,8,512]{2,1,0:T(8,128)S(1)}) custom-call(bf16[512,1024]{1,0:T(8,128)(2,1)S(1)} %bitcast.10, bf16[512,1024]{1,0:T(8,128)(2,1)S(1)} %bitcast.17, bf16[512,1024]{1,0:T(8,128)(2,1)S(1)} %bitcast.21, bf16[512,128]{1,0:T(8,128)(2,1)S(1)} %get-tuple-element.61.refs_3_.refs_2_, ...), custom_call_target="tpu_custom_call" | custom-call | flops 1024 | bytes 1024 | tf_op jit(solution)/shard_map/pallas_call | solution.py:223
  31.3 3.0 %collective-permute-done.6.refs_5_.refs_10_ = bf16[128,2176]{1,0:T(8,128)(2,1)S(1)} collective-permute-done((bf16[128,2176]{1,0:T(8,128)(2,1)S(1)}, bf16[128,2176]{1,0:T(8,128)(2,1)S(1)}, u32[]{:S(2)}, u32[]{:S(2)}) %collective-permute-start.6) | collective-permute-done | bytes 557088 | tf_op jit(solution)/shard_map/ppermute | solution.py:35
  34.3 0.0 collective-permute-start.7
  34.3 2.0 %collective-permute-done.7.refs_6_.refs_11_ = bf16[128,2176]{1,0:T(8,128)(2,1)S(1)} collective-permute-done((bf16[128,2176]{1,0:T(8,128)(2,1)S(1)}, bf16[128,2176]{1,0:T(8,128)(2,1)S(1)}, u32[]{:S(2)}, u32[]{:S(2)}) %collective-permute-start.7) | collective-permute-done | bytes 557088 | tf_op jit(solution)/shard_map/ppermute | solution.py:35
  36.3 2.6 %shard_map.106 = (bf16[8,256,512]{2,1,0:T(8,128)(2,1)S(1)}, bf16[1024,512]{1,0:T(8,128)(2,1)S(1)}, f32[8,8,512]{2,1,0:T(8,128)S(1)}) custom-call(bf16[512,1024]{1,0:T(8,128)(2,1)S(1)} %bitcast.11, bf16[1024,512]{1,0:T(8,128)(2,1)S(1)} %get-tuple-element.60.refs_1_.refs_2_.refs_3_, bf16[512,128]{1,0:T(8,128)(2,1)S(1)} %get-tuple-element.61.refs_3_.refs_2_, ...), custom_call_target="tpu_custom_call" | custom-call | flops 1024 | bytes 1024 | tf_op jit(solution)/shard_map/pallas_call | solution.py:264
  38.9 2.4 %shard_map.107 = (bf16[512,2048]{1,0:T(8,128)(2,1)S(1)}, bf16[512,2048]{1,0:T(8,128)(2,1)S(1)}, f32[8,128]{1,0:T(8,128)S(1)}) custom-call(s32[1]{0:T(128)} %bitcast.2.place_ref, bf16[1024,512]{1,0:T(8,128)(2,1)S(1)} %get-tuple-element.75.ot_ref.a_ref, bf16[512,2048]{1,0:T(8,128)(2,1)S(1)} %bitcast.25), custom_call_target="tpu_custom_call" | custom-call | flops 1024 | bytes 1024 | tf_op jit(solution)/shard_map/pallas_call | solution.py:450
  41.3 0.4 collective-permute-start.8
  41.7 5.3 %shard_map.108 = (bf16[2,384,896]{2,1,0:T(8,128)(2,1)S(1)}, bf16[2,384,896]{2,1,0:T(8,128)(2,1)S(1)}, f32[896,512]{1,0:T(8,128)S(1)}, f32[8,128]{1,0:T(8,128)S(1)}) custom-call(bf16[512,1024]{1,0:T(8,128)(2,1)S(1)} %bitcast.12, bf16[512,1024]{1,0:T(8,128)(2,1)S(1)} %get-tuple-element.69.refs_3_.refs_1_, ...), custom_call_target="tpu_custom_call" | custom-call | flops 1024 | bytes 1024 | tf_op jit(solution)/shard_map/pallas_call | solution.py:320
  46.9 0.5 collective-permute-start.11
  47.4 0.0 collective-permute-done.8.refs_1_
  47.4 0.5 shard_map.109
  47.9 1.7 %collective-permute-start.9 = (bf16[64,2048]{1,0:T(8,128)(2,1)S(1)}, bf16[64,2048]{1,0:T(8,128)(2,1)S(1)}, u32[]{:S(2)}, u32[]{:S(2)}) collective-permute-start(bf16[64,2048]{1,0:T(8,128)(2,1)S(1)} %get-tuple-element.85), channel_id=1, source_target_pairs={{0,2},{1,3},{2,4},{3,5},{4,6},{5,7},{6,0},{7,1},{8,10},{9,11},{10,... | collective-permute-start | bytes 786440 | tf_op jit(solution)/shard_map/ppermute | solution.py:40
  49.5 1.7 %collective-permute-start.10 = (bf16[64,2048]{1,0:T(8,128)(2,1)S(1)}, bf16[64,2048]{1,0:T(8,128)(2,1)S(1)}, u32[]{:S(2)}, u32[]{:S(2)}) collective-permute-start(bf16[64,2048]{1,0:T(8,128)(2,1)S(1)} %get-tuple-element.86), channel_id=1, source_target_pairs={{0,6},{1,7},{2,0},{3,1},{4,2},{5,3},{6,4},{7,5},{8,14},{9,15},{10,... | collective-permute-start | bytes 786440 | tf_op jit(solution)/shard_map/ppermute | solution.py:40
  51.2 1.4 %shard_map.110 = (bf16[2,384,128]{2,1,0:T(8,128)(2,1)S(1)}, bf16[2,384,128]{2,1,0:T(8,128)(2,1)S(1)}, f32[128,512]{1,0:T(8,128)S(1)}, f32[8,128]{1,0:T(8,128)}) custom-call(bf16[512,1024]{1,0:T(8,128)(2,1)S(1)} %bitcast.13, bf16[512,1024]{1,0:T(8,128)(2,1)S(1)} %get-tuple-element.69.refs_3_.refs_1_, ...), custom_call_target="tpu_custom_call" | custom-call | flops 1024 | bytes 1024 | tf_op jit(solution)/shard_map/pallas_call | solution.py:320
  52.6 0.0 collective-permute-start.12
  52.6 0.0 collective-permute-done.11.refs_1_
  52.6 1.4 %collective-permute-done.12.refs_3_ = bf16[2,384,128]{2,1,0:T(8,128)(2,1)S(1)} collective-permute-done((bf16[2,384,128]{2,1,0:T(8,128)(2,1)S(1)}, bf16[2,384,128]{2,1,0:T(8,128)(2,1)S(1)}, u32[]{:S(2)}, u32[]{:S(2)}) %collective-permute-start.12) | collective-permute-done | bytes 196640 | tf_op jit(solution)/shard_map/ppermute | solution.py:35
  54.1 0.4 shard_map.111
  54.4 0.8 collective-permute-start.14
  55.3 1.3 %collective-permute-start.13 = (bf16[2,128,1024]{2,1,0:T(8,128)(2,1)S(1)}, bf16[2,128,1024]{2,1,0:T(8,128)(2,1)}, u32[]{:S(2)}, u32[]{:S(2)}) collective-permute-start(bf16[2,128,1024]{2,1,0:T(8,128)(2,1)S(1)} %get-tuple-element.93.refs_7_), channel_id=1, source_target_pairs={{0,16},{8,24},{16,0},{24,8},{32,48},{40,56},{48,32},{56,40},{64,80... | collective-permute-start | bytes 1572872 | tf_op jit(solution)/shard_map/ppermute | solution.py:35
  56.6 2.6 %shard_map.112 = (bf16[512,512]{1,0:T(8,128)(2,1)S(1)}, bf16[512,512]{1,0:T(8,128)(2,1)S(1)}, bf16[512,512]{1,0:T(8,128)(2,1)S(1)}, f32[8,128]{1,0:T(8,128)S(1)}) custom-call(bf16[512,1024]{1,0:T(8,128)(2,1)S(1)} %bitcast.14, bf16[512,1024]{1,0:T(8,128)(2,1)S(1)} %bitcast.18, bf16[512,1024]{1,0:T(8,128)(2,1)S(1)} %bitcast.22, ...), custom_call_target="tpu_custom_call" | custom-call | flops 1024 | bytes 1024 | tf_op jit(solution)/shard_map/pallas_call | solution.py:367
  59.1 0.0 collective-permute-done.9.lower_ref
  59.2 0.0 collective-permute-done.10.upper_ref
  59.2 0.1 shard_map.113
  59.3 1.9 %collective-permute-start.19 = (bf16[128,2048]{1,0:T(8,128)(2,1)S(1)}, bf16[128,2048]{1,0:T(8,128)(2,1)S(1)}, u32[]{:S(2)}, u32[]{:S(2)}) collective-permute-start(bf16[128,2048]{1,0:T(8,128)(2,1)S(1)} %get-tuple-element.113), channel_id=1, source_target_pairs={{0,6},{1,7},{2,0},{3,1},{4,2},{5,3},{6,4},{7,5},{8,14},{9,15},{10,... | collective-permute-start | bytes 1572872 | tf_op jit(solution)/shard_map/ppermute | solution.py:40
  61.2 0.2 collective-permute-start.18
  61.4 3.7 %shard_map.114 = (bf16[512,2048]{1,0:T(8,128)(2,1)}, f32[8,128]{1,0:T(8,128)S(1)}) custom-call(bf16[1024,512]{1,0:T(8,128)(2,1)S(1)} %get-tuple-element.75.ot_ref.a_ref, bf16[1024,2048]{1,0:T(8,128)(2,1)S(1)} %copy-done.5, bf16[128,2048]{1,0:T(8,128)(2,1)S(1)} %get-tuple-element.95._), custom_call_target="tpu_custom_call" | custom-call | flops 20000000000 | bytes 1024 | tf_op jit(solution)/shard_map/pallas_call | solution.py:402
  65.1 3.7 %shard_map.115 = (bf16[512,1024]{1,0:T(8,128)(2,1)}, bf16[512,1024]{1,0:T(8,128)(2,1)S(1)}, bf16[512,1024]{1,0:T(8,128)(2,1)S(1)}, f32[8,128]{1,0:T(8,128)S(1)}) custom-call(bf16[512,1024]{1,0:T(8,128)(2,1)S(1)} %bitcast.15, bf16[512,1024]{1,0:T(8,128)(2,1)S(1)} %bitcast.19, bf16[512,1024]{1,0:T(8,128)(2,1)S(1)} %bitcast.23, ...), custom_call_target="tpu_custom_call" | custom-call | flops 1024 | bytes 1024 | tf_op jit(solution)/shard_map/pallas_call | solution.py:367
  68.7 0.5 collective-permute-done.14.refs_1_
  69.3 0.7 shard_map.116
  70.0 0.5 collective-permute-start.15
  70.5 2.1 %collective-permute-start.16 = (bf16[2,32,1024]{2,1,0:T(8,128)(2,1)}, bf16[2,32,1024]{2,1,0:T(8,128)(2,1)S(1)}, u32[]{:S(2)}, u32[]{:S(2)}) collective-permute-start(bf16[2,32,1024]{2,1,0:T(8,128)(2,1)} %get-tuple-element.109), channel_id=1, source_target_pairs={{0,96},{8,104},{16,112},{24,120},{32,64},{40,72},{48,80},{56,88},{... | collective-permute-start | bytes 393224 | tf_op jit(solution)/shard_map/ppermute | solution.py:35
  72.6 0.2 collective-permute-done.19.refs_2_
  72.8 2.1 %collective-permute-start.17 = (bf16[2,32,1024]{2,1,0:T(8,128)(2,1)}, bf16[2,32,1024]{2,1,0:T(8,128)(2,1)}, u32[]{:S(2)}, u32[]{:S(2)}) collective-permute-start(bf16[2,32,1024]{2,1,0:T(8,128)(2,1)} %get-tuple-element.110), channel_id=1, source_target_pairs={{0,64},{8,72},{16,80},{24,88},{32,96},{40,104},{48,112},{56,120},{... | collective-permute-start | bytes 393224 | tf_op jit(solution)/shard_map/ppermute | solution.py:35
  74.9 0.6 collective-permute-done.18.refs_1_
  75.5 1.0 %shard_map.118 = bf16[128,2048]{1,0:T(8,128)(2,1)} custom-call(bf16[128,2048]{1,0:T(8,128)(2,1)S(1)} %get-tuple-element.90.refs_12_.refs_0_, bf16[128,2048]{1,0:T(8,128)(2,1)S(1)} %collective-permute-done.18.refs_1_, bf16[128,2048]{1,0:T(8,128)(2,1)S(1)} %collective-permute-done.19.refs_2_, bf16[2,64,1024]{2,1,0:T(8,128)(2,1)S(1)} %get-tuple-element.108.refs_3_), custom_call_target="tpu_custom_call" | custom-call | flops 1024 | bytes 1024 | tf_op jit(solution)/shard_map/pallas_call | solution.py:478
  76.5 6.7 %all-to-all-start = ((bf16[16,8,2048]{2,1,0:T(8,128)(2,1)}), bf16[16,8,2048]{2,1,0:T(8,128)(2,1)S(1)}, u32[]{:S(2)}, u32[]{:S(2)}) async-start(bf16[16,8,2048]{2,1,0:T(8,128)(2,1)} %bitcast.9), calls=%async_computation | async-start | bytes 1048576 | tf_op jit(solution)/shard_map/all_to_all | solution.py:626
  83.2 0.0 collective-permute-done.13.refs_2_
  83.2 0.0 collective-permute-done.16.refs_4_
  83.3 0.0 collective-permute-done.17.refs_5_
  83.3 0.0 collective-permute-done.15.refs_3_
  83.3 2.8 %shard_map.117 = (bf16[512,1024]{1,0:T(8,128)(2,1)}, bf16[512,1024]{1,0:T(8,128)(2,1)}, f32[8,128]{1,0:T(8,128)S(1)}) custom-call(bf16[512,1024]{1,0:T(8,128)(2,1)S(1)} %get-tuple-element.103.refs_0_, bf16[512,1024]{1,0:T(8,128)(2,1)S(1)} %get-tuple-element.104.refs_1_, bf16[2,128,1024]{2,1,0:T(8,128)(2,1)} %collective-permute-done.13.refs_2_, ...), custom_call_target="tpu_custom_call" | custom-call | flops 20000000000 | bytes 1024 | tf_op jit(solution)/shard_map/pallas_call | solution.py:551
  86.0 7.2 %all-to-all-done.ref = bf16[16,8,2048]{2,1,0:T(8,128)(2,1)S(1)} async-done(((bf16[16,8,2048]{2,1,0:T(8,128)(2,1)}), bf16[16,8,2048]{2,1,0:T(8,128)(2,1)S(1)}, u32[]{:S(2)}, u32[]{:S(2)}) %all-to-all-start) | async-done | bytes 524320 | tf_op jit(solution)/shard_map/all_to_all | solution.py:626
  93.3 0.7 shard_map.119
  (11 shorter events, 0.1 us)
Async XLA Ops:
  0.6 9.7 %copy-start.3 = (bf16[1,512,2048]{2,1,0:T(8,128)(2,1)S(1)}, bf16[1,512,2048]{2,1,0:T(8,128)(2,1)}, u32[]{:S(2)}) copy-start(bf16[1,512,2048]{2,1,0:T(8,128)(2,1)} %param.11) | copy-start | bytes 6291460
  0.6 0.8 copy-start.6
  3.6 15.6 %collective-permute-start = (bf16[128,2176]{1,0:T(8,128)(2,1)S(1)}, bf16[128,2176]{1,0:T(8,128)(2,1)S(1)}, u32[]{:S(2)}, u32[]{:S(2)}) collective-permute-start(bf16[128,2176]{1,0:T(8,128)(2,1)S(1)} %get-tuple-element.63), channel_id=1, source_target_pairs={{0,16},{8,24},{16,0},{24,8},{32,48},{40,56},{48,32},{56,40},{64,80... | collective-permute-start | bytes 1671176 | tf_op jit(solution)/shard_map/ppermute | solution.py:35
  5.6 13.4 %collective-permute-start.1 = (bf16[64,2176]{1,0:T(8,128)(2,1)S(1)}, bf16[64,2176]{1,0:T(8,128)(2,1)S(1)}, u32[]{:S(2)}, u32[]{:S(2)}) collective-permute-start(bf16[64,2176]{1,0:T(8,128)(2,1)S(1)} %get-tuple-element.67), channel_id=1, source_target_pairs={{0,32},{8,40},{16,48},{24,56},{32,0},{40,8},{48,16},{56,24},{64,96... | collective-permute-start | bytes 835592 | tf_op jit(solution)/shard_map/ppermute | solution.py:35
  7.1 11.9 %collective-permute-start.3 = (bf16[32,2176]{1,0:T(8,128)(2,1)S(1)}, bf16[32,2176]{1,0:T(8,128)(2,1)S(1)}, u32[]{:S(2)}, u32[]{:S(2)}) collective-permute-start(bf16[32,2176]{1,0:T(8,128)(2,1)S(1)} %get-tuple-element.68), channel_id=1, source_target_pairs={{0,64},{8,72},{16,80},{24,88},{32,96},{40,104},{48,112},{56,120},{... | collective-permute-start | bytes 417800 | tf_op jit(solution)/shard_map/ppermute | solution.py:35
  9.9 9.2 %collective-permute-start.2 = (bf16[32,2176]{1,0:T(8,128)(2,1)S(1)}, bf16[32,2176]{1,0:T(8,128)(2,1)S(1)}, u32[]{:S(2)}, u32[]{:S(2)}) collective-permute-start(bf16[32,2176]{1,0:T(8,128)(2,1)S(1)} %get-tuple-element.68), channel_id=1, source_target_pairs={{0,96},{8,104},{16,112},{24,120},{32,64},{40,72},{48,80},{56,88},{... | collective-permute-start | bytes 417800 | tf_op jit(solution)/shard_map/ppermute | solution.py:35
  10.3 2.2 %copy-start.4 = (bf16[1024,2048]{1,0:T(8,128)(2,1)S(1)}, bf16[1024,2048]{1,0:T(8,128)(2,1)}, u32[]{:S(2)}) copy-start(bf16[1024,2048]{1,0:T(8,128)(2,1)} %w_ref.3) | copy-start | bytes 12582916
  12.5 9.4 %copy-start.2 = (bf16[1,512,1024]{2,1,0:T(8,128)(2,1)S(1)}, bf16[1,512,1024]{2,1,0:T(8,128)(2,1)}, u32[]{:S(2)}) copy-start(bf16[1,512,1024]{2,1,0:T(8,128)(2,1)} %param.8) | copy-start | bytes 3145732
  15.0 7.0 %copy-start = (bf16[1,512,1024]{2,1,0:T(8,128)(2,1)S(1)}, bf16[1,512,1024]{2,1,0:T(8,128)(2,1)}, u32[]{:S(2)}) copy-start(bf16[1,512,1024]{2,1,0:T(8,128)(2,1)} %param.6) | copy-start | bytes 3145732
  15.0 6.9 %copy-start.1 = (bf16[1,512,1024]{2,1,0:T(8,128)(2,1)S(1)}, bf16[1,512,1024]{2,1,0:T(8,128)(2,1)}, u32[]{:S(2)}) copy-start(bf16[1,512,1024]{2,1,0:T(8,128)(2,1)} %param.7) | copy-start | bytes 3145732
  19.1 2.0 %collective-permute-start.5 = (bf16[128,2176]{1,0:T(8,128)(2,1)S(1)}, bf16[128,2176]{1,0:T(8,128)(2,1)S(1)}, u32[]{:S(2)}, u32[]{:S(2)}) collective-permute-start(bf16[128,2176]{1,0:T(8,128)(2,1)S(1)} %shard_map.104.refs_6_.refs_7_), channel_id=1, source_target_pairs={{0,8},{8,0},{16,24},{24,16},{32,40},{40,32},{48,56},{56,48},{64,72... | collective-permute-start | bytes 1671176 | tf_op jit(solution)/shard_map/ppermute | solution.py:35
  19.2 2.7 %collective-permute-start.4 = (bf16[128,2176]{1,0:T(8,128)(2,1)S(1)}, bf16[128,2176]{1,0:T(8,128)(2,1)S(1)}, u32[]{:S(2)}, u32[]{:S(2)}) collective-permute-start(bf16[128,2176]{1,0:T(8,128)(2,1)S(1)} %collective-permute-done.refs_5_.refs_6_), channel_id=1, source_target_pairs={{0,8},{8,0},{16,24},{24,16},{32,40},{40,32},{48,56},{56,48},{64,72... | collective-permute-start | bytes 1671176 | tf_op jit(solution)/shard_map/ppermute | solution.py:35
  19.7 14.6 %collective-permute-start.6 = (bf16[128,2176]{1,0:T(8,128)(2,1)S(1)}, bf16[128,2176]{1,0:T(8,128)(2,1)S(1)}, u32[]{:S(2)}, u32[]{:S(2)}) collective-permute-start(bf16[128,2176]{1,0:T(8,128)(2,1)S(1)} %shard_map.104.refs_6_.refs_7_), channel_id=1, source_target_pairs={{0,16},{8,24},{16,0},{24,8},{32,48},{40,56},{48,32},{56,40},{64,80... | collective-permute-start | bytes 1671176 | tf_op jit(solution)/shard_map/ppermute | solution.py:35
  34.3 2.0 %collective-permute-start.7 = (bf16[128,2176]{1,0:T(8,128)(2,1)S(1)}, bf16[128,2176]{1,0:T(8,128)(2,1)S(1)}, u32[]{:S(2)}, u32[]{:S(2)}) collective-permute-start(bf16[128,2176]{1,0:T(8,128)(2,1)S(1)} %collective-permute-done.6.refs_5_.refs_10_), channel_id=1, source_target_pairs={{0,8},{8,0},{16,24},{24,16},{32,40},{40,32},{48,56},{56,48},{64,72... | collective-permute-start | bytes 1671176 | tf_op jit(solution)/shard_map/ppermute | solution.py:35
  41.3 6.1 %collective-permute-start.8 = (bf16[512,2048]{1,0:T(8,128)(2,1)S(1)}, bf16[512,2048]{1,0:T(8,128)(2,1)S(1)}, u32[]{:S(2)}, u32[]{:S(2)}) collective-permute-start(bf16[512,2048]{1,0:T(8,128)(2,1)S(1)} %get-tuple-element.77), channel_id=1, source_target_pairs={{0,8},{8,0},{16,24},{24,16},{32,40},{40,32},{48,56},{56,48},{64,72... | collective-permute-start | bytes 6291464 | tf_op jit(solution)/shard_map/ppermute | solution.py:35
  46.9 5.7 %collective-permute-start.11 = (bf16[2,384,896]{2,1,0:T(8,128)(2,1)S(1)}, bf16[2,384,896]{2,1,0:T(8,128)(2,1)S(1)}, u32[]{:S(2)}, u32[]{:S(2)}) collective-permute-start(bf16[2,384,896]{2,1,0:T(8,128)(2,1)S(1)} %get-tuple-element.89), channel_id=1, source_target_pairs={{0,8},{8,0},{16,24},{24,16},{32,40},{40,32},{48,56},{56,48},{64,72... | collective-permute-start | bytes 4128776 | tf_op jit(solution)/shard_map/ppermute | solution.py:35
  47.9 11.3 %collective-permute-start.9 = (bf16[64,2048]{1,0:T(8,128)(2,1)S(1)}, bf16[64,2048]{1,0:T(8,128)(2,1)S(1)}, u32[]{:S(2)}, u32[]{:S(2)}) collective-permute-start(bf16[64,2048]{1,0:T(8,128)(2,1)S(1)} %get-tuple-element.85), channel_id=1, source_target_pairs={{0,2},{1,3},{2,4},{3,5},{4,6},{5,7},{6,0},{7,1},{8,10},{9,11},{10,... | collective-permute-start | bytes 786440 | tf_op jit(solution)/shard_map/ppermute | solution.py:40
  49.5 9.6 %collective-permute-start.10 = (bf16[64,2048]{1,0:T(8,128)(2,1)S(1)}, bf16[64,2048]{1,0:T(8,128)(2,1)S(1)}, u32[]{:S(2)}, u32[]{:S(2)}) collective-permute-start(bf16[64,2048]{1,0:T(8,128)(2,1)S(1)} %get-tuple-element.86), channel_id=1, source_target_pairs={{0,6},{1,7},{2,0},{3,1},{4,2},{5,3},{6,4},{7,5},{8,14},{9,15},{10,... | collective-permute-start | bytes 786440 | tf_op jit(solution)/shard_map/ppermute | solution.py:40
  52.6 1.4 %collective-permute-start.12 = (bf16[2,384,128]{2,1,0:T(8,128)(2,1)S(1)}, bf16[2,384,128]{2,1,0:T(8,128)(2,1)S(1)}, u32[]{:S(2)}, u32[]{:S(2)}) collective-permute-start(bf16[2,384,128]{2,1,0:T(8,128)(2,1)S(1)} %get-tuple-element.92), channel_id=1, source_target_pairs={{0,8},{8,0},{16,24},{24,16},{32,40},{40,32},{48,56},{56,48},{64,72... | collective-permute-start | bytes 589832 | tf_op jit(solution)/shard_map/ppermute | solution.py:35
  54.4 14.8 %collective-permute-start.14 = (bf16[2,128,1024]{2,1,0:T(8,128)(2,1)S(1)}, bf16[2,128,1024]{2,1,0:T(8,128)(2,1)S(1)}, u32[]{:S(2)}, u32[]{:S(2)}) collective-permute-start(bf16[2,128,1024]{2,1,0:T(8,128)(2,1)S(1)} %get-tuple-element.106), channel_id=1, source_target_pairs={{0,16},{8,24},{16,0},{24,8},{32,48},{40,56},{48,32},{56,40},{64,80... | collective-permute-start | bytes 1572872 | tf_op jit(solution)/shard_map/ppermute | solution.py:35
  55.3 28.0 %collective-permute-start.13 = (bf16[2,128,1024]{2,1,0:T(8,128)(2,1)S(1)}, bf16[2,128,1024]{2,1,0:T(8,128)(2,1)}, u32[]{:S(2)}, u32[]{:S(2)}) collective-permute-start(bf16[2,128,1024]{2,1,0:T(8,128)(2,1)S(1)} %get-tuple-element.93.refs_7_), channel_id=1, source_target_pairs={{0,16},{8,24},{16,0},{24,8},{32,48},{40,56},{48,32},{56,40},{64,80... | collective-permute-start | bytes 1572872 | tf_op jit(solution)/shard_map/ppermute | solution.py:35
  56.6 4.9 %copy-start.5 = (bf16[1024,2048]{1,0:T(8,128)(2,1)S(1)}, bf16[1024,2048]{1,0:T(8,128)(2,1)}, u32[]{:S(2)}) copy-start(bf16[1024,2048]{1,0:T(8,128)(2,1)} %w_ref.3) | copy-start | bytes 12582916
  59.3 13.5 %collective-permute-start.19 = (bf16[128,2048]{1,0:T(8,128)(2,1)S(1)}, bf16[128,2048]{1,0:T(8,128)(2,1)S(1)}, u32[]{:S(2)}, u32[]{:S(2)}) collective-permute-start(bf16[128,2048]{1,0:T(8,128)(2,1)S(1)} %get-tuple-element.113), channel_id=1, source_target_pairs={{0,6},{1,7},{2,0},{3,1},{4,2},{5,3},{6,4},{7,5},{8,14},{9,15},{10,... | collective-permute-start | bytes 1572872 | tf_op jit(solution)/shard_map/ppermute | solution.py:40
  61.2 14.3 %collective-permute-start.18 = (bf16[128,2048]{1,0:T(8,128)(2,1)S(1)}, bf16[128,2048]{1,0:T(8,128)(2,1)S(1)}, u32[]{:S(2)}, u32[]{:S(2)}) collective-permute-start(bf16[128,2048]{1,0:T(8,128)(2,1)S(1)} %get-tuple-element.95._), channel_id=1, source_target_pairs={{0,2},{1,3},{2,4},{3,5},{4,6},{5,7},{6,0},{7,1},{8,10},{9,11},{10,... | collective-permute-start | bytes 1572872 | tf_op jit(solution)/shard_map/ppermute | solution.py:40
  70.0 13.2 %collective-permute-start.15 = (bf16[2,64,1024]{2,1,0:T(8,128)(2,1)S(1)}, bf16[2,64,1024]{2,1,0:T(8,128)(2,1)}, u32[]{:S(2)}, u32[]{:S(2)}) collective-permute-start(bf16[2,64,1024]{2,1,0:T(8,128)(2,1)S(1)} %get-tuple-element.108.refs_3_), channel_id=1, source_target_pairs={{0,32},{8,40},{16,48},{24,56},{32,0},{40,8},{48,16},{56,24},{64,96... | collective-permute-start | bytes 786440 | tf_op jit(solution)/shard_map/ppermute | solution.py:35
  70.5 12.7 %collective-permute-start.16 = (bf16[2,32,1024]{2,1,0:T(8,128)(2,1)}, bf16[2,32,1024]{2,1,0:T(8,128)(2,1)S(1)}, u32[]{:S(2)}, u32[]{:S(2)}) collective-permute-start(bf16[2,32,1024]{2,1,0:T(8,128)(2,1)} %get-tuple-element.109), channel_id=1, source_target_pairs={{0,96},{8,104},{16,112},{24,120},{32,64},{40,72},{48,80},{56,88},{... | collective-permute-start | bytes 393224 | tf_op jit(solution)/shard_map/ppermute | solution.py:35
  72.8 10.5 %collective-permute-start.17 = (bf16[2,32,1024]{2,1,0:T(8,128)(2,1)}, bf16[2,32,1024]{2,1,0:T(8,128)(2,1)}, u32[]{:S(2)}, u32[]{:S(2)}) collective-permute-start(bf16[2,32,1024]{2,1,0:T(8,128)(2,1)} %get-tuple-element.110), channel_id=1, source_target_pairs={{0,64},{8,72},{16,80},{24,88},{32,96},{40,104},{48,112},{56,120},{... | collective-permute-start | bytes 393224 | tf_op jit(solution)/shard_map/ppermute | solution.py:35
  76.5 16.7 %all-to-all-start = ((bf16[16,8,2048]{2,1,0:T(8,128)(2,1)}), bf16[16,8,2048]{2,1,0:T(8,128)(2,1)S(1)}, u32[]{:S(2)}, u32[]{:S(2)}) async-start(bf16[16,8,2048]{2,1,0:T(8,128)(2,1)} %bitcast.9), calls=%async_computation | async-start | bytes 1048576 | tf_op jit(solution)/shard_map/all_to_all | solution.py:626

commit v3 on v2

--- a/solution.py
+++ b/solution.py
@@ -154,7 +154,6 @@
 
 
 COARSE_ROWS = 768
-FIRST = 7
 RATE = SCALE * math.log2(math.e)
 
 
@@ -504,29 +503,6 @@
     )(*arrays, *after)
 
 
-def back_sum_kernel(*refs):
-    outs = refs[len(refs) - 3 :]
-    column = 0
-    for keep, received in ((refs[0], refs[1]), (refs[2], refs[3])):
-        width = keep.shape[2]
-        for place, out in enumerate(outs):
-            at = (slice(None), slice(place * 128, place * 128 + 128), slice(None))
-            total = keep[at].astype(F32) + received[at].astype(F32)
-            out[:, :, column : column + width] = total.astype(BF16)
-        column = column + width
-
-
-def back_sum(arrays, after):
-    return pl.pallas_call(
-        back_sum_kernel,
-        in_specs=[WHOLE] * 4 + [ANY] * len(after),
-        out_specs=[WHOLE] * 3,
-        out_shape=[jax.ShapeDtypeStruct((2, 128, HD), BF16)] * 3,
-        compiler_params=params(8),
-        cost_estimate=SMALL,
-    )(*arrays, *after)
-
-
 def finish_kernel(*refs):
     dk_ref, dv_ref, one, two, three, four = refs[:6]
     outs, mark_ref = refs[-3:-1], refs[-1]
@@ -604,21 +580,23 @@
 
     late, attention, rows = late_forward(query, grad_across, fq, mixed, stats, later)
     kept, given, mark = grad_weight_part(place, attention, cotangent)
-    one = coarse_backward(query, grad_attention, grad_across, rows, early, late, pieces, range(FIRST), [mark])
-    parts = split_sum([kept, swap(given, "ctx", 1)], 0, (128, 128, 64, 64, 128), [one[3]])
+    keep, give, partial_q, mark = coarse_backward(
+        query, grad_attention, grad_across, rows, early, late, pieces, range(HEADS), [mark]
+    )
+    parts = split_sum([kept, swap(given, "ctx", 1)], 0, (128, 128, 64, 64, 128), [mark])
     lower, upper = shift(parts[2], "dp", 2), shift(parts[3], "dp", -2)
-    rest = coarse_backward(query, grad_attention, grad_across, rows, early, late, pieces, range(FIRST, HEADS), [parts[0]])
-    own_one, own_two, own_xz = back_sum([one[0], swap(one[1], "ctx", 1), rest[0], swap(rest[1], "ctx", 1)], [])
+    own_one, own_two, own_xz = split_sum([keep, swap(give, "ctx", 1)], 1, (128, 128, 128), [parts[0]])
     back_xz = swap(own_xz, "ctx", 2)
-    back_z = swap(own_one, "ctx", 2)
-    partials = [(0, FIRST, one[2]), (FIRST, HEADS, rest[2])]
+    partials = [(0, HEADS, partial_q)]
     *earlier, mark = local_backward(
-        query, key, value, grad_across, rows, early, partials, range(4), (), [own_one]
+        query, key, value, grad_across, rows, early, partials, range(7), (), [own_one]
     )
     up, down = relay([parts[1], parts[4], lower, upper], [mark])
     output, mark = project(attention, out_weight, up)
+    own_one, mark = lax.optimization_barrier((own_one, mark))
+    back_z = swap(own_one, "ctx", 2)
     grad_query, dk, dv, mark = local_backward(
-        query, key, value, grad_across, rows, early, partials, range(4, HEADS), earlier, [mark]
+        query, key, value, grad_across, rows, early, partials, range(7, HEADS), earlier, [mark]
     )
     two, three, four = split_sum([own_two, back_xz], 1, (64, 32, 32), [mark])
     returned = [back_z, swap(two, "ctx", 4), swap(three, "ctx", 12), swap(four, "ctx", 8)]

time: 94.3 us -> 92.9 us (0.985)
  waiting for transfers between devices: 21 us -> 19.3 us
  starting transfers between devices: 27.4 us -> 28.4 us
    ppermute x16 -> x15, waiting for transfers between devices: 12.9 us -> 11.2 us  [swap(): lax.ppermute(array, axis, [(i, i ^ bits) for i in range(lax.axis_size(axi...]
    ppermute x4, starting transfers between devices: 5.4 us -> 6.61 us  [shift(): lax.ppermute(array, axis, [(i, (i + step) % size) for i in range(size)])]
    all_to_all x1, starting transfers between devices: 6.68 us -> 5.54 us  [body(): lax.all_to_all(summed.reshape(16, 8, D), ('ctx', 'dp'), 0, 0, axis_index_...]
    ppermute x16 -> x15, starting transfers between devices: 15.3 us -> 16.2 us  [swap(): lax.ppermute(array, axis, [(i, i ^ bits) for i in range(lax.axis_size(axi...]
    pallas_call x2 -> x1, Pallas kernels: 6.7 us -> 5.98 us  [coarse_backward(): pl.pallas_call(partial(coarse_backward_kernel, heads), in_specs=[WHOLE] *...]
    pallas_call x3 -> x4, Pallas kernels: 2.23 us -> 2.66 us  [split_sum(): pl.pallas_call(partial(split_sum_kernel, len(arrays), axis, bounds), in_s...]
  transfers between devices with their start and end apart: 21 -> 20, of which waited for: 10 -> 8; matrix products, arithmetic and copies ran while one was open for 0% -> 0% of each run, Pallas kernels for 36% -> 36%
where the time goes in v3:
time: 92.9 us; the launch traced here: 92.6 us
  Pallas kernels  41.1 us (44%)
  starting transfers between devices  28.4 us (31%)
  waiting for transfers between devices  19.3 us (21%)
  local copies, waits for them, and re-layouts  3.03 us (3%)
    ppermute x15, starting transfers between devices, swap(): lax.ppermute(array, axis, [(i, i ^ bits) for i in range(lax.axis_size(axi...  16.2 us
    ppermute x15, waiting for transfers between devices, swap(): lax.ppermute(array, axis, [(i, i ^ bits) for i in range(lax.axis_size(axi...  11.2 us
    pallas_call x1, Pallas kernels, early_forward(): pl.pallas_call(early_forward_kernel, in_specs=[WHOLE] * 9 + [ANY] * len(a...  9.34 us
    all_to_all x1, waiting for transfers between devices, body(): lax.all_to_all(summed.reshape(16, 8, D), ('ctx', 'dp'), 0, 0, axis_index_...  7.23 us
    ppermute x4, starting transfers between devices, shift(): lax.ppermute(array, axis, [(i, (i + step) % size) for i in range(size)])  6.61 us
    pallas_call x2, Pallas kernels, local_backward(): pl.pallas_call(partial(local_backward_kernel, heads, [part[:2] for part i...  6.3 us
    pallas_call x1, Pallas kernels, coarse_backward(): pl.pallas_call(partial(coarse_backward_kernel, heads), in_specs=[WHOLE] *...  5.98 us
    all_to_all x1, starting transfers between devices, body(): lax.all_to_all(summed.reshape(16, 8, D), ('ctx', 'dp'), 0, 0, axis_index_...  5.54 us
  transfers between devices with their start and end apart: 20, of which 8 were waited for; matrix products, arithmetic and copies ran while one was open for 0% of the time, Pallas kernels for 36%

profile of v3, /device:TPU:0, one launch (start us, length us, event | category | flops | bytes accessed | tf_op | source)
XLA Modules:
  0.0 92.6 jit_solution(3727580870211445329)
XLA Ops:
  0.6 0.0 copy-start.3
  0.6 0.0 copy-start.6
  0.7 0.8 copy-done.6
  1.5 2.1 %shard_map.102 = (bf16[128,2176]{1,0:T(8,128)(2,1)S(1)}, bf16[64,2176]{1,0:T(8,128)(2,1)S(1)}, bf16[32,2176]{1,0:T(8,128)(2,1)S(1)}, bf16[512,128]{1,0:T(8,128)(...) custom-call(s32[1]{0:T(128)} %bitcast.2.place_ref, s32[1,512]{1,0:T(1,128)S(1)} %copy-done.6, ...), custom_call_target="tpu_custom_call" | custom-call | flops 1024 | bytes 1024 | tf_op jit(solution)/shard_map/pallas_call | solution.py:130
  3.6 2.1 %collective-permute-start = (bf16[128,2176]{1,0:T(8,128)(2,1)S(1)}, bf16[128,2176]{1,0:T(8,128)(2,1)S(1)}, u32[]{:S(2)}, u32[]{:S(2)}) collective-permute-start(bf16[128,2176]{1,0:T(8,128)(2,1)S(1)} %get-tuple-element.62), channel_id=1, source_target_pairs={{0,16},{8,24},{16,0},{24,8},{32,48},{40,56},{48,32},{56,40},{64,80... | collective-permute-start | bytes 1671176 | tf_op jit(solution)/shard_map/ppermute | solution.py:35
  5.6 1.5 %collective-permute-start.1 = (bf16[64,2176]{1,0:T(8,128)(2,1)S(1)}, bf16[64,2176]{1,0:T(8,128)(2,1)S(1)}, u32[]{:S(2)}, u32[]{:S(2)}) collective-permute-start(bf16[64,2176]{1,0:T(8,128)(2,1)S(1)} %get-tuple-element.66), channel_id=1, source_target_pairs={{0,32},{8,40},{16,48},{24,56},{32,0},{40,8},{48,16},{56,24},{64,96... | collective-permute-start | bytes 835592 | tf_op jit(solution)/shard_map/ppermute | solution.py:35
  7.1 2.1 %collective-permute-start.2 = (bf16[32,2176]{1,0:T(8,128)(2,1)S(1)}, bf16[32,2176]{1,0:T(8,128)(2,1)S(1)}, u32[]{:S(2)}, u32[]{:S(2)}) collective-permute-start(bf16[32,2176]{1,0:T(8,128)(2,1)S(1)} %get-tuple-element.67), channel_id=1, source_target_pairs={{0,96},{8,104},{16,112},{24,120},{32,64},{40,72},{48,80},{56,88},{... | collective-permute-start | bytes 417800 | tf_op jit(solution)/shard_map/ppermute | solution.py:35
  9.2 0.6 collective-permute-start.3
  9.9 2.2 %copy-done.4 = bf16[1024,2048]{1,0:T(8,128)(2,1)S(1)} copy-done((bf16[1024,2048]{1,0:T(8,128)(2,1)S(1)}, bf16[1024,2048]{1,0:T(8,128)(2,1)}, u32[]{:S(2)}) %copy-start.4) | copy-done | bytes 4194328
  12.1 2.4 %shard_map.101 = (bf16[512,1024]{1,0:T(8,128)(2,1)S(1)}, bf16[1024,512]{1,0:T(8,128)(2,1)S(1)}) custom-call(bf16[512,2048]{1,0:T(8,128)(2,1)S(1)} %bitcast.23, bf16[1024,2048]{1,0:T(8,128)(2,1)S(1)} %copy-done.4), custom_call_target="tpu_custom_call" | custom-call | flops 1024 | bytes 1024 | tf_op jit(solution)/shard_map/pallas_call | solution.py:384
  14.5 0.0 copy-start
  14.5 0.0 copy-start.1
  14.5 0.0 collective-permute-done.2.refs_1_
  14.5 4.4 %collective-permute-done.3.refs_2_ = bf16[32,2176]{1,0:T(8,128)(2,1)S(1)} collective-permute-done((bf16[32,2176]{1,0:T(8,128)(2,1)S(1)}, bf16[32,2176]{1,0:T(8,128)(2,1)S(1)}, u32[]{:S(2)}, u32[]{:S(2)}) %collective-permute-start.3) | collective-permute-done | bytes 139296 | tf_op jit(solution)/shard_map/ppermute | solution.py:35
  18.9 0.0 collective-permute-done.1.refs_0_
  19.0 0.1 collective-permute-start.5
  19.1 0.0 collective-permute-done.refs_5_.refs_6_
  19.1 0.5 collective-permute-start.4
  19.6 0.4 collective-permute-start.6
  20.0 1.0 %collective-permute-done.5.refs_8_.refs_9_ = bf16[128,2176]{1,0:T(8,128)(2,1)S(1)} collective-permute-done((bf16[128,2176]{1,0:T(8,128)(2,1)S(1)}, bf16[128,2176]{1,0:T(8,128)(2,1)S(1)}, u32[]{:S(2)}, u32[]{:S(2)}) %collective-permute-start.5) | collective-permute-done | bytes 557088 | tf_op jit(solution)/shard_map/ppermute | solution.py:35
  21.0 0.8 collective-permute-done.4.refs_7_.refs_8_
  21.8 0.0 copy-done.2
  21.8 9.3 %shard_map.105 = (bf16[8,1024,512]{2,1,0:T(8,128)(2,1)S(1)}, f32[1024,512]{1,0:T(8,128)S(1)}, f32[8,8,512]{2,1,0:T(8,128)S(1)}) custom-call(bf16[512,1024]{1,0:T(8,128)(2,1)S(1)} %bitcast.10, bf16[512,1024]{1,0:T(8,128)(2,1)S(1)} %bitcast.16, bf16[512,1024]{1,0:T(8,128)(2,1)S(1)} %bitcast.20, bf16[512,128]{1,0:T(8,128)(2,1)S(1)} %get-tuple-element.60.refs_3_.refs_2_, ...), custom_call_target="tpu_custom_call" | custom-call | flops 1024 | bytes 1024 | tf_op jit(solution)/shard_map/pallas_call | solution.py:222
  31.2 3.0 %collective-permute-done.6.refs_5_.refs_10_ = bf16[128,2176]{1,0:T(8,128)(2,1)S(1)} collective-permute-done((bf16[128,2176]{1,0:T(8,128)(2,1)S(1)}, bf16[128,2176]{1,0:T(8,128)(2,1)S(1)}, u32[]{:S(2)}, u32[]{:S(2)}) %collective-permute-start.6) | collective-permute-done | bytes 557088 | tf_op jit(solution)/shard_map/ppermute | solution.py:35
  34.2 0.0 collective-permute-start.7
  34.2 2.0 %collective-permute-done.7.refs_6_.refs_11_ = bf16[128,2176]{1,0:T(8,128)(2,1)S(1)} collective-permute-done((bf16[128,2176]{1,0:T(8,128)(2,1)S(1)}, bf16[128,2176]{1,0:T(8,128)(2,1)S(1)}, u32[]{:S(2)}, u32[]{:S(2)}) %collective-permute-start.7) | collective-permute-done | bytes 557088 | tf_op jit(solution)/shard_map/ppermute | solution.py:35
  36.2 2.6 %shard_map.106 = (bf16[8,256,512]{2,1,0:T(8,128)(2,1)S(1)}, bf16[1024,512]{1,0:T(8,128)(2,1)S(1)}, f32[8,8,512]{2,1,0:T(8,128)S(1)}) custom-call(bf16[512,1024]{1,0:T(8,128)(2,1)S(1)} %bitcast.11, bf16[1024,512]{1,0:T(8,128)(2,1)S(1)} %get-tuple-element.59.refs_1_.refs_2_.refs_3_, bf16[512,128]{1,0:T(8,128)(2,1)S(1)} %get-tuple-element.60.refs_3_.refs_2_, ...), custom_call_target="tpu_custom_call" | custom-call | flops 1024 | bytes 1024 | tf_op jit(solution)/shard_map/pallas_call | solution.py:263
  38.8 2.3 %shard_map.107 = (bf16[512,2048]{1,0:T(8,128)(2,1)S(1)}, bf16[512,2048]{1,0:T(8,128)(2,1)S(1)}, f32[8,128]{1,0:T(8,128)S(1)}) custom-call(s32[1]{0:T(128)} %bitcast.2.place_ref, bf16[1024,512]{1,0:T(8,128)(2,1)S(1)} %get-tuple-element.74.ot_ref.a_ref, bf16[512,2048]{1,0:T(8,128)(2,1)S(1)} %bitcast.24), custom_call_target="tpu_custom_call" | custom-call | flops 1024 | bytes 1024 | tf_op jit(solution)/shard_map/pallas_call | solution.py:449
  41.1 0.4 collective-permute-start.8
  41.5 6.0 %shard_map.108 = (bf16[2,384,1024]{2,1,0:T(8,128)(2,1)S(1)}, bf16[2,384,1024]{2,1,0:T(8,128)(2,1)S(1)}, f32[1024,512]{1,0:T(8,128)S(1)}, f32[8,128]{1,0:T(8,128)S(1)}) custom-call(bf16[512,1024]{1,0:T(8,128)(2,1)S(1)} %bitcast.12, bf16[512,1024]{1,0:T(8,128)(2,1)S(1)} %get-tuple-element.68.refs_3_.refs_1_, ...), custom_call_target="tpu_custom_call" | custom-call | flops 1024 | bytes 1024 | tf_op jit(solution)/shard_map/pallas_call | solution.py:319
  47.5 0.4 collective-permute-start.11
  48.0 0.0 collective-permute-done.8.refs_1_
  48.0 0.5 shard_map.109
  48.5 1.6 %collective-permute-start.9 = (bf16[64,2048]{1,0:T(8,128)(2,1)S(1)}, bf16[64,2048]{1,0:T(8,128)(2,1)S(1)}, u32[]{:S(2)}, u32[]{:S(2)}) collective-permute-start(bf16[64,2048]{1,0:T(8,128)(2,1)S(1)} %get-tuple-element.84), channel_id=1, source_target_pairs={{0,2},{1,3},{2,4},{3,5},{4,6},{5,7},{6,0},{7,1},{8,10},{9,11},{10,... | collective-permute-start | bytes 786440 | tf_op jit(solution)/shard_map/ppermute | solution.py:40
  50.2 1.7 %collective-permute-start.10 = (bf16[64,2048]{1,0:T(8,128)(2,1)S(1)}, bf16[64,2048]{1,0:T(8,128)(2,1)S(1)}, u32[]{:S(2)}, u32[]{:S(2)}) collective-permute-start(bf16[64,2048]{1,0:T(8,128)(2,1)S(1)} %get-tuple-element.85), channel_id=1, source_target_pairs={{0,6},{1,7},{2,0},{3,1},{4,2},{5,3},{6,4},{7,5},{8,14},{9,15},{10,... | collective-permute-start | bytes 786440 | tf_op jit(solution)/shard_map/ppermute | solution.py:40
  51.8 0.0 collective-permute-done.11.refs_1_
  51.8 0.4 shard_map.110
  52.2 1.1 %collective-permute-start.13 = (bf16[2,128,1024]{2,1,0:T(8,128)(2,1)S(1)}, bf16[2,128,1024]{2,1,0:T(8,128)(2,1)S(1)}, u32[]{:S(2)}, u32[]{:S(2)}) collective-permute-start(bf16[2,128,1024]{2,1,0:T(8,128)(2,1)S(1)} %get-tuple-element.104), channel_id=1, source_target_pairs={{0,16},{8,24},{16,0},{24,8},{32,48},{40,56},{48,32},{56,40},{64,80... | collective-permute-start | bytes 1572872 | tf_op jit(solution)/shard_map/ppermute | solution.py:35
  53.3 4.3 %shard_map.111 = (bf16[512,896]{1,0:T(8,128)(2,1)S(1)}, bf16[512,896]{1,0:T(8,128)(2,1)S(1)}, bf16[512,896]{1,0:T(8,128)(2,1)S(1)}, f32[8,128]{1,0:T(8,128)S(1)}) custom-call(bf16[512,1024]{1,0:T(8,128)(2,1)S(1)} %bitcast.13, bf16[512,1024]{1,0:T(8,128)(2,1)S(1)} %bitcast.17, bf16[512,1024]{1,0:T(8,128)(2,1)S(1)} %bitcast.21, ...), custom_call_target="tpu_custom_call" | custom-call | flops 1024 | bytes 1024 | tf_op jit(solution)/shard_map/pallas_call | solution.py:366
  57.6 0.6 collective-permute-done.9.lower_ref
  58.2 0.0 collective-permute-done.10.upper_ref
  58.2 0.1 shard_map.112
  58.4 1.6 %collective-permute-start.17 = (bf16[128,2048]{1,0:T(8,128)(2,1)S(1)}, bf16[128,2048]{1,0:T(8,128)(2,1)S(1)}, u32[]{:S(2)}, u32[]{:S(2)}) collective-permute-start(bf16[128,2048]{1,0:T(8,128)(2,1)S(1)} %get-tuple-element.92._), channel_id=1, source_target_pairs={{0,2},{1,3},{2,4},{3,5},{4,6},{5,7},{6,0},{7,1},{8,10},{9,11},{10,... | collective-permute-start | bytes 1572872 | tf_op jit(solution)/shard_map/ppermute | solution.py:40
  60.0 1.7 %collective-permute-start.18 = (bf16[128,2048]{1,0:T(8,128)(2,1)S(1)}, bf16[128,2048]{1,0:T(8,128)(2,1)S(1)}, u32[]{:S(2)}, u32[]{:S(2)}) collective-permute-start(bf16[128,2048]{1,0:T(8,128)(2,1)S(1)} %get-tuple-element.111), channel_id=1, source_target_pairs={{0,6},{1,7},{2,0},{3,1},{4,2},{5,3},{6,4},{7,5},{8,14},{9,15},{10,... | collective-permute-start | bytes 1572872 | tf_op jit(solution)/shard_map/ppermute | solution.py:40
  61.7 0.0 copy-done.5
  61.7 3.7 %shard_map.113 = (bf16[512,2048]{1,0:T(8,128)(2,1)}, f32[8,128]{1,0:T(8,128)S(1)}) custom-call(bf16[1024,512]{1,0:T(8,128)(2,1)S(1)} %get-tuple-element.74.ot_ref.a_ref, bf16[1024,2048]{1,0:T(8,128)(2,1)S(1)} %copy-done.5, bf16[128,2048]{1,0:T(8,128)(2,1)S(1)} %get-tuple-element.92._), custom_call_target="tpu_custom_call" | custom-call | flops 20000000000 | bytes 1024 | tf_op jit(solution)/shard_map/pallas_call | solution.py:401
  65.4 0.8 collective-permute-start.12
  66.3 2.0 %shard_map.114 = (bf16[512,1024]{1,0:T(8,128)(2,1)}, bf16[512,1024]{1,0:T(8,128)(2,1)S(1)}, bf16[512,1024]{1,0:T(8,128)(2,1)S(1)}, f32[8,128]{1,0:T(8,128)S(1)}) custom-call(bf16[512,1024]{1,0:T(8,128)(2,1)S(1)} %bitcast.14, bf16[512,1024]{1,0:T(8,128)(2,1)S(1)} %bitcast.18, bf16[512,1024]{1,0:T(8,128)(2,1)S(1)} %bitcast.22, ...), custom_call_target="tpu_custom_call" | custom-call | flops 1024 | bytes 1024 | tf_op jit(solution)/shard_map/pallas_call | solution.py:366
  68.3 0.0 collective-permute-done.13.refs_1_
  68.3 0.8 shard_map.115
  69.1 1.5 %collective-permute-start.14 = (bf16[2,64,1024]{2,1,0:T(8,128)(2,1)S(1)}, bf16[2,64,1024]{2,1,0:T(8,128)(2,1)}, u32[]{:S(2)}, u32[]{:S(2)}) collective-permute-start(bf16[2,64,1024]{2,1,0:T(8,128)(2,1)S(1)} %get-tuple-element.106.refs_3_), channel_id=1, source_target_pairs={{0,32},{8,40},{16,48},{24,56},{32,0},{40,8},{48,16},{56,24},{64,96... | collective-permute-start | bytes 786440 | tf_op jit(solution)/shard_map/ppermute | solution.py:35
  70.5 2.1 %collective-permute-start.15 = (bf16[2,32,1024]{2,1,0:T(8,128)(2,1)}, bf16[2,32,1024]{2,1,0:T(8,128)(2,1)S(1)}, u32[]{:S(2)}, u32[]{:S(2)}) collective-permute-start(bf16[2,32,1024]{2,1,0:T(8,128)(2,1)} %get-tuple-element.107), channel_id=1, source_target_pairs={{0,96},{8,104},{16,112},{24,120},{32,64},{40,72},{48,80},{56,88},{... | collective-permute-start | bytes 393224 | tf_op jit(solution)/shard_map/ppermute | solution.py:35
  72.7 0.2 collective-permute-done.17.refs_1_
  72.8 2.5 %collective-permute-start.16 = (bf16[2,32,1024]{2,1,0:T(8,128)(2,1)}, bf16[2,32,1024]{2,1,0:T(8,128)(2,1)}, u32[]{:S(2)}, u32[]{:S(2)}) collective-permute-start(bf16[2,32,1024]{2,1,0:T(8,128)(2,1)} %get-tuple-element.108), channel_id=1, source_target_pairs={{0,64},{8,72},{16,80},{24,88},{32,96},{40,104},{48,112},{56,120},{... | collective-permute-start | bytes 393224 | tf_op jit(solution)/shard_map/ppermute | solution.py:35
  75.3 0.0 collective-permute-done.18.refs_2_
  75.3 1.0 %shard_map.117 = bf16[128,2048]{1,0:T(8,128)(2,1)} custom-call(bf16[128,2048]{1,0:T(8,128)(2,1)S(1)} %get-tuple-element.89.refs_2_.refs_0_, bf16[128,2048]{1,0:T(8,128)(2,1)S(1)} %collective-permute-done.17.refs_1_, bf16[128,2048]{1,0:T(8,128)(2,1)S(1)} %collective-permute-done.18.refs_2_, bf16[2,64,1024]{2,1,0:T(8,128)(2,1)S(1)} %get-tuple-element.106.refs_3_), custom_call_target="tpu_custom_call" | custom-call | flops 1024 | bytes 1024 | tf_op jit(solution)/shard_map/pallas_call | solution.py:477
  76.4 5.5 %all-to-all-start = ((bf16[16,8,2048]{2,1,0:T(8,128)(2,1)}), bf16[16,8,2048]{2,1,0:T(8,128)(2,1)S(1)}, u32[]{:S(2)}, u32[]{:S(2)}) async-start(bf16[16,8,2048]{2,1,0:T(8,128)(2,1)} %bitcast.9), calls=%async_computation | async-start | bytes 1048576 | tf_op jit(solution)/shard_map/all_to_all | solution.py:604
  81.9 0.0 collective-permute-done.15.refs_4_
  81.9 0.0 collective-permute-done.16.refs_5_
  81.9 0.0 collective-permute-done.12.refs_2_
  81.9 0.0 collective-permute-done.14.refs_3_
  81.9 2.8 %shard_map.116 = (bf16[512,1024]{1,0:T(8,128)(2,1)}, bf16[512,1024]{1,0:T(8,128)(2,1)}, f32[8,128]{1,0:T(8,128)S(1)}) custom-call(bf16[512,1024]{1,0:T(8,128)(2,1)S(1)} %get-tuple-element.100.refs_0_, bf16[512,1024]{1,0:T(8,128)(2,1)S(1)} %get-tuple-element.101.refs_1_, bf16[2,128,1024]{2,1,0:T(8,128)(2,1)} %collective-permute-done.12.refs_2_, ...), custom_call_target="tpu_custom_call" | custom-call | flops 20000000000 | bytes 1024 | tf_op jit(solution)/shard_map/pallas_call | solution.py:527
  84.7 7.2 %all-to-all-done.ref = bf16[16,8,2048]{2,1,0:T(8,128)(2,1)S(1)} async-done(((bf16[16,8,2048]{2,1,0:T(8,128)(2,1)}), bf16[16,8,2048]{2,1,0:T(8,128)(2,1)S(1)}, u32[]{:S(2)}, u32[]{:S(2)}) %all-to-all-start) | async-done | bytes 524320 | tf_op jit(solution)/shard_map/all_to_all | solution.py:604
  91.9 0.7 shard_map.118
  (8 shorter events, 0.1 us)
Async XLA Ops:
  0.6 9.2 %copy-start.3 = (bf16[1,512,2048]{2,1,0:T(8,128)(2,1)S(1)}, bf16[1,512,2048]{2,1,0:T(8,128)(2,1)}, u32[]{:S(2)}) copy-start(bf16[1,512,2048]{2,1,0:T(8,128)(2,1)} %param.11) | copy-start | bytes 6291460
  0.6 0.8 copy-start.6
  3.6 15.5 %collective-permute-start = (bf16[128,2176]{1,0:T(8,128)(2,1)S(1)}, bf16[128,2176]{1,0:T(8,128)(2,1)S(1)}, u32[]{:S(2)}, u32[]{:S(2)}) collective-permute-start(bf16[128,2176]{1,0:T(8,128)(2,1)S(1)} %get-tuple-element.62), channel_id=1, source_target_pairs={{0,16},{8,24},{16,0},{24,8},{32,48},{40,56},{48,32},{56,40},{64,80... | collective-permute-start | bytes 1671176 | tf_op jit(solution)/shard_map/ppermute | solution.py:35
  5.6 13.3 %collective-permute-start.1 = (bf16[64,2176]{1,0:T(8,128)(2,1)S(1)}, bf16[64,2176]{1,0:T(8,128)(2,1)S(1)}, u32[]{:S(2)}, u32[]{:S(2)}) collective-permute-start(bf16[64,2176]{1,0:T(8,128)(2,1)S(1)} %get-tuple-element.66), channel_id=1, source_target_pairs={{0,32},{8,40},{16,48},{24,56},{32,0},{40,8},{48,16},{56,24},{64,96... | collective-permute-start | bytes 835592 | tf_op jit(solution)/shard_map/ppermute | solution.py:35
  7.1 7.4 %collective-permute-start.2 = (bf16[32,2176]{1,0:T(8,128)(2,1)S(1)}, bf16[32,2176]{1,0:T(8,128)(2,1)S(1)}, u32[]{:S(2)}, u32[]{:S(2)}) collective-permute-start(bf16[32,2176]{1,0:T(8,128)(2,1)S(1)} %get-tuple-element.67), channel_id=1, source_target_pairs={{0,96},{8,104},{16,112},{24,120},{32,64},{40,72},{48,80},{56,88},{... | collective-permute-start | bytes 417800 | tf_op jit(solution)/shard_map/ppermute | solution.py:35
  9.2 9.7 %collective-permute-start.3 = (bf16[32,2176]{1,0:T(8,128)(2,1)S(1)}, bf16[32,2176]{1,0:T(8,128)(2,1)S(1)}, u32[]{:S(2)}, u32[]{:S(2)}) collective-permute-start(bf16[32,2176]{1,0:T(8,128)(2,1)S(1)} %get-tuple-element.67), channel_id=1, source_target_pairs={{0,64},{8,72},{16,80},{24,88},{32,96},{40,104},{48,112},{56,120},{... | collective-permute-start | bytes 417800 | tf_op jit(solution)/shard_map/ppermute | solution.py:35
  9.9 2.2 %copy-start.4 = (bf16[1024,2048]{1,0:T(8,128)(2,1)S(1)}, bf16[1024,2048]{1,0:T(8,128)(2,1)}, u32[]{:S(2)}) copy-start(bf16[1024,2048]{1,0:T(8,128)(2,1)} %w_ref.3) | copy-start | bytes 12582916
  12.1 9.8 %copy-start.2 = (bf16[1,512,1024]{2,1,0:T(8,128)(2,1)S(1)}, bf16[1,512,1024]{2,1,0:T(8,128)(2,1)}, u32[]{:S(2)}) copy-start(bf16[1,512,1024]{2,1,0:T(8,128)(2,1)} %param.8) | copy-start | bytes 3145732
  14.5 7.3 %copy-start = (bf16[1,512,1024]{2,1,0:T(8,128)(2,1)S(1)}, bf16[1,512,1024]{2,1,0:T(8,128)(2,1)}, u32[]{:S(2)}) copy-start(bf16[1,512,1024]{2,1,0:T(8,128)(2,1)} %param.6) | copy-start | bytes 3145732
  14.5 7.3 %copy-start.1 = (bf16[1,512,1024]{2,1,0:T(8,128)(2,1)S(1)}, bf16[1,512,1024]{2,1,0:T(8,128)(2,1)}, u32[]{:S(2)}) copy-start(bf16[1,512,1024]{2,1,0:T(8,128)(2,1)} %param.7) | copy-start | bytes 3145732
  19.0 2.0 %collective-permute-start.5 = (bf16[128,2176]{1,0:T(8,128)(2,1)S(1)}, bf16[128,2176]{1,0:T(8,128)(2,1)S(1)}, u32[]{:S(2)}, u32[]{:S(2)}) collective-permute-start(bf16[128,2176]{1,0:T(8,128)(2,1)S(1)} %shard_map.104.refs_6_.refs_7_), channel_id=1, source_target_pairs={{0,8},{8,0},{16,24},{24,16},{32,40},{40,32},{48,56},{56,48},{64,72... | collective-permute-start | bytes 1671176 | tf_op jit(solution)/shard_map/ppermute | solution.py:35
  19.1 2.7 %collective-permute-start.4 = (bf16[128,2176]{1,0:T(8,128)(2,1)S(1)}, bf16[128,2176]{1,0:T(8,128)(2,1)S(1)}, u32[]{:S(2)}, u32[]{:S(2)}) collective-permute-start(bf16[128,2176]{1,0:T(8,128)(2,1)S(1)} %collective-permute-done.refs_5_.refs_6_), channel_id=1, source_target_pairs={{0,8},{8,0},{16,24},{24,16},{32,40},{40,32},{48,56},{56,48},{64,72... | collective-permute-start | bytes 1671176 | tf_op jit(solution)/shard_map/ppermute | solution.py:35
  19.6 14.6 %collective-permute-start.6 = (bf16[128,2176]{1,0:T(8,128)(2,1)S(1)}, bf16[128,2176]{1,0:T(8,128)(2,1)S(1)}, u32[]{:S(2)}, u32[]{:S(2)}) collective-permute-start(bf16[128,2176]{1,0:T(8,128)(2,1)S(1)} %shard_map.104.refs_6_.refs_7_), channel_id=1, source_target_pairs={{0,16},{8,24},{16,0},{24,8},{32,48},{40,56},{48,32},{56,40},{64,80... | collective-permute-start | bytes 1671176 | tf_op jit(solution)/shard_map/ppermute | solution.py:35
  34.2 2.0 %collective-permute-start.7 = (bf16[128,2176]{1,0:T(8,128)(2,1)S(1)}, bf16[128,2176]{1,0:T(8,128)(2,1)S(1)}, u32[]{:S(2)}, u32[]{:S(2)}) collective-permute-start(bf16[128,2176]{1,0:T(8,128)(2,1)S(1)} %collective-permute-done.6.refs_5_.refs_10_), channel_id=1, source_target_pairs={{0,8},{8,0},{16,24},{24,16},{32,40},{40,32},{48,56},{56,48},{64,72... | collective-permute-start | bytes 1671176 | tf_op jit(solution)/shard_map/ppermute | solution.py:35
  41.1 6.8 %collective-permute-start.8 = (bf16[512,2048]{1,0:T(8,128)(2,1)S(1)}, bf16[512,2048]{1,0:T(8,128)(2,1)S(1)}, u32[]{:S(2)}, u32[]{:S(2)}) collective-permute-start(bf16[512,2048]{1,0:T(8,128)(2,1)S(1)} %get-tuple-element.76), channel_id=1, source_target_pairs={{0,8},{8,0},{16,24},{24,16},{32,40},{40,32},{48,56},{56,48},{64,72... | collective-permute-start | bytes 6291464 | tf_op jit(solution)/shard_map/ppermute | solution.py:35
  47.5 4.3 %collective-permute-start.11 = (bf16[2,384,1024]{2,1,0:T(8,128)(2,1)S(1)}, bf16[2,384,1024]{2,1,0:T(8,128)(2,1)S(1)}, u32[]{:S(2)}, u32[]{:S(2)}) collective-permute-start(bf16[2,384,1024]{2,1,0:T(8,128)(2,1)S(1)} %get-tuple-element.88), channel_id=1, source_target_pairs={{0,8},{8,0},{16,24},{24,16},{32,40},{40,32},{48,56},{56,48},{64,72... | collective-permute-start | bytes 4718600 | tf_op jit(solution)/shard_map/ppermute | solution.py:35
  48.5 9.7 %collective-permute-start.9 = (bf16[64,2048]{1,0:T(8,128)(2,1)S(1)}, bf16[64,2048]{1,0:T(8,128)(2,1)S(1)}, u32[]{:S(2)}, u32[]{:S(2)}) collective-permute-start(bf16[64,2048]{1,0:T(8,128)(2,1)S(1)} %get-tuple-element.84), channel_id=1, source_target_pairs={{0,2},{1,3},{2,4},{3,5},{4,6},{5,7},{6,0},{7,1},{8,10},{9,11},{10,... | collective-permute-start | bytes 786440 | tf_op jit(solution)/shard_map/ppermute | solution.py:40
  50.2 8.1 %collective-permute-start.10 = (bf16[64,2048]{1,0:T(8,128)(2,1)S(1)}, bf16[64,2048]{1,0:T(8,128)(2,1)S(1)}, u32[]{:S(2)}, u32[]{:S(2)}) collective-permute-start(bf16[64,2048]{1,0:T(8,128)(2,1)S(1)} %get-tuple-element.85), channel_id=1, source_target_pairs={{0,6},{1,7},{2,0},{3,1},{4,2},{5,3},{6,4},{7,5},{8,14},{9,15},{10,... | collective-permute-start | bytes 786440 | tf_op jit(solution)/shard_map/ppermute | solution.py:40
  52.2 16.1 %collective-permute-start.13 = (bf16[2,128,1024]{2,1,0:T(8,128)(2,1)S(1)}, bf16[2,128,1024]{2,1,0:T(8,128)(2,1)S(1)}, u32[]{:S(2)}, u32[]{:S(2)}) collective-permute-start(bf16[2,128,1024]{2,1,0:T(8,128)(2,1)S(1)} %get-tuple-element.104), channel_id=1, source_target_pairs={{0,16},{8,24},{16,0},{24,8},{32,48},{40,56},{48,32},{56,40},{64,80... | collective-permute-start | bytes 1572872 | tf_op jit(solution)/shard_map/ppermute | solution.py:35
  53.3 8.4 %copy-start.5 = (bf16[1024,2048]{1,0:T(8,128)(2,1)S(1)}, bf16[1024,2048]{1,0:T(8,128)(2,1)}, u32[]{:S(2)}) copy-start(bf16[1024,2048]{1,0:T(8,128)(2,1)} %w_ref.3) | copy-start | bytes 12582916
  58.4 14.5 %collective-permute-start.17 = (bf16[128,2048]{1,0:T(8,128)(2,1)S(1)}, bf16[128,2048]{1,0:T(8,128)(2,1)S(1)}, u32[]{:S(2)}, u32[]{:S(2)}) collective-permute-start(bf16[128,2048]{1,0:T(8,128)(2,1)S(1)} %get-tuple-element.92._), channel_id=1, source_target_pairs={{0,2},{1,3},{2,4},{3,5},{4,6},{5,7},{6,0},{7,1},{8,10},{9,11},{10,... | collective-permute-start | bytes 1572872 | tf_op jit(solution)/shard_map/ppermute | solution.py:40
  60.0 15.3 %collective-permute-start.18 = (bf16[128,2048]{1,0:T(8,128)(2,1)S(1)}, bf16[128,2048]{1,0:T(8,128)(2,1)S(1)}, u32[]{:S(2)}, u32[]{:S(2)}) collective-permute-start(bf16[128,2048]{1,0:T(8,128)(2,1)S(1)} %get-tuple-element.111), channel_id=1, source_target_pairs={{0,6},{1,7},{2,0},{3,1},{4,2},{5,3},{6,4},{7,5},{8,14},{9,15},{10,... | collective-permute-start | bytes 1572872 | tf_op jit(solution)/shard_map/ppermute | solution.py:40
  65.4 16.5 %collective-permute-start.12 = (bf16[2,128,1024]{2,1,0:T(8,128)(2,1)S(1)}, bf16[2,128,1024]{2,1,0:T(8,128)(2,1)}, u32[]{:S(2)}, u32[]{:S(2)}) collective-permute-start(bf16[2,128,1024]{2,1,0:T(8,128)(2,1)S(1)} %get-tuple-element.102.refs_7_), channel_id=1, source_target_pairs={{0,16},{8,24},{16,0},{24,8},{32,48},{40,56},{48,32},{56,40},{64,80... | collective-permute-start | bytes 1572872 | tf_op jit(solution)/shard_map/ppermute | solution.py:35
  69.1 12.9 %collective-permute-start.14 = (bf16[2,64,1024]{2,1,0:T(8,128)(2,1)S(1)}, bf16[2,64,1024]{2,1,0:T(8,128)(2,1)}, u32[]{:S(2)}, u32[]{:S(2)}) collective-permute-start(bf16[2,64,1024]{2,1,0:T(8,128)(2,1)S(1)} %get-tuple-element.106.refs_3_), channel_id=1, source_target_pairs={{0,32},{8,40},{16,48},{24,56},{32,0},{40,8},{48,16},{56,24},{64,96... | collective-permute-start | bytes 786440 | tf_op jit(solution)/shard_map/ppermute | solution.py:35
  70.5 11.4 %collective-permute-start.15 = (bf16[2,32,1024]{2,1,0:T(8,128)(2,1)}, bf16[2,32,1024]{2,1,0:T(8,128)(2,1)S(1)}, u32[]{:S(2)}, u32[]{:S(2)}) collective-permute-start(bf16[2,32,1024]{2,1,0:T(8,128)(2,1)} %get-tuple-element.107), channel_id=1, source_target_pairs={{0,96},{8,104},{16,112},{24,120},{32,64},{40,72},{48,80},{56,88},{... | collective-permute-start | bytes 393224 | tf_op jit(solution)/shard_map/ppermute | solution.py:35
  72.8 9.1 %collective-permute-start.16 = (bf16[2,32,1024]{2,1,0:T(8,128)(2,1)}, bf16[2,32,1024]{2,1,0:T(8,128)(2,1)}, u32[]{:S(2)}, u32[]{:S(2)}) collective-permute-start(bf16[2,32,1024]{2,1,0:T(8,128)(2,1)} %get-tuple-element.108), channel_id=1, source_target_pairs={{0,64},{8,72},{16,80},{24,88},{32,96},{40,104},{48,112},{56,120},{... | collective-permute-start | bytes 393224 | tf_op jit(solution)/shard_map/ppermute | solution.py:35
  76.4 15.6 %all-to-all-start = ((bf16[16,8,2048]{2,1,0:T(8,128)(2,1)}), bf16[16,8,2048]{2,1,0:T(8,128)(2,1)S(1)}, u32[]{:S(2)}, u32[]{:S(2)}) async-start(bf16[16,8,2048]{2,1,0:T(8,128)(2,1)} %bitcast.9), calls=%async_computation | async-start | bytes 1048576 | tf_op jit(solution)/shard_map/all_to_all | solution.py:604

commit v4 on v3

--- a/solution.py
+++ b/solution.py
@@ -79,10 +79,11 @@
 
 
 def pool_kernel(place_ref, seg_hbm, key_hbm, value_hbm, one, two, three, fq_ref, fk_ref, mark_ref, seg_ref, key_ref, value_ref, sems):
-    copies = [
-        pltpu.make_async_copy(source, target, sems.at[place])
-        for place, (source, target) in enumerate(((seg_hbm, seg_ref), (key_hbm, key_ref), (value_hbm, value_ref)))
-    ]
+    copies = [pltpu.make_async_copy(seg_hbm, seg_ref, sems.at[0])]
+    for source, target in ((key_hbm, key_ref), (value_hbm, value_ref)):
+        for start in range(0, HD, 256):
+            at = pl.ds(start, 256)
+            copies.append(pltpu.make_async_copy(source.at[:, at], target.at[:, at], sems.at[len(copies)]))
     for copy in copies:
         copy.start()
     mark_ref[...] = jnp.zeros_like(mark_ref)
@@ -108,12 +109,12 @@
         parts = offset_parts(factor)
         offset = jnp.where(lane == 2, parts[0], jnp.where(lane == 3, parts[1], jnp.where(lane == 4, parts[2], 0.0)))
         out[:, 2 * HD :] = (picked[starts[place] : starts[place + 1]] + offset).astype(BF16)
-    for copy, ref, column in zip(copies[1:], (key_ref, value_ref), (0, HD)):
+    for place, copy in enumerate(copies[1:]):
+        ref, start, column = (key_ref, value_ref)[place // 4], place % 4 * 256, place * 256
         copy.wait()
-        for start in range(0, HD, 256):
-            mean = dot_nn(pool, ref[:, start : start + 256])
-            for place, out in enumerate(outs):
-                out[:, column + start : column + start + 256] = mean[starts[place] : starts[place + 1]].astype(BF16)
+        mean = dot_nn(pool, ref[:, start : start + 256])
+        for level, out in enumerate(outs):
+            out[:, column : column + 256] = mean[starts[level] : starts[level + 1]].astype(BF16)
 
 
 WIDTH = 2 * HD + HEAD_DIM
@@ -132,7 +133,7 @@
         in_specs=[pl.BlockSpec(memory_space=pltpu.SMEM)] + [HBM] * 3,
         out_specs=[WHOLE] * 6,
         out_shape=[jax.ShapeDtypeStruct((count, WIDTH), BF16) for count in COARSE] + [feature, feature, MARK],
-        scratch_shapes=[pltpu.VMEM((1, ROWS), jnp.int32), token, token, pltpu.SemaphoreType.DMA((3,))],
+        scratch_shapes=[pltpu.VMEM((1, ROWS), jnp.int32), token, token, pltpu.SemaphoreType.DMA((9,))],
         compiler_params=params(POOL_LIMIT),
         cost_estimate=SMALL,
     )(place, seg, key, value)

time: 92.9 us -> 94 us (1.012)
  Pallas kernels: 41.1 us -> 42.3 us
    pallas_call x1, Pallas kernels: 2.08 us -> 3.2 us  [pool(): pl.pallas_call(pool_kernel, in_specs=[pl.BlockSpec(memory_space=pltpu.SME...]
where the time goes in v4:
time: 94 us; the launch traced here: 93.8 us
  Pallas kernels  42.3 us (45%)
  starting transfers between devices  28.4 us (30%)
  waiting for transfers between devices  19.3 us (21%)
  local copies, waits for them, and re-layouts  3.03 us (3%)
    ppermute x15, starting transfers between devices, swap(): lax.ppermute(array, axis, [(i, i ^ bits) for i in range(lax.axis_size(axi...  16.2 us
    ppermute x15, waiting for transfers between devices, swap(): lax.ppermute(array, axis, [(i, i ^ bits) for i in range(lax.axis_size(axi...  11.2 us
    pallas_call x1, Pallas kernels, early_forward(): pl.pallas_call(early_forward_kernel, in_specs=[WHOLE] * 9 + [ANY] * len(a...  9.34 us
    all_to_all x1, waiting for transfers between devices, body(): lax.all_to_all(summed.reshape(16, 8, D), ('ctx', 'dp'), 0, 0, axis_index_...  7.23 us
    ppermute x4, starting transfers between devices, shift(): lax.ppermute(array, axis, [(i, (i + step) % size) for i in range(size)])  6.61 us
    pallas_call x2, Pallas kernels, local_backward(): pl.pallas_call(partial(local_backward_kernel, heads, [part[:2] for part i...  6.3 us
    pallas_call x1, Pallas kernels, coarse_backward(): pl.pallas_call(partial(coarse_backward_kernel, heads), in_specs=[WHOLE] *...  5.98 us
    all_to_all x1, starting transfers between devices, body(): lax.all_to_all(summed.reshape(16, 8, D), ('ctx', 'dp'), 0, 0, axis_index_...  5.53 us
  transfers between devices with their start and end apart: 20, of which 8 were waited for; matrix products, arithmetic and copies ran while one was open for 0% of the time, Pallas kernels for 36%

profile of v4, /device:TPU:0, one launch (start us, length us, event | category | flops | bytes accessed | tf_op | source)
XLA Modules:
  0.0 93.8 jit_solution(2698066167681421409)
XLA Ops:
  0.6 0.0 copy-start.3
  0.7 0.8 copy-done.6
  1.5 3.2 %shard_map.102 = (bf16[128,2176]{1,0:T(8,128)(2,1)S(1)}, bf16[64,2176]{1,0:T(8,128)(2,1)S(1)}, bf16[32,2176]{1,0:T(8,128)(2,1)S(1)}, bf16[512,128]{1,0:T(8,128)(...) custom-call(s32[1]{0:T(128)} %bitcast.2.place_ref, s32[1,512]{1,0:T(1,128)S(1)} %copy-done.6, ...), custom_call_target="tpu_custom_call" | custom-call | flops 1024 | bytes 1024 | tf_op jit(solution)/shard_map/pallas_call | solution.py:131
  4.7 2.1 %collective-permute-start = (bf16[128,2176]{1,0:T(8,128)(2,1)S(1)}, bf16[128,2176]{1,0:T(8,128)(2,1)S(1)}, u32[]{:S(2)}, u32[]{:S(2)}) collective-permute-start(bf16[128,2176]{1,0:T(8,128)(2,1)S(1)} %get-tuple-element.62), channel_id=1, source_target_pairs={{0,16},{8,24},{16,0},{24,8},{32,48},{40,56},{48,32},{56,40},{64,80... | collective-permute-start | bytes 1671176 | tf_op jit(solution)/shard_map/ppermute | solution.py:35
  6.8 1.5 %collective-permute-start.1 = (bf16[64,2176]{1,0:T(8,128)(2,1)S(1)}, bf16[64,2176]{1,0:T(8,128)(2,1)S(1)}, u32[]{:S(2)}, u32[]{:S(2)}) collective-permute-start(bf16[64,2176]{1,0:T(8,128)(2,1)S(1)} %get-tuple-element.66), channel_id=1, source_target_pairs={{0,32},{8,40},{16,48},{24,56},{32,0},{40,8},{48,16},{56,24},{64,96... | collective-permute-start | bytes 835592 | tf_op jit(solution)/shard_map/ppermute | solution.py:35
  8.3 2.1 %collective-permute-start.2 = (bf16[32,2176]{1,0:T(8,128)(2,1)S(1)}, bf16[32,2176]{1,0:T(8,128)(2,1)S(1)}, u32[]{:S(2)}, u32[]{:S(2)}) collective-permute-start(bf16[32,2176]{1,0:T(8,128)(2,1)S(1)} %get-tuple-element.67), channel_id=1, source_target_pairs={{0,96},{8,104},{16,112},{24,120},{32,64},{40,72},{48,80},{56,88},{... | collective-permute-start | bytes 417800 | tf_op jit(solution)/shard_map/ppermute | solution.py:35
  10.4 0.6 collective-permute-start.3
  11.0 0.0 copy-done.3
  11.0 2.2 %copy-done.4 = bf16[1024,2048]{1,0:T(8,128)(2,1)S(1)} copy-done((bf16[1024,2048]{1,0:T(8,128)(2,1)S(1)}, bf16[1024,2048]{1,0:T(8,128)(2,1)}, u32[]{:S(2)}) %copy-start.4) | copy-done | bytes 4194328
  13.2 2.4 %shard_map.101 = (bf16[512,1024]{1,0:T(8,128)(2,1)S(1)}, bf16[1024,512]{1,0:T(8,128)(2,1)S(1)}) custom-call(bf16[512,2048]{1,0:T(8,128)(2,1)S(1)} %bitcast.23, bf16[1024,2048]{1,0:T(8,128)(2,1)S(1)} %copy-done.4), custom_call_target="tpu_custom_call" | custom-call | flops 1024 | bytes 1024 | tf_op jit(solution)/shard_map/pallas_call | solution.py:385
  15.6 0.0 copy-start
  15.6 0.0 copy-start.1
  15.6 0.0 collective-permute-done.2.refs_1_
  15.7 4.4 %collective-permute-done.3.refs_2_ = bf16[32,2176]{1,0:T(8,128)(2,1)S(1)} collective-permute-done((bf16[32,2176]{1,0:T(8,128)(2,1)S(1)}, bf16[32,2176]{1,0:T(8,128)(2,1)S(1)}, u32[]{:S(2)}, u32[]{:S(2)}) %collective-permute-start.3) | collective-permute-done | bytes 139296 | tf_op jit(solution)/shard_map/ppermute | solution.py:35
  20.1 0.0 collective-permute-done.1.refs_0_
  20.1 0.1 collective-permute-start.5
  20.2 0.0 collective-permute-done.refs_5_.refs_6_
  20.2 0.5 collective-permute-start.4
  20.7 0.4 collective-permute-start.6
  21.1 1.0 %collective-permute-done.5.refs_8_.refs_9_ = bf16[128,2176]{1,0:T(8,128)(2,1)S(1)} collective-permute-done((bf16[128,2176]{1,0:T(8,128)(2,1)S(1)}, bf16[128,2176]{1,0:T(8,128)(2,1)S(1)}, u32[]{:S(2)}, u32[]{:S(2)}) %collective-permute-start.5) | collective-permute-done | bytes 557088 | tf_op jit(solution)/shard_map/ppermute | solution.py:35
  22.1 0.8 collective-permute-done.4.refs_7_.refs_8_
  22.9 0.0 copy-done.2
  23.0 9.3 %shard_map.105 = (bf16[8,1024,512]{2,1,0:T(8,128)(2,1)S(1)}, f32[1024,512]{1,0:T(8,128)S(1)}, f32[8,8,512]{2,1,0:T(8,128)S(1)}) custom-call(bf16[512,1024]{1,0:T(8,128)(2,1)S(1)} %bitcast.10, bf16[512,1024]{1,0:T(8,128)(2,1)S(1)} %bitcast.16, bf16[512,1024]{1,0:T(8,128)(2,1)S(1)} %bitcast.20, bf16[512,128]{1,0:T(8,128)(2,1)S(1)} %get-tuple-element.60.refs_3_.refs_2_, ...), custom_call_target="tpu_custom_call" | custom-call | flops 1024 | bytes 1024 | tf_op jit(solution)/shard_map/pallas_call | solution.py:223
  32.3 3.0 %collective-permute-done.6.refs_5_.refs_10_ = bf16[128,2176]{1,0:T(8,128)(2,1)S(1)} collective-permute-done((bf16[128,2176]{1,0:T(8,128)(2,1)S(1)}, bf16[128,2176]{1,0:T(8,128)(2,1)S(1)}, u32[]{:S(2)}, u32[]{:S(2)}) %collective-permute-start.6) | collective-permute-done | bytes 557088 | tf_op jit(solution)/shard_map/ppermute | solution.py:35
  35.3 0.0 collective-permute-start.7
  35.3 2.0 %collective-permute-done.7.refs_6_.refs_11_ = bf16[128,2176]{1,0:T(8,128)(2,1)S(1)} collective-permute-done((bf16[128,2176]{1,0:T(8,128)(2,1)S(1)}, bf16[128,2176]{1,0:T(8,128)(2,1)S(1)}, u32[]{:S(2)}, u32[]{:S(2)}) %collective-permute-start.7) | collective-permute-done | bytes 557088 | tf_op jit(solution)/shard_map/ppermute | solution.py:35
  37.3 2.6 %shard_map.106 = (bf16[8,256,512]{2,1,0:T(8,128)(2,1)S(1)}, bf16[1024,512]{1,0:T(8,128)(2,1)S(1)}, f32[8,8,512]{2,1,0:T(8,128)S(1)}) custom-call(bf16[512,1024]{1,0:T(8,128)(2,1)S(1)} %bitcast.11, bf16[1024,512]{1,0:T(8,128)(2,1)S(1)} %get-tuple-element.59.refs_1_.refs_2_.refs_3_, bf16[512,128]{1,0:T(8,128)(2,1)S(1)} %get-tuple-element.60.refs_3_.refs_2_, ...), custom_call_target="tpu_custom_call" | custom-call | flops 1024 | bytes 1024 | tf_op jit(solution)/shard_map/pallas_call | solution.py:264
  39.9 2.3 %shard_map.107 = (bf16[512,2048]{1,0:T(8,128)(2,1)S(1)}, bf16[512,2048]{1,0:T(8,128)(2,1)S(1)}, f32[8,128]{1,0:T(8,128)S(1)}) custom-call(s32[1]{0:T(128)} %bitcast.2.place_ref, bf16[1024,512]{1,0:T(8,128)(2,1)S(1)} %get-tuple-element.74.ot_ref.a_ref, bf16[512,2048]{1,0:T(8,128)(2,1)S(1)} %bitcast.24), custom_call_target="tpu_custom_call" | custom-call | flops 1024 | bytes 1024 | tf_op jit(solution)/shard_map/pallas_call | solution.py:450
  42.3 0.4 collective-permute-start.8
  42.7 6.0 %shard_map.108 = (bf16[2,384,1024]{2,1,0:T(8,128)(2,1)S(1)}, bf16[2,384,1024]{2,1,0:T(8,128)(2,1)S(1)}, f32[1024,512]{1,0:T(8,128)S(1)}, f32[8,128]{1,0:T(8,128)S(1)}) custom-call(bf16[512,1024]{1,0:T(8,128)(2,1)S(1)} %bitcast.12, bf16[512,1024]{1,0:T(8,128)(2,1)S(1)} %get-tuple-element.68.refs_3_.refs_1_, ...), custom_call_target="tpu_custom_call" | custom-call | flops 1024 | bytes 1024 | tf_op jit(solution)/shard_map/pallas_call | solution.py:320
  48.6 0.5 collective-permute-start.11
  49.1 0.0 collective-permute-done.8.refs_1_
  49.1 0.5 shard_map.109
  49.7 1.6 %collective-permute-start.9 = (bf16[64,2048]{1,0:T(8,128)(2,1)S(1)}, bf16[64,2048]{1,0:T(8,128)(2,1)S(1)}, u32[]{:S(2)}, u32[]{:S(2)}) collective-permute-start(bf16[64,2048]{1,0:T(8,128)(2,1)S(1)} %get-tuple-element.84), channel_id=1, source_target_pairs={{0,2},{1,3},{2,4},{3,5},{4,6},{5,7},{6,0},{7,1},{8,10},{9,11},{10,... | collective-permute-start | bytes 786440 | tf_op jit(solution)/shard_map/ppermute | solution.py:40
  51.3 1.7 %collective-permute-start.10 = (bf16[64,2048]{1,0:T(8,128)(2,1)S(1)}, bf16[64,2048]{1,0:T(8,128)(2,1)S(1)}, u32[]{:S(2)}, u32[]{:S(2)}) collective-permute-start(bf16[64,2048]{1,0:T(8,128)(2,1)S(1)} %get-tuple-element.85), channel_id=1, source_target_pairs={{0,6},{1,7},{2,0},{3,1},{4,2},{5,3},{6,4},{7,5},{8,14},{9,15},{10,... | collective-permute-start | bytes 786440 | tf_op jit(solution)/shard_map/ppermute | solution.py:40
  53.0 0.0 collective-permute-done.11.refs_1_
  53.0 0.4 shard_map.110
  53.3 1.1 %collective-permute-start.13 = (bf16[2,128,1024]{2,1,0:T(8,128)(2,1)S(1)}, bf16[2,128,1024]{2,1,0:T(8,128)(2,1)S(1)}, u32[]{:S(2)}, u32[]{:S(2)}) collective-permute-start(bf16[2,128,1024]{2,1,0:T(8,128)(2,1)S(1)} %get-tuple-element.104), channel_id=1, source_target_pairs={{0,16},{8,24},{16,0},{24,8},{32,48},{40,56},{48,32},{56,40},{64,80... | collective-permute-start | bytes 1572872 | tf_op jit(solution)/shard_map/ppermute | solution.py:35
  54.5 4.3 %shard_map.111 = (bf16[512,896]{1,0:T(8,128)(2,1)S(1)}, bf16[512,896]{1,0:T(8,128)(2,1)S(1)}, bf16[512,896]{1,0:T(8,128)(2,1)S(1)}, f32[8,128]{1,0:T(8,128)S(1)}) custom-call(bf16[512,1024]{1,0:T(8,128)(2,1)S(1)} %bitcast.13, bf16[512,1024]{1,0:T(8,128)(2,1)S(1)} %bitcast.17, bf16[512,1024]{1,0:T(8,128)(2,1)S(1)} %bitcast.21, ...), custom_call_target="tpu_custom_call" | custom-call | flops 1024 | bytes 1024 | tf_op jit(solution)/shard_map/pallas_call | solution.py:367
  58.7 0.6 collective-permute-done.9.lower_ref
  59.3 0.0 collective-permute-done.10.upper_ref
  59.4 0.1 shard_map.112
  59.5 1.6 %collective-permute-start.17 = (bf16[128,2048]{1,0:T(8,128)(2,1)S(1)}, bf16[128,2048]{1,0:T(8,128)(2,1)S(1)}, u32[]{:S(2)}, u32[]{:S(2)}) collective-permute-start(bf16[128,2048]{1,0:T(8,128)(2,1)S(1)} %get-tuple-element.92._), channel_id=1, source_target_pairs={{0,2},{1,3},{2,4},{3,5},{4,6},{5,7},{6,0},{7,1},{8,10},{9,11},{10,... | collective-permute-start | bytes 1572872 | tf_op jit(solution)/shard_map/ppermute | solution.py:40
  61.1 1.7 %collective-permute-start.18 = (bf16[128,2048]{1,0:T(8,128)(2,1)S(1)}, bf16[128,2048]{1,0:T(8,128)(2,1)S(1)}, u32[]{:S(2)}, u32[]{:S(2)}) collective-permute-start(bf16[128,2048]{1,0:T(8,128)(2,1)S(1)} %get-tuple-element.111), channel_id=1, source_target_pairs={{0,6},{1,7},{2,0},{3,1},{4,2},{5,3},{6,4},{7,5},{8,14},{9,15},{10,... | collective-permute-start | bytes 1572872 | tf_op jit(solution)/shard_map/ppermute | solution.py:40
  62.8 0.0 copy-done.5
  62.8 3.7 %shard_map.113 = (bf16[512,2048]{1,0:T(8,128)(2,1)}, f32[8,128]{1,0:T(8,128)S(1)}) custom-call(bf16[1024,512]{1,0:T(8,128)(2,1)S(1)} %get-tuple-element.74.ot_ref.a_ref, bf16[1024,2048]{1,0:T(8,128)(2,1)S(1)} %copy-done.5, bf16[128,2048]{1,0:T(8,128)(2,1)S(1)} %get-tuple-element.92._), custom_call_target="tpu_custom_call" | custom-call | flops 20000000000 | bytes 1024 | tf_op jit(solution)/shard_map/pallas_call | solution.py:402
  66.5 0.8 collective-permute-start.12
  67.4 2.0 %shard_map.114 = (bf16[512,1024]{1,0:T(8,128)(2,1)}, bf16[512,1024]{1,0:T(8,128)(2,1)S(1)}, bf16[512,1024]{1,0:T(8,128)(2,1)S(1)}, f32[8,128]{1,0:T(8,128)S(1)}) custom-call(bf16[512,1024]{1,0:T(8,128)(2,1)S(1)} %bitcast.14, bf16[512,1024]{1,0:T(8,128)(2,1)S(1)} %bitcast.18, bf16[512,1024]{1,0:T(8,128)(2,1)S(1)} %bitcast.22, ...), custom_call_target="tpu_custom_call" | custom-call | flops 1024 | bytes 1024 | tf_op jit(solution)/shard_map/pallas_call | solution.py:367
  69.4 0.0 collective-permute-done.13.refs_1_
  69.4 0.8 shard_map.115
  70.2 1.5 %collective-permute-start.14 = (bf16[2,64,1024]{2,1,0:T(8,128)(2,1)S(1)}, bf16[2,64,1024]{2,1,0:T(8,128)(2,1)}, u32[]{:S(2)}, u32[]{:S(2)}) collective-permute-start(bf16[2,64,1024]{2,1,0:T(8,128)(2,1)S(1)} %get-tuple-element.106.refs_3_), channel_id=1, source_target_pairs={{0,32},{8,40},{16,48},{24,56},{32,0},{40,8},{48,16},{56,24},{64,96... | collective-permute-start | bytes 786440 | tf_op jit(solution)/shard_map/ppermute | solution.py:35
  71.7 2.1 %collective-permute-start.15 = (bf16[2,32,1024]{2,1,0:T(8,128)(2,1)}, bf16[2,32,1024]{2,1,0:T(8,128)(2,1)S(1)}, u32[]{:S(2)}, u32[]{:S(2)}) collective-permute-start(bf16[2,32,1024]{2,1,0:T(8,128)(2,1)} %get-tuple-element.107), channel_id=1, source_target_pairs={{0,96},{8,104},{16,112},{24,120},{32,64},{40,72},{48,80},{56,88},{... | collective-permute-start | bytes 393224 | tf_op jit(solution)/shard_map/ppermute | solution.py:35
  73.8 0.2 collective-permute-done.17.refs_1_
  73.9 2.5 %collective-permute-start.16 = (bf16[2,32,1024]{2,1,0:T(8,128)(2,1)}, bf16[2,32,1024]{2,1,0:T(8,128)(2,1)}, u32[]{:S(2)}, u32[]{:S(2)}) collective-permute-start(bf16[2,32,1024]{2,1,0:T(8,128)(2,1)} %get-tuple-element.108), channel_id=1, source_target_pairs={{0,64},{8,72},{16,80},{24,88},{32,96},{40,104},{48,112},{56,120},{... | collective-permute-start | bytes 393224 | tf_op jit(solution)/shard_map/ppermute | solution.py:35
  76.5 0.0 collective-permute-done.18.refs_2_
  76.5 1.0 %shard_map.117 = bf16[128,2048]{1,0:T(8,128)(2,1)} custom-call(bf16[128,2048]{1,0:T(8,128)(2,1)S(1)} %get-tuple-element.89.refs_2_.refs_0_, bf16[128,2048]{1,0:T(8,128)(2,1)S(1)} %collective-permute-done.17.refs_1_, bf16[128,2048]{1,0:T(8,128)(2,1)S(1)} %collective-permute-done.18.refs_2_, bf16[2,64,1024]{2,1,0:T(8,128)(2,1)S(1)} %get-tuple-element.106.refs_3_), custom_call_target="tpu_custom_call" | custom-call | flops 1024 | bytes 1024 | tf_op jit(solution)/shard_map/pallas_call | solution.py:478
  77.5 5.5 %all-to-all-start = ((bf16[16,8,2048]{2,1,0:T(8,128)(2,1)}), bf16[16,8,2048]{2,1,0:T(8,128)(2,1)S(1)}, u32[]{:S(2)}, u32[]{:S(2)}) async-start(bf16[16,8,2048]{2,1,0:T(8,128)(2,1)} %bitcast.9), calls=%async_computation | async-start | bytes 1048576 | tf_op jit(solution)/shard_map/all_to_all | solution.py:605
  83.0 0.0 collective-permute-done.15.refs_4_
  83.0 0.0 collective-permute-done.16.refs_5_
  83.0 0.0 collective-permute-done.12.refs_2_
  83.0 0.0 collective-permute-done.14.refs_3_
  83.1 2.8 %shard_map.116 = (bf16[512,1024]{1,0:T(8,128)(2,1)}, bf16[512,1024]{1,0:T(8,128)(2,1)}, f32[8,128]{1,0:T(8,128)S(1)}) custom-call(bf16[512,1024]{1,0:T(8,128)(2,1)S(1)} %get-tuple-element.100.refs_0_, bf16[512,1024]{1,0:T(8,128)(2,1)S(1)} %get-tuple-element.101.refs_1_, bf16[2,128,1024]{2,1,0:T(8,128)(2,1)} %collective-permute-done.12.refs_2_, ...), custom_call_target="tpu_custom_call" | custom-call | flops 20000000000 | bytes 1024 | tf_op jit(solution)/shard_map/pallas_call | solution.py:528
  85.8 7.2 %all-to-all-done.ref = bf16[16,8,2048]{2,1,0:T(8,128)(2,1)S(1)} async-done(((bf16[16,8,2048]{2,1,0:T(8,128)(2,1)}), bf16[16,8,2048]{2,1,0:T(8,128)(2,1)S(1)}, u32[]{:S(2)}, u32[]{:S(2)}) %all-to-all-start) | async-done | bytes 524320 | tf_op jit(solution)/shard_map/all_to_all | solution.py:605
  93.0 0.7 shard_map.118
  (8 shorter events, 0.1 us)
Async XLA Ops:
  0.6 10.4 %copy-start.3 = (bf16[1,512,2048]{2,1,0:T(8,128)(2,1)S(1)}, bf16[1,512,2048]{2,1,0:T(8,128)(2,1)}, u32[]{:S(2)}) copy-start(bf16[1,512,2048]{2,1,0:T(8,128)(2,1)} %param.11) | copy-start | bytes 6291460
  0.6 0.8 copy-start.6
  4.7 15.5 %collective-permute-start = (bf16[128,2176]{1,0:T(8,128)(2,1)S(1)}, bf16[128,2176]{1,0:T(8,128)(2,1)S(1)}, u32[]{:S(2)}, u32[]{:S(2)}) collective-permute-start(bf16[128,2176]{1,0:T(8,128)(2,1)S(1)} %get-tuple-element.62), channel_id=1, source_target_pairs={{0,16},{8,24},{16,0},{24,8},{32,48},{40,56},{48,32},{56,40},{64,80... | collective-permute-start | bytes 1671176 | tf_op jit(solution)/shard_map/ppermute | solution.py:35
  6.8 13.3 %collective-permute-start.1 = (bf16[64,2176]{1,0:T(8,128)(2,1)S(1)}, bf16[64,2176]{1,0:T(8,128)(2,1)S(1)}, u32[]{:S(2)}, u32[]{:S(2)}) collective-permute-start(bf16[64,2176]{1,0:T(8,128)(2,1)S(1)} %get-tuple-element.66), channel_id=1, source_target_pairs={{0,32},{8,40},{16,48},{24,56},{32,0},{40,8},{48,16},{56,24},{64,96... | collective-permute-start | bytes 835592 | tf_op jit(solution)/shard_map/ppermute | solution.py:35
  8.3 7.4 %collective-permute-start.2 = (bf16[32,2176]{1,0:T(8,128)(2,1)S(1)}, bf16[32,2176]{1,0:T(8,128)(2,1)S(1)}, u32[]{:S(2)}, u32[]{:S(2)}) collective-permute-start(bf16[32,2176]{1,0:T(8,128)(2,1)S(1)} %get-tuple-element.67), channel_id=1, source_target_pairs={{0,96},{8,104},{16,112},{24,120},{32,64},{40,72},{48,80},{56,88},{... | collective-permute-start | bytes 417800 | tf_op jit(solution)/shard_map/ppermute | solution.py:35
  10.4 9.7 %collective-permute-start.3 = (bf16[32,2176]{1,0:T(8,128)(2,1)S(1)}, bf16[32,2176]{1,0:T(8,128)(2,1)S(1)}, u32[]{:S(2)}, u32[]{:S(2)}) collective-permute-start(bf16[32,2176]{1,0:T(8,128)(2,1)S(1)} %get-tuple-element.67), channel_id=1, source_target_pairs={{0,64},{8,72},{16,80},{24,88},{32,96},{40,104},{48,112},{56,120},{... | collective-permute-start | bytes 417800 | tf_op jit(solution)/shard_map/ppermute | solution.py:35
  11.0 2.2 %copy-start.4 = (bf16[1024,2048]{1,0:T(8,128)(2,1)S(1)}, bf16[1024,2048]{1,0:T(8,128)(2,1)}, u32[]{:S(2)}) copy-start(bf16[1024,2048]{1,0:T(8,128)(2,1)} %w_ref.3) | copy-start | bytes 12582916
  13.2 9.8 %copy-start.2 = (bf16[1,512,1024]{2,1,0:T(8,128)(2,1)S(1)}, bf16[1,512,1024]{2,1,0:T(8,128)(2,1)}, u32[]{:S(2)}) copy-start(bf16[1,512,1024]{2,1,0:T(8,128)(2,1)} %param.8) | copy-start | bytes 3145732
  15.6 7.3 %copy-start = (bf16[1,512,1024]{2,1,0:T(8,128)(2,1)S(1)}, bf16[1,512,1024]{2,1,0:T(8,128)(2,1)}, u32[]{:S(2)}) copy-start(bf16[1,512,1024]{2,1,0:T(8,128)(2,1)} %param.6) | copy-start | bytes 3145732
  15.6 7.3 %copy-start.1 = (bf16[1,512,1024]{2,1,0:T(8,128)(2,1)S(1)}, bf16[1,512,1024]{2,1,0:T(8,128)(2,1)}, u32[]{:S(2)}) copy-start(bf16[1,512,1024]{2,1,0:T(8,128)(2,1)} %param.7) | copy-start | bytes 3145732
  20.1 2.0 %collective-permute-start.5 = (bf16[128,2176]{1,0:T(8,128)(2,1)S(1)}, bf16[128,2176]{1,0:T(8,128)(2,1)S(1)}, u32[]{:S(2)}, u32[]{:S(2)}) collective-permute-start(bf16[128,2176]{1,0:T(8,128)(2,1)S(1)} %shard_map.104.refs_6_.refs_7_), channel_id=1, source_target_pairs={{0,8},{8,0},{16,24},{24,16},{32,40},{40,32},{48,56},{56,48},{64,72... | collective-permute-start | bytes 1671176 | tf_op jit(solution)/shard_map/ppermute | solution.py:35
  20.2 2.7 %collective-permute-start.4 = (bf16[128,2176]{1,0:T(8,128)(2,1)S(1)}, bf16[128,2176]{1,0:T(8,128)(2,1)S(1)}, u32[]{:S(2)}, u32[]{:S(2)}) collective-permute-start(bf16[128,2176]{1,0:T(8,128)(2,1)S(1)} %collective-permute-done.refs_5_.refs_6_), channel_id=1, source_target_pairs={{0,8},{8,0},{16,24},{24,16},{32,40},{40,32},{48,56},{56,48},{64,72... | collective-permute-start | bytes 1671176 | tf_op jit(solution)/shard_map/ppermute | solution.py:35
  20.7 14.6 %collective-permute-start.6 = (bf16[128,2176]{1,0:T(8,128)(2,1)S(1)}, bf16[128,2176]{1,0:T(8,128)(2,1)S(1)}, u32[]{:S(2)}, u32[]{:S(2)}) collective-permute-start(bf16[128,2176]{1,0:T(8,128)(2,1)S(1)} %shard_map.104.refs_6_.refs_7_), channel_id=1, source_target_pairs={{0,16},{8,24},{16,0},{24,8},{32,48},{40,56},{48,32},{56,40},{64,80... | collective-permute-start | bytes 1671176 | tf_op jit(solution)/shard_map/ppermute | solution.py:35
  35.3 2.0 %collective-permute-start.7 = (bf16[128,2176]{1,0:T(8,128)(2,1)S(1)}, bf16[128,2176]{1,0:T(8,128)(2,1)S(1)}, u32[]{:S(2)}, u32[]{:S(2)}) collective-permute-start(bf16[128,2176]{1,0:T(8,128)(2,1)S(1)} %collective-permute-done.6.refs_5_.refs_10_), channel_id=1, source_target_pairs={{0,8},{8,0},{16,24},{24,16},{32,40},{40,32},{48,56},{56,48},{64,72... | collective-permute-start | bytes 1671176 | tf_op jit(solution)/shard_map/ppermute | solution.py:35
  42.3 6.8 %collective-permute-start.8 = (bf16[512,2048]{1,0:T(8,128)(2,1)S(1)}, bf16[512,2048]{1,0:T(8,128)(2,1)S(1)}, u32[]{:S(2)}, u32[]{:S(2)}) collective-permute-start(bf16[512,2048]{1,0:T(8,128)(2,1)S(1)} %get-tuple-element.76), channel_id=1, source_target_pairs={{0,8},{8,0},{16,24},{24,16},{32,40},{40,32},{48,56},{56,48},{64,72... | collective-permute-start | bytes 6291464 | tf_op jit(solution)/shard_map/ppermute | solution.py:35
  48.6 4.3 %collective-permute-start.11 = (bf16[2,384,1024]{2,1,0:T(8,128)(2,1)S(1)}, bf16[2,384,1024]{2,1,0:T(8,128)(2,1)S(1)}, u32[]{:S(2)}, u32[]{:S(2)}) collective-permute-start(bf16[2,384,1024]{2,1,0:T(8,128)(2,1)S(1)} %get-tuple-element.88), channel_id=1, source_target_pairs={{0,8},{8,0},{16,24},{24,16},{32,40},{40,32},{48,56},{56,48},{64,72... | collective-permute-start | bytes 4718600 | tf_op jit(solution)/shard_map/ppermute | solution.py:35
  49.7 9.7 %collective-permute-start.9 = (bf16[64,2048]{1,0:T(8,128)(2,1)S(1)}, bf16[64,2048]{1,0:T(8,128)(2,1)S(1)}, u32[]{:S(2)}, u32[]{:S(2)}) collective-permute-start(bf16[64,2048]{1,0:T(8,128)(2,1)S(1)} %get-tuple-element.84), channel_id=1, source_target_pairs={{0,2},{1,3},{2,4},{3,5},{4,6},{5,7},{6,0},{7,1},{8,10},{9,11},{10,... | collective-permute-start | bytes 786440 | tf_op jit(solution)/shard_map/ppermute | solution.py:40
  51.3 8.1 %collective-permute-start.10 = (bf16[64,2048]{1,0:T(8,128)(2,1)S(1)}, bf16[64,2048]{1,0:T(8,128)(2,1)S(1)}, u32[]{:S(2)}, u32[]{:S(2)}) collective-permute-start(bf16[64,2048]{1,0:T(8,128)(2,1)S(1)} %get-tuple-element.85), channel_id=1, source_target_pairs={{0,6},{1,7},{2,0},{3,1},{4,2},{5,3},{6,4},{7,5},{8,14},{9,15},{10,... | collective-permute-start | bytes 786440 | tf_op jit(solution)/shard_map/ppermute | solution.py:40
  53.3 16.1 %collective-permute-start.13 = (bf16[2,128,1024]{2,1,0:T(8,128)(2,1)S(1)}, bf16[2,128,1024]{2,1,0:T(8,128)(2,1)S(1)}, u32[]{:S(2)}, u32[]{:S(2)}) collective-permute-start(bf16[2,128,1024]{2,1,0:T(8,128)(2,1)S(1)} %get-tuple-element.104), channel_id=1, source_target_pairs={{0,16},{8,24},{16,0},{24,8},{32,48},{40,56},{48,32},{56,40},{64,80... | collective-permute-start | bytes 1572872 | tf_op jit(solution)/shard_map/ppermute | solution.py:35
  54.5 8.3 %copy-start.5 = (bf16[1024,2048]{1,0:T(8,128)(2,1)S(1)}, bf16[1024,2048]{1,0:T(8,128)(2,1)}, u32[]{:S(2)}) copy-start(bf16[1024,2048]{1,0:T(8,128)(2,1)} %w_ref.3) | copy-start | bytes 12582916
  59.5 14.5 %collective-permute-start.17 = (bf16[128,2048]{1,0:T(8,128)(2,1)S(1)}, bf16[128,2048]{1,0:T(8,128)(2,1)S(1)}, u32[]{:S(2)}, u32[]{:S(2)}) collective-permute-start(bf16[128,2048]{1,0:T(8,128)(2,1)S(1)} %get-tuple-element.92._), channel_id=1, source_target_pairs={{0,2},{1,3},{2,4},{3,5},{4,6},{5,7},{6,0},{7,1},{8,10},{9,11},{10,... | collective-permute-start | bytes 1572872 | tf_op jit(solution)/shard_map/ppermute | solution.py:40
  61.1 15.3 %collective-permute-start.18 = (bf16[128,2048]{1,0:T(8,128)(2,1)S(1)}, bf16[128,2048]{1,0:T(8,128)(2,1)S(1)}, u32[]{:S(2)}, u32[]{:S(2)}) collective-permute-start(bf16[128,2048]{1,0:T(8,128)(2,1)S(1)} %get-tuple-element.111), channel_id=1, source_target_pairs={{0,6},{1,7},{2,0},{3,1},{4,2},{5,3},{6,4},{7,5},{8,14},{9,15},{10,... | collective-permute-start | bytes 1572872 | tf_op jit(solution)/shard_map/ppermute | solution.py:40
  66.5 16.5 %collective-permute-start.12 = (bf16[2,128,1024]{2,1,0:T(8,128)(2,1)S(1)}, bf16[2,128,1024]{2,1,0:T(8,128)(2,1)}, u32[]{:S(2)}, u32[]{:S(2)}) collective-permute-start(bf16[2,128,1024]{2,1,0:T(8,128)(2,1)S(1)} %get-tuple-element.102.refs_7_), channel_id=1, source_target_pairs={{0,16},{8,24},{16,0},{24,8},{32,48},{40,56},{48,32},{56,40},{64,80... | collective-permute-start | bytes 1572872 | tf_op jit(solution)/shard_map/ppermute | solution.py:35
  70.2 12.9 %collective-permute-start.14 = (bf16[2,64,1024]{2,1,0:T(8,128)(2,1)S(1)}, bf16[2,64,1024]{2,1,0:T(8,128)(2,1)}, u32[]{:S(2)}, u32[]{:S(2)}) collective-permute-start(bf16[2,64,1024]{2,1,0:T(8,128)(2,1)S(1)} %get-tuple-element.106.refs_3_), channel_id=1, source_target_pairs={{0,32},{8,40},{16,48},{24,56},{32,0},{40,8},{48,16},{56,24},{64,96... | collective-permute-start | bytes 786440 | tf_op jit(solution)/shard_map/ppermute | solution.py:35
  71.7 11.3 %collective-permute-start.15 = (bf16[2,32,1024]{2,1,0:T(8,128)(2,1)}, bf16[2,32,1024]{2,1,0:T(8,128)(2,1)S(1)}, u32[]{:S(2)}, u32[]{:S(2)}) collective-permute-start(bf16[2,32,1024]{2,1,0:T(8,128)(2,1)} %get-tuple-element.107), channel_id=1, source_target_pairs={{0,96},{8,104},{16,112},{24,120},{32,64},{40,72},{48,80},{56,88},{... | collective-permute-start | bytes 393224 | tf_op jit(solution)/shard_map/ppermute | solution.py:35
  73.9 9.1 %collective-permute-start.16 = (bf16[2,32,1024]{2,1,0:T(8,128)(2,1)}, bf16[2,32,1024]{2,1,0:T(8,128)(2,1)}, u32[]{:S(2)}, u32[]{:S(2)}) collective-permute-start(bf16[2,32,1024]{2,1,0:T(8,128)(2,1)} %get-tuple-element.108), channel_id=1, source_target_pairs={{0,64},{8,72},{16,80},{24,88},{32,96},{40,104},{48,112},{56,120},{... | collective-permute-start | bytes 393224 | tf_op jit(solution)/shard_map/ppermute | solution.py:35
  77.5 15.6 %all-to-all-start = ((bf16[16,8,2048]{2,1,0:T(8,128)(2,1)}), bf16[16,8,2048]{2,1,0:T(8,128)(2,1)S(1)}, u32[]{:S(2)}, u32[]{:S(2)}) async-start(bf16[16,8,2048]{2,1,0:T(8,128)(2,1)} %bitcast.9), calls=%async_computation | async-start | bytes 1048576 | tf_op jit(solution)/shard_map/all_to_all | solution.py:605
